TPU v7x, 32 devices: a whole 2x2x4 slice. The times are simulated.
32 devices in a mesh: lat: 8 (over z, y), depth: 4 (over x, core).
Axes of the slice: x: 2, y: 2, z: 4, core: 2. Of those that a mesh axis runs over, the one named last changes fastest.
Arguments:
- thermal_anomaly: float32 [128, 32, 2048], P('depth', 'lat'), may hold values from -6 to 6
- water_anomaly: float32 [128, 32, 2048], P('depth', 'lat'), may hold values from -6 to 6
- substrate_class_label: int32 [32, 2048], P('lat'), may hold values from 0 to 11
- sideways_thermal_spread: float32 [12], replicated, may hold values from 0.1 to 0.6
- sideways_water_factors: float32 [12], replicated, may hold values from 0.1 to 0.9
- thermal_solve_matrix: float32 [128, 128], replicated, may hold values from -0.3 to 1.3, as said below
- water_solve_matrix: float32 [128, 128], replicated, may hold values from -0.3 to 1.3, as said below
Outputs:
- temperature_next: float32 [128, 32, 2048], P('depth', 'lat')
- moisture_next: float32 [128, 32, 2048], P('depth', 'lat')
Inputs may be any that keep to these rules, and one draw needn't show every extreme that they name: `thermal_solve_matrix`: a dense matrix with unit diagonal. `water_solve_matrix`: a dense matrix with unit diagonal.
All inputs are finite; a program needn't handle non-finite values.
Results may differ from a plain program's by a relative error of at most 0.00007.
Values sent between devices are 32-bit elements; how exact they have to be, the bound alone decides.
No kernel may reach another device: no remote copies, remote signals or barrier semaphores. Data moves between devices by JAX's collectives and lax.ppermute only.
A program may use at most 128 MiB of HBM per device.

v0:
```python
import jax
import jax.numpy as jnp
from jax import lax
from jax.sharding import PartitionSpec as P

VERTICAL_POINTS = 128
LSUB = 4


RATE = 0.25


def extended(cells, sides, width):
    for axis, dim in sides:
        count = lax.axis_size(axis)
        ends = count - 1
        head = lax.slice_in_dim(cells, 0, width, axis=dim)
        tail = lax.slice_in_dim(cells, cells.shape[dim] - width, cells.shape[dim], axis=dim)
        cells = jnp.concatenate(
            [
                lax.ppermute(tail, axis, [(i, (i + 1) % count) for i in range(ends)]),
                cells,
                lax.ppermute(head, axis, [((i + 1) % count, i) for i in range(ends)]),
            ],
            axis=dim,
        )
    return cells


def cheb_matrix(count):
    index = jnp.arange(count).astype(jnp.float32)
    nodes = jnp.cos(jnp.pi * index / (count - 1))
    ends = jnp.where((index == 0) | (index == count - 1), 2.0, 1.0)
    signs = jnp.where(jnp.arange(count) % 2 == 0, 1.0, -1.0)
    weight = (ends * signs).astype(jnp.float32)
    diagonal = jnp.arange(count)[:, None] == jnp.arange(count)[None, :]
    spread = nodes[:, None] - nodes[None, :]
    off = weight[:, None] / weight[None, :] / jnp.where(diagonal, 1.0, spread)
    off = jnp.where(diagonal, 0.0, off)
    return (off - jnp.diag(jnp.sum(off, axis=1)), nodes)


def lateral_sum(after, before, centre):
    zeros = jnp.zeros_like(centre[..., :1])
    east = jnp.concatenate([centre[..., 1:], zeros], axis=-1)
    west = jnp.concatenate([zeros, centre[..., :-1]], axis=-1)
    return after + before + east + west - 4.0 * centre


def advance(profile_snapshot, lap, kappa_heat, kappa_moist):
    wet = profile_snapshot[1]
    kappa_t = kappa_heat * (1.0 + 0.5 * wet * wet / (1.0 + wet * wet))
    return jnp.stack(
        [
            profile_snapshot[0] + RATE * kappa_t * lap[0],
            profile_snapshot[1] + RATE * kappa_moist * lap[1],
        ]
    )


def column_step(pair, kappa_cols, deriv, nodes, thermal_solve_matrix, water_solve_matrix):
    high = lax.Precision.HIGHEST
    scale = (1.0 - nodes * nodes) / deriv.shape[0]
    flux = kappa_cols[None, :, :] * pair[1]
    drain = jnp.einsum("zk,kmc->zmc", deriv, flux, precision=high)
    drain = drain * scale[:, None, None]
    rhs_heat = pair[0] - 0.25 * drain
    rhs_wet = pair[1] + 0.5 * drain
    new_heat = jnp.einsum("zk,kmc->zmc", thermal_solve_matrix, rhs_heat, precision=high)
    new_wet = jnp.einsum("zk,kmc->zmc", water_solve_matrix, rhs_wet, precision=high)
    return jnp.stack([new_heat, new_wet])


def per_device(
    thermal_anomaly,
    water_anomaly,
    substrate_class_label,
    sideways_thermal_spread,
    sideways_water_factors,
    thermal_solve_matrix,
    water_solve_matrix,
):
    labels = jnp.arange(sideways_thermal_spread.shape[0], dtype=jnp.int32)
    onehot = (substrate_class_label[None, :, :] == labels[:, None, None]).astype(jnp.float32)
    kappa_heat = jnp.sum(onehot * sideways_thermal_spread[:, None, None], axis=0)
    kappa_moist = jnp.sum(onehot * sideways_water_factors[:, None, None], axis=0)
    profile_snapshot = jnp.stack([thermal_anomaly, water_anomaly])
    for step in range(LSUB):
        padded = extended(profile_snapshot, (("lat", 2),), 1)
        lap = lateral_sum(padded[:, :, 2:], padded[:, :, :-2], profile_snapshot)
        profile_snapshot = advance(profile_snapshot, lap, kappa_heat, kappa_moist)
    deriv, nodes = cheb_matrix(VERTICAL_POINTS)
    columns = lax.all_to_all(profile_snapshot, "depth", split_axis=3, concat_axis=1, tiled=True)
    width = columns.shape[3]
    start = lax.axis_index("depth") * width
    kappa_cols = lax.dynamic_slice_in_dim(kappa_moist, start, width, 1)
    solved = column_step(
        columns, kappa_cols, deriv, nodes, thermal_solve_matrix, water_solve_matrix
    )
    result = lax.all_to_all(solved, "depth", split_axis=1, concat_axis=3, tiled=True)
    return (result[0], result[1])


def solution(mesh):
    return jax.shard_map(
        per_device,
        mesh=mesh,
        in_specs=(
            P("depth", "lat", None),
            P("depth", "lat", None),
            P("lat", None),
            P(),
            P(),
            P(),
            P(),
        ),
        out_specs=(P("depth", "lat", None), P("depth", "lat", None)),
        check_vma=False,
    )
```

profile of v0, /device:TPU:0, one launch (start us, length us, event | category | flops | bytes accessed | tf_op | source)
XLA Modules:
  0.0 234.5 jit_solution(4967800890876535665)
XLA Ops:
  0.6 0.0 copy-start
  0.6 2.8 %copy_bitcast_fusion = (f32[1,32,4,2048]{3,1,2,0:T(8,128)S(1)}, f32[1,32,4,2048]{3,1,2,0:T(8,128)S(1)}) fusion(f32[32,4,2048]{2,1,0:T(4,128)} %param.7, f32[32,4,2048]{2,1,0:T(4,128)} %param.8), kind=kLoop, calls=%fused_computation.136 | loop fusion | bytes 4194304 | tf_op jit(solution)/shard_map/stack | solution.py:87
  3.4 0.1 fusion.73
  3.5 1.3 collective-permute-start
  4.8 0.0 copy-start.5
  4.8 0.0 copy-start.6
  4.9 5.7 %collective-permute-start.1 = (f32[2,32,1,2048]{3,1,2,0:T(8,128)S(1)}, f32[2,32,1,2048]{3,1,2,0:T(8,128)S(1)}, u32[]{:S(2)}, u32[]{:S(2)}) collective-permute-start(f32[2,32,1,2048]{3,1,2,0:T(8,128)S(1)} %get-tuple-element.39), channel_id=1, source_target_pairs={{0,4},{4,8},{8,12},{12,16},{16,20},{20,24},{24,28},{1,5},{5,9},{9,... | collective-permute-start | bytes 1572872 | tf_op jit(solution)/shard_map/ppermute | solution.py:21
  10.5 0.8 fusion.12
  11.3 0.3 select_reduce_fusion.1
  11.6 8.7 %collective-permute-done = f32[2,32,1,2048]{3,1,2,0:T(8,128)S(1)} collective-permute-done((f32[2,32,1,2048]{3,1,2,0:T(8,128)S(1)}, f32[2,32,1,2048]{3,1,2,0:T(8,128)S(1)}, u32[]{:S(2)}, u32[]{:S(2)}) %collective-permute-start) | collective-permute-done | bytes 524320 | tf_op jit(solution)/shard_map/ppermute | solution.py:23
  20.3 11.4 %collective-permute-done.1 = f32[2,32,1,2048]{3,1,2,0:T(8,128)S(1)} collective-permute-done((f32[2,32,1,2048]{3,1,2,0:T(8,128)S(1)}, f32[2,32,1,2048]{3,1,2,0:T(8,128)S(1)}, u32[]{:S(2)}, u32[]{:S(2)}) %collective-permute-start.1) | collective-permute-done | bytes 524320 | tf_op jit(solution)/shard_map/ppermute | solution.py:21
  31.7 1.0 fusion.15
  32.8 0.2 copy-done.2
  32.9 0.3 copy-done.3
  33.3 1.4 fusion.33
  34.7 0.1 fusion.71
  34.8 1.3 collective-permute-start.2
  36.1 5.0 %collective-permute-start.3 = (f32[2,32,1,2048]{3,1,2,0:T(8,128)S(1)}, f32[2,32,1,2048]{3,1,2,0:T(8,128)S(1)}, u32[]{:S(2)}, u32[]{:S(2)}) collective-permute-start(f32[2,32,1,2048]{3,1,2,0:T(8,128)S(1)} %get-tuple-element.35), channel_id=1, source_target_pairs={{0,4},{4,8},{8,12},{12,16},{16,20},{20,24},{24,28},{1,5},{5,9},{9,... | collective-permute-start | bytes 1572872 | tf_op jit(solution)/shard_map/ppermute | solution.py:21
  41.1 0.8 fusion.8
  41.9 9.4 %collective-permute-done.2 = f32[2,32,1,2048]{3,1,2,0:T(8,128)S(1)} collective-permute-done((f32[2,32,1,2048]{3,1,2,0:T(8,128)S(1)}, f32[2,32,1,2048]{3,1,2,0:T(8,128)S(1)}, u32[]{:S(2)}, u32[]{:S(2)}) %collective-permute-start.2) | collective-permute-done | bytes 524320 | tf_op jit(solution)/shard_map/ppermute | solution.py:23
  51.3 11.4 %collective-permute-done.3 = f32[2,32,1,2048]{3,1,2,0:T(8,128)S(1)} collective-permute-done((f32[2,32,1,2048]{3,1,2,0:T(8,128)S(1)}, f32[2,32,1,2048]{3,1,2,0:T(8,128)S(1)}, u32[]{:S(2)}, u32[]{:S(2)}) %collective-permute-start.3) | collective-permute-done | bytes 524320 | tf_op jit(solution)/shard_map/ppermute | solution.py:21
  62.7 1.0 fusion.11
  63.7 0.5 fusion.39
  64.2 0.1 fusion.69
  64.3 1.3 collective-permute-start.4
  65.6 5.0 %collective-permute-start.5 = (f32[2,32,1,2048]{3,1,2,0:T(8,128)S(1)}, f32[2,32,1,2048]{3,1,2,0:T(8,128)S(1)}, u32[]{:S(2)}, u32[]{:S(2)}) collective-permute-start(f32[2,32,1,2048]{3,1,2,0:T(8,128)S(1)} %get-tuple-element.31), channel_id=1, source_target_pairs={{0,4},{4,8},{8,12},{12,16},{16,20},{20,24},{24,28},{1,5},{5,9},{9,... | collective-permute-start | bytes 1572872 | tf_op jit(solution)/shard_map/ppermute | solution.py:21
  70.6 0.8 fusion.4
  71.4 9.4 %collective-permute-done.4 = f32[2,32,1,2048]{3,1,2,0:T(8,128)S(1)} collective-permute-done((f32[2,32,1,2048]{3,1,2,0:T(8,128)S(1)}, f32[2,32,1,2048]{3,1,2,0:T(8,128)S(1)}, u32[]{:S(2)}, u32[]{:S(2)}) %collective-permute-start.4) | collective-permute-done | bytes 524320 | tf_op jit(solution)/shard_map/ppermute | solution.py:23
  80.8 11.4 %collective-permute-done.5 = f32[2,32,1,2048]{3,1,2,0:T(8,128)S(1)} collective-permute-done((f32[2,32,1,2048]{3,1,2,0:T(8,128)S(1)}, f32[2,32,1,2048]{3,1,2,0:T(8,128)S(1)}, u32[]{:S(2)}, u32[]{:S(2)}) %collective-permute-start.5) | collective-permute-done | bytes 524320 | tf_op jit(solution)/shard_map/ppermute | solution.py:21
  92.2 1.0 fusion.7
  93.2 0.5 fusion.45
  93.7 0.1 fusion.67
  93.8 1.3 collective-permute-start.6
  95.1 5.2 %collective-permute-start.7 = (f32[2,32,1,2048]{3,1,2,0:T(8,128)S(1)}, f32[2,32,1,2048]{3,1,2,0:T(8,128)S(1)}, u32[]{:S(2)}, u32[]{:S(2)}) collective-permute-start(f32[2,32,1,2048]{3,1,2,0:T(8,128)S(1)} %get-tuple-element.27), channel_id=1, source_target_pairs={{0,4},{4,8},{8,12},{12,16},{16,20},{20,24},{24,28},{1,5},{5,9},{9,... | collective-permute-start | bytes 1572872 | tf_op jit(solution)/shard_map/ppermute | solution.py:21
  100.3 0.8 fusion
  101.1 9.2 %collective-permute-done.6 = f32[2,32,1,2048]{3,1,2,0:T(8,128)S(1)} collective-permute-done((f32[2,32,1,2048]{3,1,2,0:T(8,128)S(1)}, f32[2,32,1,2048]{3,1,2,0:T(8,128)S(1)}, u32[]{:S(2)}, u32[]{:S(2)}) %collective-permute-start.6) | collective-permute-done | bytes 524320 | tf_op jit(solution)/shard_map/ppermute | solution.py:23
  110.3 11.4 %collective-permute-done.7 = f32[2,32,1,2048]{3,1,2,0:T(8,128)S(1)} collective-permute-done((f32[2,32,1,2048]{3,1,2,0:T(8,128)S(1)}, f32[2,32,1,2048]{3,1,2,0:T(8,128)S(1)}, u32[]{:S(2)}, u32[]{:S(2)}) %collective-permute-start.7) | collective-permute-done | bytes 524320 | tf_op jit(solution)/shard_map/ppermute | solution.py:21
  121.7 1.0 fusion.3
  122.7 0.5 fusion.66
  123.2 0.2 pad_maximum_fusion.20
  123.5 5.9 %copy.72 = f32[2,32,4,2048]{1,2,0,3:T(4,128)} copy(f32[2,32,4,2048]{3,1,2,0:T(8,128)S(1)} %pad_maximum_fusion.20) | data formatting | bytes 4194304 | tf_op jit(solution)/shard_map/stack | solution.py:53
  129.3 8.5 %reshape.83 = f32[4,1,131072]{2,1,0:T(1,128)} reshape(f32[2048,2,4,32]{3,2,1,0:T(4,128)} %bitcast.84) | data formatting | bytes 4194304
  137.8 3.6 %all-to-all-start = ((f32[4,1,131072]{2,1,0:T(1,128)}), f32[4,1,131072]{2,1,0:T(1,128)S(1)}, u32[]{:S(2)}, u32[]{:S(2)}) async-start(f32[4,1,131072]{2,1,0:T(1,128)} %reshape.83), calls=%async_computation | async-start | bytes 4194304 | tf_op jit(solution)/shard_map/all_to_all | solution.py:93
  141.5 0.2 fusion.83
  141.7 25.4 %all-to-all-done = f32[4,1,131072]{2,1,0:T(1,128)S(1)} async-done(((f32[4,1,131072]{2,1,0:T(1,128)}), f32[4,1,131072]{2,1,0:T(1,128)S(1)}, u32[]{:S(2)}, u32[]{:S(2)}) %all-to-all-start) | async-done | bytes 2097184 | tf_op jit(solution)/shard_map/all_to_all | solution.py:93
  167.1 1.3 copy-done.1
  168.4 0.5 broadcast.200
  168.9 7.7 %reduce = f32[4,131072]{1,0:T(4,128)S(1)} reduce(f32[4,1,131072]{2,1,0:T(1,128)} %copy-done.1, f32[]{:T(128)} %broadcast.200), dimensions={1}, to_apply=%all_to_all.22.reduce_sub_computation | reduce | bytes 4194308 | tf_op jit(solution)/shard_map/all_to_all | solution.py:93
  176.6 7.8 %reshape.84 = f32[2048,2,4,32]{3,2,1,0:T(4,128)} reshape(f32[4,131072]{1,0:T(4,128)S(1)} %reduce) | data formatting | bytes 4194304
  184.5 6.9 %copy.73 = f32[2,32,4,4,512]{4,1,3,2,0:T(8,128)S(1)} copy(f32[2,32,4,4,512]{1,2,0,4,3:T(4,128)} %bitcast.85) | data formatting | bytes 4194304 | tf_op jit(solution)/shard_map/all_to_all | solution.py:93
  191.4 0.2 fusion.97
  191.6 1.1 convolution_multiply_fusion
  192.7 0.0 copy-start.4
  192.7 1.8 convolution_bitcast_fusion
  194.6 1.8 convolution_bitcast_fusion.1
  196.4 0.1 pad_maximum_fusion.21
  196.6 2.1 copy.76
  198.6 29.3 %all_to_all.30 = f32[2,128,4,512]{3,2,0,1:T(4,128)S(1)} all-to-all(f32[2,128,4,512]{3,2,0,1:T(4,128)} %copy.76), channel_id=1, replica_groups=mesh['lat'=8,'depth'=4] {'depth'}, dimensions={1} | all-to-all | bytes 4194304 | tf_op jit(solution)/shard_map/all_to_all | solution.py:100
  227.9 1.2 copy.77
  229.1 0.3 fusion.96
  229.4 0.7 copy.85
  230.1 1.9 reshape.82
  231.9 0.7 copy.84
  232.6 1.9 reshape.81
  (13 shorter events, 0.1 us)
Async XLA Ops:
  0.6 192.1 %copy-start = (f32[128,128]{1,0:T(8,128)S(1)}, f32[128,128]{1,0:T(8,128)}, u32[]{:S(2)}) copy-start(f32[128,128]{1,0:T(8,128)} %param.13) | copy-start | bytes 196612
  3.5 16.8 %collective-permute-start = (f32[2,32,1,2048]{3,1,2,0:T(8,128)S(1)}, f32[2,32,1,2048]{3,1,2,0:T(8,128)S(1)}, u32[]{:S(2)}, u32[]{:S(2)}) collective-permute-start(f32[2,32,1,2048]{3,1,2,0:T(8,128)S(1)} %get-tuple-element.38), channel_id=1, source_target_pairs={{4,0},{8,4},{12,8},{16,12},{20,16},{24,20},{28,24},{5,1},{9,5},{13... | collective-permute-start | bytes 1572872 | tf_op jit(solution)/shard_map/ppermute | solution.py:23
  4.8 6.5 %copy-start.5 = (s32[4,2048]{1,0:T(4,128)S(1)}, s32[4,2048]{1,0:T(4,128)}, u32[]{:S(2)}) copy-start(s32[4,2048]{1,0:T(4,128)} %param.9) | copy-start | bytes 98308
  4.8 6.5 %copy-start.6 = (f32[12]{0:T(128)S(1)}, f32[12]{0:T(128)}, u32[]{:S(2)}) copy-start(f32[12]{0:T(128)} %param.10) | copy-start | bytes 148
  4.9 6.5 %copy-start.7 = (f32[12]{0:T(128)S(1)}, f32[12]{0:T(128)}, u32[]{:S(2)}) copy-start(f32[12]{0:T(128)} %param.11) | copy-start | bytes 148
  4.9 26.8 %collective-permute-start.1 = (f32[2,32,1,2048]{3,1,2,0:T(8,128)S(1)}, f32[2,32,1,2048]{3,1,2,0:T(8,128)S(1)}, u32[]{:S(2)}, u32[]{:S(2)}) collective-permute-start(f32[2,32,1,2048]{3,1,2,0:T(8,128)S(1)} %get-tuple-element.39), channel_id=1, source_target_pairs={{0,4},{4,8},{8,12},{12,16},{16,20},{20,24},{24,28},{1,5},{5,9},{9,... | collective-permute-start | bytes 1572872 | tf_op jit(solution)/shard_map/ppermute | solution.py:21
  31.7 1.2 copy-start.2
  31.7 1.5 copy-start.3
  34.8 16.5 %collective-permute-start.2 = (f32[2,32,1,2048]{3,1,2,0:T(8,128)S(1)}, f32[2,32,1,2048]{3,1,2,0:T(8,128)S(1)}, u32[]{:S(2)}, u32[]{:S(2)}) collective-permute-start(f32[2,32,1,2048]{3,1,2,0:T(8,128)S(1)} %get-tuple-element.34), channel_id=1, source_target_pairs={{4,0},{8,4},{12,8},{16,12},{20,16},{24,20},{28,24},{5,1},{9,5},{13... | collective-permute-start | bytes 1572872 | tf_op jit(solution)/shard_map/ppermute | solution.py:23
  36.1 26.6 %collective-permute-start.3 = (f32[2,32,1,2048]{3,1,2,0:T(8,128)S(1)}, f32[2,32,1,2048]{3,1,2,0:T(8,128)S(1)}, u32[]{:S(2)}, u32[]{:S(2)}) collective-permute-start(f32[2,32,1,2048]{3,1,2,0:T(8,128)S(1)} %get-tuple-element.35), channel_id=1, source_target_pairs={{0,4},{4,8},{8,12},{12,16},{16,20},{20,24},{24,28},{1,5},{5,9},{9,... | collective-permute-start | bytes 1572872 | tf_op jit(solution)/shard_map/ppermute | solution.py:21
  64.3 16.5 %collective-permute-start.4 = (f32[2,32,1,2048]{3,1,2,0:T(8,128)S(1)}, f32[2,32,1,2048]{3,1,2,0:T(8,128)S(1)}, u32[]{:S(2)}, u32[]{:S(2)}) collective-permute-start(f32[2,32,1,2048]{3,1,2,0:T(8,128)S(1)} %get-tuple-element.30), channel_id=1, source_target_pairs={{4,0},{8,4},{12,8},{16,12},{20,16},{24,20},{28,24},{5,1},{9,5},{13... | collective-permute-start | bytes 1572872 | tf_op jit(solution)/shard_map/ppermute | solution.py:23
  65.6 26.6 %collective-permute-start.5 = (f32[2,32,1,2048]{3,1,2,0:T(8,128)S(1)}, f32[2,32,1,2048]{3,1,2,0:T(8,128)S(1)}, u32[]{:S(2)}, u32[]{:S(2)}) collective-permute-start(f32[2,32,1,2048]{3,1,2,0:T(8,128)S(1)} %get-tuple-element.31), channel_id=1, source_target_pairs={{0,4},{4,8},{8,12},{12,16},{16,20},{20,24},{24,28},{1,5},{5,9},{9,... | collective-permute-start | bytes 1572872 | tf_op jit(solution)/shard_map/ppermute | solution.py:21
  93.8 16.5 %collective-permute-start.6 = (f32[2,32,1,2048]{3,1,2,0:T(8,128)S(1)}, f32[2,32,1,2048]{3,1,2,0:T(8,128)S(1)}, u32[]{:S(2)}, u32[]{:S(2)}) collective-permute-start(f32[2,32,1,2048]{3,1,2,0:T(8,128)S(1)} %get-tuple-element.26), channel_id=1, source_target_pairs={{4,0},{8,4},{12,8},{16,12},{20,16},{24,20},{28,24},{5,1},{9,5},{13... | collective-permute-start | bytes 1572872 | tf_op jit(solution)/shard_map/ppermute | solution.py:23
  95.1 26.6 %collective-permute-start.7 = (f32[2,32,1,2048]{3,1,2,0:T(8,128)S(1)}, f32[2,32,1,2048]{3,1,2,0:T(8,128)S(1)}, u32[]{:S(2)}, u32[]{:S(2)}) collective-permute-start(f32[2,32,1,2048]{3,1,2,0:T(8,128)S(1)} %get-tuple-element.27), channel_id=1, source_target_pairs={{0,4},{4,8},{8,12},{12,16},{16,20},{20,24},{24,28},{1,5},{5,9},{9,... | collective-permute-start | bytes 1572872 | tf_op jit(solution)/shard_map/ppermute | solution.py:21
  137.8 29.3 %all-to-all-start = ((f32[4,1,131072]{2,1,0:T(1,128)}), f32[4,1,131072]{2,1,0:T(1,128)S(1)}, u32[]{:S(2)}, u32[]{:S(2)}) async-start(f32[4,1,131072]{2,1,0:T(1,128)} %reshape.83), calls=%async_computation | async-start | bytes 4194304 | tf_op jit(solution)/shard_map/all_to_all | solution.py:93
  167.1 1.3 copy-start.1
  192.7 1.8 copy-start.4
where the time goes:
time: 235 us; the launch traced here: 234 us
  waiting for transfers between devices  108 us (46%)
  local copies, waits for them, and re-layouts  43.1 us (18%)
  starting transfers between devices  29.8 us (13%)
  blocking collectives  29.3 us (12%)
  other arithmetic  19.1 us (8%)
  matrix products  4.72 us (2%)
    ppermute x4, waiting for transfers between devices, extended(): lax.ppermute(tail, axis, [(i, (i + 1) % count) for i in range(ends)])  45.5 us
    ppermute x4, waiting for transfers between devices, extended(): lax.ppermute(head, axis, [((i + 1) % count, i) for i in range(ends)])  36.6 us
    all_to_all x1, blocking collectives, per_device(): lax.all_to_all(solved, 'depth', split_axis=1, concat_axis=3, tiled=True)  29.3 us
    all_to_all x1, waiting for transfers between devices, per_device(): lax.all_to_all(profile_snapshot, 'depth', split_axis=3, concat_axis=1, ti...  25.4 us
    unnamed x22, local copies, waits for them, and re-layouts  23.2 us
    ppermute x4, starting transfers between devices, extended(): lax.ppermute(tail, axis, [(i, (i + 1) % count) for i in range(ends)])  21 us
    all_to_all x1, other arithmetic, per_device(): lax.all_to_all(profile_snapshot, 'depth', split_axis=3, concat_axis=1, ti...  7.72 us
    all_to_all x2, local copies, waits for them, and re-layouts, per_device(): lax.all_to_all(profile_snapshot, 'depth', split_axis=3, concat_axis=1, ti...  7.41 us
  transfers between devices with their start and end apart: 9, of which 9 were waited for; matrix products, arithmetic and copies ran while one was open for 2% of the time, Pallas kernels for 0%

commit v1 on v0

v1 whole, which is shorter than its diff:
```python
import functools

import jax
import jax.numpy as jnp
import numpy as np
from jax import lax
from jax.experimental import pallas as pl
from jax.experimental.pallas import tpu as pltpu
from jax.sharding import PartitionSpec as P

DEPTH = 128
SLAB = 32
ROWS = 4
RATE = 0.25
CHUNKS = 2
JOINT = ("lat", "depth")
BODY = 2 * ROWS * SLAB
VMEM_LIMIT = 48 * 1024 * 1024


def params():
    return pltpu.CompilerParams(vmem_limit_bytes=VMEM_LIMIT)


def cost(flops, nbytes):
    return pl.CostEstimate(flops=flops, bytes_accessed=nbytes, transcendentals=0)


def scaled_cheb(count):
    f32 = np.float32
    index = np.arange(count).astype(f32)
    nodes = np.cos((f32(np.pi) * index / f32(count - 1)).astype(f32)).astype(f32)
    ends = np.where((index == 0) | (index == count - 1), 2.0, 1.0)
    signs = np.where(np.arange(count) % 2 == 0, 1.0, -1.0)
    weight = (ends * signs).astype(f32)
    diagonal = np.eye(count, dtype=bool)
    spread = nodes[:, None] - nodes[None, :]
    off = weight[:, None] / weight[None, :] / np.where(diagonal, f32(1.0), spread)
    off = np.where(diagonal, f32(0.0), off).astype(f32)
    deriv = off - np.diag(np.sum(off, axis=1, dtype=f32))
    scale = (f32(1.0) - nodes * nodes) / f32(count)
    return (scale[:, None] * deriv).astype(f32)


def place():
    lat = lax.axis_index("lat")
    dep = lax.axis_index("depth")
    return lax.rem(lat, 2), lax.div(dep, 2), lax.rem(dep, 2)


def quarter():
    y, x, _ = place()
    return 2 * y + x


def column_start(k, mask, width):
    return pl.multiple_of((lax.bitwise_xor(quarter(), mask) * CHUNKS + k) * width, 128)


def lanes(shape):
    return lax.broadcasted_iota(jnp.int32, shape, len(shape) - 1)


def pack_kernel(k, width, heat_ref, wet_ref, label_ref, *blocks):
    columns = heat_ref.shape[2]
    lane = lanes((SLAB, 128))
    lane8 = lanes((8, 128))
    lane4 = lanes((ROWS, 128))
    for mask in range(4):
        start = column_start(k, mask, width)
        left = pl.multiple_of(jnp.maximum(start - 128, 0), 128)
        right = pl.multiple_of(jnp.minimum(start + width, columns - 128), 128)
        keep_left = (start > 0).astype(jnp.float32)
        keep_right = (start + width < columns).astype(jnp.float32)
        for f, ref in enumerate((heat_ref, wet_ref)):
            packed = jnp.zeros((8, 128), jnp.float32)
            for r in range(ROWS):
                base = (f * ROWS + r) * SLAB
                blocks[mask][base : base + SLAB, :] = ref[:, r, pl.ds(start, width)]
                edge = jnp.where(
                    lane >= 64,
                    ref[:, r, pl.ds(left, 128)] * keep_left,
                    ref[:, r, pl.ds(right, 128)] * keep_right,
                )
                for g in range(SLAB // 8):
                    at = 8 * (r * (SLAB // 8) + g)
                    moved = pltpu.roll(edge[8 * g : 8 * g + 8], (at + 4) % 128, 1)
                    packed = jnp.where((lane8 >= at) & (lane8 < at + 8), moved, packed)
            blocks[mask][BODY : BODY + 8, 128 * f : 128 * f + 128] = packed
        blocks[mask][BODY + 8 : BODY + 12, :] = (
            label_ref[:, pl.ds(start, width)] + 1
        ).astype(jnp.float32)
        edge = jnp.where(
            lane4 >= 124,
            (label_ref[:, pl.ds(left, 128)] + 1).astype(jnp.float32) * keep_left,
            (label_ref[:, pl.ds(right, 128)] + 1).astype(jnp.float32) * keep_right,
        )
        blocks[mask][BODY + 12 : BODY + 16, :] = jnp.zeros((ROWS, width), jnp.float32)
        blocks[mask][BODY + 12 : BODY + 16, :128] = jnp.where(
            (lane4 >= 124) | (lane4 < 4), edge, 0.0
        )


def pack(k, width, heat, wet, label):
    shape = jax.ShapeDtypeStruct((BODY + 16, width), jnp.float32)
    return pl.pallas_call(
        functools.partial(pack_kernel, k, width),
        out_shape=[shape] * 4,
        in_specs=[pl.BlockSpec(memory_space=pltpu.VMEM)] * 3,
        out_specs=[pl.BlockSpec(memory_space=pltpu.VMEM)] * 4,
        compiler_params=params(),
        cost_estimate=cost(0, 4 << 20),
        name="pack",
    )(heat, wet, label)


def prep_kernel(thermal_ref, water_ref, cheb_ref, stack_w_ref, stack_h_ref):
    _, x, c = place()
    dot = functools.partial(
        jnp.dot, precision=lax.Precision.HIGHEST, preferred_element_type=jnp.float32
    )

    def depth_of(n):
        slab, inner = lax.div(n, SLAB), lax.rem(n, SLAB)
        dx = lax.rem(slab, 2)
        dc = lax.div(slab, 2)
        return (2 * lax.rem(x + dx, 2) + lax.rem(c + dc, 2)) * SLAB + inner

    row = lax.broadcasted_iota(jnp.int32, (DEPTH, DEPTH), 0)
    col = lax.broadcasted_iota(jnp.int32, (DEPTH, DEPTH), 1)
    order = (row == depth_of(col)).astype(jnp.float32)
    picks = (depth_of(row[: 2 * SLAB]) == col[: 2 * SLAB]).astype(jnp.float32)
    thermal = dot(picks, thermal_ref[...])
    water = dot(picks, water_ref[...])
    cheb = cheb_ref[...]
    stack_w = jnp.concatenate(
        [water, -0.25 * dot(thermal, cheb), 0.5 * dot(water, cheb)], axis=0
    )
    for ref, stack in ((stack_w_ref, stack_w), (stack_h_ref, thermal)):
        ordered = dot(stack, order)
        high = ordered.astype(jnp.bfloat16)
        low = (ordered - high.astype(jnp.float32)).astype(jnp.bfloat16)
        count = ordered.shape[0]
        ref[:count, :] = high
        ref[count:, :] = low


def prep(thermal, water):
    cheb = jnp.asarray(scaled_cheb(DEPTH))
    return pl.pallas_call(
        prep_kernel,
        out_shape=[
            jax.ShapeDtypeStruct((12 * SLAB, DEPTH), jnp.bfloat16),
            jax.ShapeDtypeStruct((4 * SLAB, DEPTH), jnp.bfloat16),
        ],
        in_specs=[pl.BlockSpec(memory_space=pltpu.VMEM)] * 3,
        out_specs=[pl.BlockSpec(memory_space=pltpu.VMEM)] * 2,
        compiler_params=params(),
        cost_estimate=cost(1 << 24, 1 << 18),
        name="prep",
    )(thermal, water, cheb)


def substep(above, here, below, kappa_heat, kappa_moist):
    laps = []
    size = here[0].shape[1]
    for f in range(2):
        u = here[f]
        sides = pltpu.roll(u, 1, 1) + pltpu.roll(u, size - 1, 1)
        laps.append((above[f] + below[f]) + sides - 4.0 * u)
    heat, wet = here
    body = 1.0 + wet * wet
    guess = pl.reciprocal(body, approx=True)
    inverse = guess * (2.0 - body * guess)
    spread = kappa_heat * (1.5 - 0.5 * inverse)
    return heat + spread * laps[0], wet + kappa_moist * laps[1]


def factors(label, spread_ref, factor_ref):
    heat = jnp.zeros(label.shape, jnp.float32)
    moist = jnp.zeros(label.shape, jnp.float32)
    for i in range(spread_ref.shape[0]):
        here = label == i + 1.0
        heat = jnp.where(here, spread_ref[i], heat)
        moist = jnp.where(here, factor_ref[i], moist)
    return heat, moist


def stencil_kernel(
    width, own, rx, ry, rxy, p1, p2, spread_ref, factor_ref, post, km_ref, kap
):
    y, _, _ = place()
    count = 4 * ROWS
    for j, block in enumerate((p2.at[0], own, ry, p1.at[0])):
        label = block[BODY + 8 : BODY + 16, :]
        body = factors(label[:ROWS], spread_ref, factor_ref)
        edge = factors(label[ROWS:, :128], spread_ref, factor_ref)
        if 1 <= j < 3:
            km_ref[(j - 1) * ROWS : j * ROWS, :] = body[1]
        for f in range(2):
            whole = RATE * jnp.concatenate([body[f], edge[f]], axis=1)
            back = jnp.concatenate(
                [whole[r : r + 1] for r in reversed(range(ROWS))], axis=0
            )
            kap[f, j * ROWS : j * ROWS + ROWS, :] = jnp.where(y == 1, back, whole)

    def stored(r):
        return jnp.where(y == 1, ROWS - 1 - r, r)

    for s in range(2):
        blocks = (p2.at[s], (own, rx)[s], (ry, rxy)[s], p1.at[s])

        def group(g, carry):
            def load(j):
                block, r = blocks[j // ROWS], stored(j % ROWS)
                shift = lax.rem(252 - 8 * (r * (SLAB // 8) + g), 128)
                fields = []
                for f in range(2):
                    at = pl.multiple_of((f * ROWS + r) * SLAB + 8 * g, 8)
                    edge = pltpu.roll(
                        block[BODY : BODY + 8, 128 * f : 128 * f + 128], shift, 1
                    )
                    fields.append(jnp.concatenate([block[pl.ds(at, 8), :], edge], axis=1))
                return tuple(fields)

            levels = [dict() for _ in range(5)]
            for j in range(count + 4):
                if j < count:
                    levels[0][j] = load(j)
                for t in range(1, 5):
                    i = j - t
                    if t <= i < count - t:
                        prev = levels[t - 1]
                        levels[t][i] = substep(
                            prev[i - 1],
                            prev[i],
                            prev[i + 1],
                            kap[0, i : i + 1, :],
                            kap[1, i : i + 1, :],
                        )
                        if t == 4:
                            strip, r = divmod(i - ROWS, ROWS)
                            for f in range(2):
                                post[
                                    f,
                                    strip * ROWS + stored(r),
                                    pl.ds(pl.multiple_of(s * SLAB + 8 * g, 8), 8),
                                    :,
                                ] = levels[4][i][f][:, :width]
            return carry

        lax.fori_loop(0, SLAB // 8, group, 0)


def stencil(width, own, rx, ry, rxy, p1, p2, spread, factor):
    return pl.pallas_call(
        functools.partial(stencil_kernel, width),
        out_shape=[
            jax.ShapeDtypeStruct((2, 2 * ROWS, 2 * SLAB, width), jnp.float32),
            jax.ShapeDtypeStruct((2 * ROWS, width), jnp.float32),
        ],
        in_specs=[pl.BlockSpec(memory_space=pltpu.VMEM)] * 6
        + [pl.BlockSpec(memory_space=pltpu.SMEM)] * 2,
        out_specs=[pl.BlockSpec(memory_space=pltpu.VMEM)] * 2,
        scratch_shapes=[pltpu.VMEM((2, 4 * ROWS, width + 128), jnp.float32)],
        compiler_params=params(),
        cost_estimate=cost(1 << 24, 4 << 20),
        name="stencil",
    )(own, rx, ry, rxy, p1, p2, spread, factor)


def split(values):
    high = values.astype(jnp.bfloat16)
    return high, (values - high.astype(jnp.float32)).astype(jnp.bfloat16)


def solve_kernel(mine, other, stack_w, stack_h, km, *blocks):
    dot = functools.partial(jnp.dot, preferred_element_type=jnp.float32)
    half = 2 * SLAB

    def apply(stack, values):
        high, low = split(values)
        count = stack.shape[0] // 2
        both = dot(stack[...], high)
        return both[:count] + both[count:] + dot(stack[:count, :], low)

    for r in range(2 * ROWS):
        heat = apply(stack_h, jnp.concatenate([mine[0, r], other[0, r]], axis=0))
        wet = apply(stack_w, jnp.concatenate([mine[1, r], other[1, r]], axis=0))
        factor = km[r : r + 1, :]
        results = (
            heat + factor * wet[half : 2 * half],
            wet[:half] + factor * wet[2 * half :],
        )
        strip, inner = divmod(r, ROWS)
        for f in range(2):
            base = (f * ROWS + inner) * SLAB
            for slab in range(2):
                blocks[2 * strip + slab][base : base + SLAB, :] = results[f][
                    slab * SLAB : slab * SLAB + SLAB
                ]


def solve(width, mine, other, stack_w, stack_h, km):
    shape = jax.ShapeDtypeStruct((BODY, width), jnp.float32)
    return pl.pallas_call(
        solve_kernel,
        out_shape=[shape] * 4,
        in_specs=[pl.BlockSpec(memory_space=pltpu.VMEM)] * 5,
        out_specs=[pl.BlockSpec(memory_space=pltpu.VMEM)] * 4,
        compiler_params=params(),
        cost_estimate=cost(1 << 26, 4 << 20),
        name="solve",
    )(mine, other, stack_w, stack_h, km)


def assemble_kernel(width, *refs):
    blocks, outs = refs[:-2], refs[-2:]
    for k in range(CHUNKS):
        for mask in range(4):
            start = column_start(k, mask, width)
            for f in range(2):
                for r in range(ROWS):
                    base = (f * ROWS + r) * SLAB
                    outs[f][:, r, pl.ds(start, width)] = blocks[4 * k + mask][
                        base : base + SLAB, :
                    ]


def assemble(width, columns, blocks):
    shape = jax.ShapeDtypeStruct((SLAB, ROWS, columns), jnp.float32)
    return pl.pallas_call(
        functools.partial(assemble_kernel, width),
        out_shape=[shape] * 2,
        in_specs=[pl.BlockSpec(memory_space=pltpu.VMEM)] * len(blocks),
        out_specs=[pl.BlockSpec(memory_space=pltpu.VMEM)] * 2,
        compiler_params=params(),
        cost_estimate=cost(0, 4 << 20),
        name="assemble",
    )(*blocks)


def routes(strips):
    cells = [(l, d) for l in range(strips) for d in range(4)]

    def pairs(to):
        return [
            (l * 4 + d, to(l, d)[0] * 4 + to(l, d)[1])
            for l, d in cells
            if 0 <= to(l, d)[0] < strips
        ]

    return {
        "x": pairs(lambda l, d: (l, d ^ 2)),
        "y": pairs(lambda l, d: (l ^ 1, d)),
        "xy": pairs(lambda l, d: (l ^ 1, d ^ 2)),
        "core": pairs(lambda l, d: (l, d ^ 1)),
        "own": pairs(lambda l, d: (l + 2 if l % 2 else l - 2, d)),
        "partner": pairs(lambda l, d: (l - 2 if l % 2 else l + 2, d)),
    }


def per_device(strips, heat, wet, label, spread, factor, thermal, water):
    columns = heat.shape[2]
    width = columns // (4 * CHUNKS)
    route = routes(strips)

    def send(array, name):
        return lax.ppermute(array, JOINT, route[name])

    received = []
    for k in range(CHUNKS):
        own, bx, by, bxy = pack(k, width, heat, wet, label)
        received.append((own, send(bx, "x"), send(by, "y"), send(bxy, "xy")))
    stack_w, stack_h = prep(thermal, water)
    blocks = []
    for k in range(CHUNKS):
        own, rx, ry, rxy = received[k]
        p1 = send(jnp.stack([own, rx]), "own")
        p2 = send(jnp.stack([ry, rxy]), "partner")
        post, km = stencil(width, own, rx, ry, rxy, p1, p2, spread, factor)
        other = send(post, "core")
        kept, bx, by, bxy = solve(width, post, other, stack_w, stack_h, km)
        blocks += [kept, send(bx, "x"), send(by, "y"), send(bxy, "xy")]
    return tuple(assemble(width, columns, blocks))


def solution(mesh):
    return jax.shard_map(
        functools.partial(per_device, mesh.shape["lat"]),
        mesh=mesh,
        in_specs=(
            P("depth", "lat", None),
            P("depth", "lat", None),
            P("lat", None),
            P(),
            P(),
            P(),
            P(),
        ),
        out_specs=(P("depth", "lat", None), P("depth", "lat", None)),
        check_vma=False,
    )
```

time: 235 us -> 88.9 us (0.38)
  waiting for transfers between devices: 108 us -> 29.2 us
  local copies, waits for them, and re-layouts: 43.1 us -> 3.23 us
  blocking collectives: 29.3 us -> 0 us
  Pallas kernels: 0 us -> 22 us
  other arithmetic: 19.1 us -> 0.15 us
  matrix products: 4.72 us -> 0 us
  starting transfers between devices: 29.8 us -> 33.2 us
    ppermute x8 -> x18, waiting for transfers between devices: 82.2 us -> 29.2 us  [send(): return lax.ppermute(array, JOINT, route[name])]
    all_to_all x1 -> x0, blocking collectives: 29.3 us -> none  [per_device(): lax.all_to_all(solved, 'depth', split_axis=1, concat_axis=3, tiled=True)]
    all_to_all x1 -> x0, waiting for transfers between devices: 25.4 us -> none  [per_device(): lax.all_to_all(profile_snapshot, 'depth', split_axis=3, concat_axis=1, ti...]
    pallas_call x0 -> x8, Pallas kernels: none -> 22 us  [the longest x2 14.2 us: stencil(): pl.pallas_call(functools.partial(stencil_kernel, width), out_shape=[jax.S...]
    unnamed x22 -> x16, local copies, waits for them, and re-layouts: 23.2 us -> 3.23 us
    another operation x3 -> x0, local copies, waits for them, and re-layouts: 10.7 us -> none  [the longest x1 5.88 us: advance(): jnp.stack([profile_snapshot[0] + RATE * kappa_t * lap[0], profile_snapsho...]
    all_to_all x3 -> x0, local copies, waits for them, and re-layouts: 8.63 us -> none  [the longest x2 7.41 us: per_device(): lax.all_to_all(profile_snapshot, 'depth', split_axis=3, concat_axis=1, ti...]
    all_to_all x1 -> x0, other arithmetic: 7.72 us -> none  [per_device(): lax.all_to_all(profile_snapshot, 'depth', split_axis=3, concat_axis=1, ti...]
  transfers between devices with their start and end apart: 9 -> 18, of which waited for: 9 -> 12; matrix products, arithmetic and copies ran while one was open for 2% -> 0% of each run, Pallas kernels for 0% -> 21%
where the time goes in v1:
time: 88.9 us; the launch traced here: 88.6 us
  starting transfers between devices  33.2 us (37%)
  waiting for transfers between devices  29.2 us (33%)
  Pallas kernels  22 us (25%)
  local copies, waits for them, and re-layouts  3.23 us (4%)
    ppermute x18, starting transfers between devices, send(): return lax.ppermute(array, JOINT, route[name])  33.2 us
    ppermute x18, waiting for transfers between devices, send(): return lax.ppermute(array, JOINT, route[name])  29.2 us
    pallas_call x2, Pallas kernels, stencil(): pl.pallas_call(functools.partial(stencil_kernel, width), out_shape=[jax.S...  14.2 us
    unnamed x16, local copies, waits for them, and re-layouts  3.23 us
    pallas_call x2, Pallas kernels, pack(): pl.pallas_call(functools.partial(pack_kernel, k, width), out_shape=[shape...  2.88 us
    pallas_call x1, Pallas kernels, assemble(): pl.pallas_call(functools.partial(assemble_kernel, width), out_shape=[shap...  2.29 us
    pallas_call x2, Pallas kernels, solve(): pl.pallas_call(solve_kernel, out_shape=[shape] * 4, in_specs=[pl.BlockSpe...  1.96 us
  transfers between devices with their start and end apart: 18, of which 12 were waited for; matrix products, arithmetic and copies ran while one was open for 0% of the time, Pallas kernels for 21%

profile of v1, /device:TPU:0, one launch (start us, length us, event | category | flops | bytes accessed | tf_op | source)
XLA Modules:
  0.0 88.6 jit_solution(4176004507592408607)
XLA Ops:
  0.6 0.0 copy-start
  0.6 1.2 %copy-done = f32[32,4,2048]{2,1,0:T(4,128)S(1)} copy-done((f32[32,4,2048]{2,1,0:T(4,128)S(1)}, f32[32,4,2048]{2,1,0:T(4,128)}, u32[]{:S(2)}) %copy-start) | copy-done | bytes 1048600
  1.9 0.0 copy-start.1
  1.9 1.2 %copy-done.1 = f32[32,4,2048]{2,1,0:T(4,128)S(1)} copy-done((f32[32,4,2048]{2,1,0:T(4,128)S(1)}, f32[32,4,2048]{2,1,0:T(4,128)}, u32[]{:S(2)}) %copy-start.1) | copy-done | bytes 1048600
  3.1 0.0 copy-start.2
  3.1 0.8 copy-done.2
  3.8 1.4 %pack.3 = (f32[272,256]{1,0:T(8,128)S(1)}, f32[272,256]{1,0:T(8,128)S(1)}, f32[272,256]{1,0:T(8,128)S(1)}, f32[272,256]{1,0:T(8,128)S(1)}) custom-call(f32[32,4,2048]{2,1,0:T(4,128)S(1)} %copy-done, f32[32,4,2048]{2,1,0:T(4,128)S(1)} %copy-done.1, s32[4,2048]{1,0:T(4,128)S(1)} %copy-done.2), custom_call_target="tpu_custom_call" | custom-call | bytes 4194304 | tf_op jit(solution)/shard_map/pack/pallas_call | solution.py:106
  5.3 3.0 %collective-permute-start.9 = (f32[272,256]{1,0:T(8,128)S(1)}, f32[272,256]{1,0:T(8,128)S(1)}, u32[]{:S(2)}, u32[]{:S(2)}) collective-permute-start(f32[272,256]{1,0:T(8,128)S(1)} %get-tuple-element.37), channel_id=1, source_target_pairs={{0,2},{1,3},{2,0},{3,1},{4,6},{5,7},{6,4},{7,5},{8,10},{9,11},{10,... | collective-permute-start | bytes 835592 | tf_op jit(solution)/shard_map/ppermute | solution.py:369
  8.3 1.5 %collective-permute-start.10 = (f32[272,256]{1,0:T(8,128)S(1)}, f32[272,256]{1,0:T(8,128)S(1)}, u32[]{:S(2)}, u32[]{:S(2)}) collective-permute-start(f32[272,256]{1,0:T(8,128)S(1)} %get-tuple-element.38), channel_id=1, source_target_pairs={{0,4},{1,5},{2,6},{3,7},{4,0},{5,1},{6,2},{7,3},{8,12},{9,13},{10,... | collective-permute-start | bytes 835592 | tf_op jit(solution)/shard_map/ppermute | solution.py:369
  9.8 0.0 collective-permute-start.11
  9.8 1.4 %pack.2 = (f32[272,256]{1,0:T(8,128)S(1)}, f32[272,256]{1,0:T(8,128)S(1)}, f32[272,256]{1,0:T(8,128)S(1)}, f32[272,256]{1,0:T(8,128)S(1)}) custom-call(f32[32,4,2048]{2,1,0:T(4,128)S(1)} %copy-done, f32[32,4,2048]{2,1,0:T(4,128)S(1)} %copy-done.1, s32[4,2048]{1,0:T(4,128)S(1)} %copy-done.2), custom_call_target="tpu_custom_call" | custom-call | bytes 4194304 | tf_op jit(solution)/shard_map/pack/pallas_call | solution.py:106
  11.3 2.0 %collective-permute-start = (f32[272,256]{1,0:T(8,128)S(1)}, f32[272,256]{1,0:T(8,128)S(1)}, u32[]{:S(2)}, u32[]{:S(2)}) collective-permute-start(f32[272,256]{1,0:T(8,128)S(1)} %get-tuple-element.25), channel_id=1, source_target_pairs={{0,2},{1,3},{2,0},{3,1},{4,6},{5,7},{6,4},{7,5},{8,10},{9,11},{10,... | collective-permute-start | bytes 835592 | tf_op jit(solution)/shard_map/ppermute | solution.py:369
  13.3 1.5 %collective-permute-start.1 = (f32[272,256]{1,0:T(8,128)S(1)}, f32[272,256]{1,0:T(8,128)S(1)}, u32[]{:S(2)}, u32[]{:S(2)}) collective-permute-start(f32[272,256]{1,0:T(8,128)S(1)} %get-tuple-element.26), channel_id=1, source_target_pairs={{0,4},{1,5},{2,6},{3,7},{4,0},{5,1},{6,2},{7,3},{8,12},{9,13},{10,... | collective-permute-start | bytes 835592 | tf_op jit(solution)/shard_map/ppermute | solution.py:369
  14.8 1.0 %collective-permute-done.9.rx = f32[272,256]{1,0:T(8,128)S(1)} collective-permute-done((f32[272,256]{1,0:T(8,128)S(1)}, f32[272,256]{1,0:T(8,128)S(1)}, u32[]{:S(2)}, u32[]{:S(2)}) %collective-permute-start.9) | collective-permute-done | bytes 278560 | tf_op jit(solution)/shard_map/ppermute | solution.py:369
  15.8 3.0 %collective-permute-start.2 = (f32[272,256]{1,0:T(8,128)S(1)}, f32[272,256]{1,0:T(8,128)S(1)}, u32[]{:S(2)}, u32[]{:S(2)}) collective-permute-start(f32[272,256]{1,0:T(8,128)S(1)} %get-tuple-element.27), channel_id=1, source_target_pairs={{0,6},{1,7},{2,4},{3,5},{4,2},{5,3},{6,0},{7,1},{8,14},{9,15},{10,... | collective-permute-start | bytes 835592 | tf_op jit(solution)/shard_map/ppermute | solution.py:369
  18.8 5.0 %collective-permute-done.10.ry = f32[272,256]{1,0:T(8,128)S(1)} collective-permute-done((f32[272,256]{1,0:T(8,128)S(1)}, f32[272,256]{1,0:T(8,128)S(1)}, u32[]{:S(2)}, u32[]{:S(2)}) %collective-permute-start.10) | collective-permute-done | bytes 278560 | tf_op jit(solution)/shard_map/ppermute | solution.py:369
  23.8 1.3 %collective-permute-start.12 = (f32[2,272,256]{2,1,0:T(8,128)S(1)}, f32[2,272,256]{2,1,0:T(8,128)S(1)}, u32[]{:S(2)}, u32[]{:S(2)}) collective-permute-start(f32[2,272,256]{2,1,0:T(8,128)S(1)} %pad_maximum_fusion.2), channel_id=1, source_target_pairs={{4,12},{5,13},{6,14},{7,15},{8,0},{9,1},{10,2},{11,3},{12,20},{13,... | collective-permute-start | bytes 1671176 | tf_op jit(solution)/shard_map/ppermute | solution.py:369
  25.1 0.0 collective-permute-done.11.rxy
  25.2 4.6 %collective-permute-start.13 = (f32[2,272,256]{2,1,0:T(8,128)S(1)}, f32[2,272,256]{2,1,0:T(8,128)S(1)}, u32[]{:S(2)}, u32[]{:S(2)}) collective-permute-start(f32[2,272,256]{2,1,0:T(8,128)S(1)} %pad_maximum_fusion.3), channel_id=1, source_target_pairs={{0,8},{1,9},{2,10},{3,11},{8,16},{9,17},{10,18},{11,19},{12,4},{13... | collective-permute-start | bytes 1671176 | tf_op jit(solution)/shard_map/ppermute | solution.py:369
  29.8 0.0 collective-permute-done.rx
  29.8 1.3 %collective-permute-start.3 = (f32[2,272,256]{2,1,0:T(8,128)S(1)}, f32[2,272,256]{2,1,0:T(8,128)S(1)}, u32[]{:S(2)}, u32[]{:S(2)}) collective-permute-start(f32[2,272,256]{2,1,0:T(8,128)S(1)} %pad_maximum_fusion), channel_id=1, source_target_pairs={{4,12},{5,13},{6,14},{7,15},{8,0},{9,1},{10,2},{11,3},{12,20},{13,... | collective-permute-start | bytes 1671176 | tf_op jit(solution)/shard_map/ppermute | solution.py:369
  31.1 3.2 %collective-permute-done.1.ry = f32[272,256]{1,0:T(8,128)S(1)} collective-permute-done((f32[272,256]{1,0:T(8,128)S(1)}, f32[272,256]{1,0:T(8,128)S(1)}, u32[]{:S(2)}, u32[]{:S(2)}) %collective-permute-start.1) | collective-permute-done | bytes 278560 | tf_op jit(solution)/shard_map/ppermute | solution.py:369
  34.3 0.0 collective-permute-done.2.rxy
  34.3 0.0 copy-start.6
  34.3 0.0 copy-start.7
  34.4 3.5 %collective-permute-start.4 = (f32[2,272,256]{2,1,0:T(8,128)S(1)}, f32[2,272,256]{2,1,0:T(8,128)S(1)}, u32[]{:S(2)}, u32[]{:S(2)}) collective-permute-start(f32[2,272,256]{2,1,0:T(8,128)S(1)} %pad_maximum_fusion.1), channel_id=1, source_target_pairs={{0,8},{1,9},{2,10},{3,11},{8,16},{9,17},{10,18},{11,19},{12,4},{13... | collective-permute-start | bytes 1671176 | tf_op jit(solution)/shard_map/ppermute | solution.py:369
  37.9 1.8 %collective-permute-done.12.p1 = f32[2,272,256]{2,1,0:T(8,128)S(1)} collective-permute-done((f32[2,272,256]{2,1,0:T(8,128)S(1)}, f32[2,272,256]{2,1,0:T(8,128)S(1)}, u32[]{:S(2)}, u32[]{:S(2)}) %collective-permute-start.12) | collective-permute-done | bytes 557088 | tf_op jit(solution)/shard_map/ppermute | solution.py:369
  39.7 0.0 collective-permute-done.13.p2
  39.7 0.0 copy-done.6
  39.7 0.0 copy-done.7
  39.7 7.1 %stencil.3 = (f32[2,8,64,256]{3,2,1,0:T(8,128)S(1)}, f32[8,256]{1,0:T(8,128)S(1)}) custom-call(f32[272,256]{1,0:T(8,128)S(1)} %get-tuple-element.36.own, f32[272,256]{1,0:T(8,128)S(1)} %collective-permute-done.9.rx, f32[272,256]{1,0:T(8,128)S(1)} %collective-permute-done.10.ry, f32[272,256]{1,0:T(8,128)S(1)} %collective-permute-done.11.rxy, ...), custom_call_target="tpu_custom_call" | custom-call | flops 16777216 | bytes 4194304 | tf_op jit(solution)/shard_map/stencil/pallas_call | solution.py:256
  46.8 0.0 copy-start.3
  46.8 0.0 copy-start.4
  46.8 0.0 copy-start.5
  46.9 0.1 collective-permute-start.14
  46.9 0.3 collective-permute-done.3.p1
  47.2 1.5 %collective-permute-done.4.p2 = f32[2,272,256]{2,1,0:T(8,128)S(1)} collective-permute-done((f32[2,272,256]{2,1,0:T(8,128)S(1)}, f32[2,272,256]{2,1,0:T(8,128)S(1)}, u32[]{:S(2)}, u32[]{:S(2)}) %collective-permute-start.4) | collective-permute-done | bytes 557088 | tf_op jit(solution)/shard_map/ppermute | solution.py:369
  48.7 7.1 %stencil.2 = (f32[2,8,64,256]{3,2,1,0:T(8,128)S(1)}, f32[8,256]{1,0:T(8,128)S(1)}) custom-call(f32[272,256]{1,0:T(8,128)S(1)} %get-tuple-element.24.own, f32[272,256]{1,0:T(8,128)S(1)} %collective-permute-done.rx, f32[272,256]{1,0:T(8,128)S(1)} %collective-permute-done.1.ry, f32[272,256]{1,0:T(8,128)S(1)} %collective-permute-done.2.rxy, ...), custom_call_target="tpu_custom_call" | custom-call | flops 16777216 | bytes 4194304 | tf_op jit(solution)/shard_map/stencil/pallas_call | solution.py:256
  55.8 0.1 collective-permute-start.5
  55.9 0.0 copy-done.3
  55.9 0.0 copy-done.4
  55.9 0.0 copy-done.5
  55.9 0.7 prep.1
  56.6 0.0 collective-permute-done.14.other
  56.7 1.0 %solve.3 = (f32[256,256]{1,0:T(8,128)S(1)}, f32[256,256]{1,0:T(8,128)S(1)}, f32[256,256]{1,0:T(8,128)S(1)}, f32[256,256]{1,0:T(8,128)S(1)}) custom-call(f32[2,8,64,256]{3,2,1,0:T(8,128)S(1)} %get-tuple-element.40.mine, f32[2,8,64,256]{3,2,1,0:T(8,128)S(1)} %collective-permute-done.14.other, bf16[384,128]{1,0:T(8,128)(2,1)S(1)} %get-tuple-element.29.stack_w, ...), custom_call_target="tpu_custom_call" | custom-call | flops 67108864 | bytes 4194304 | tf_op jit(solution)/shard_map/solve/pallas_call | solution.py:306
  57.7 1.5 %collective-permute-start.15 = (f32[256,256]{1,0:T(8,128)S(1)}, f32[256,256]{1,0:T(8,128)S(1)}, u32[]{:S(2)}, u32[]{:S(2)}) collective-permute-start(f32[256,256]{1,0:T(8,128)S(1)} %get-tuple-element.43), channel_id=1, source_target_pairs={{0,2},{1,3},{2,0},{3,1},{4,6},{5,7},{6,4},{7,5},{8,10},{9,11},{10,... | collective-permute-start | bytes 786440 | tf_op jit(solution)/shard_map/ppermute | solution.py:369
  59.1 2.7 %collective-permute-start.16 = (f32[256,256]{1,0:T(8,128)S(1)}, f32[256,256]{1,0:T(8,128)S(1)}, u32[]{:S(2)}, u32[]{:S(2)}) collective-permute-start(f32[256,256]{1,0:T(8,128)S(1)} %get-tuple-element.44), channel_id=1, source_target_pairs={{0,4},{1,5},{2,6},{3,7},{4,0},{5,1},{6,2},{7,3},{8,12},{9,13},{10,... | collective-permute-start | bytes 786440 | tf_op jit(solution)/shard_map/ppermute | solution.py:369
  61.8 0.9 %collective-permute-start.17 = (f32[256,256]{1,0:T(8,128)S(1)}, f32[256,256]{1,0:T(8,128)S(1)}, u32[]{:S(2)}, u32[]{:S(2)}) collective-permute-start(f32[256,256]{1,0:T(8,128)S(1)} %get-tuple-element.45), channel_id=1, source_target_pairs={{0,6},{1,7},{2,4},{3,5},{4,2},{5,3},{6,0},{7,1},{8,14},{9,15},{10,... | collective-permute-start | bytes 786440 | tf_op jit(solution)/shard_map/ppermute | solution.py:369
  62.8 0.0 collective-permute-done.5.other
  62.8 1.0 %solve.2 = (f32[256,256]{1,0:T(8,128)S(1)}, f32[256,256]{1,0:T(8,128)S(1)}, f32[256,256]{1,0:T(8,128)S(1)}, f32[256,256]{1,0:T(8,128)S(1)}) custom-call(f32[2,8,64,256]{3,2,1,0:T(8,128)S(1)} %get-tuple-element.28.mine, f32[2,8,64,256]{3,2,1,0:T(8,128)S(1)} %collective-permute-done.5.other, bf16[384,128]{1,0:T(8,128)(2,1)S(1)} %get-tuple-element.29.stack_w, ...), custom_call_target="tpu_custom_call" | custom-call | flops 67108864 | bytes 4194304 | tf_op jit(solution)/shard_map/solve/pallas_call | solution.py:306
  63.8 0.6 collective-permute-start.6
  64.4 2.0 %collective-permute-start.7 = (f32[256,256]{1,0:T(8,128)S(1)}, f32[256,256]{1,0:T(8,128)S(1)}, u32[]{:S(2)}, u32[]{:S(2)}) collective-permute-start(f32[256,256]{1,0:T(8,128)S(1)} %get-tuple-element.34), channel_id=1, source_target_pairs={{0,4},{1,5},{2,6},{3,7},{4,0},{5,1},{6,2},{7,3},{8,12},{9,13},{10,... | collective-permute-start | bytes 786440 | tf_op jit(solution)/shard_map/ppermute | solution.py:369
  66.4 0.4 collective-permute-done.15.refs_5_
  66.8 3.6 %collective-permute-start.8 = (f32[256,256]{1,0:T(8,128)S(1)}, f32[256,256]{1,0:T(8,128)S(1)}, u32[]{:S(2)}, u32[]{:S(2)}) collective-permute-start(f32[256,256]{1,0:T(8,128)S(1)} %get-tuple-element.35), channel_id=1, source_target_pairs={{0,6},{1,7},{2,4},{3,5},{4,2},{5,3},{6,0},{7,1},{8,14},{9,15},{10,... | collective-permute-start | bytes 786440 | tf_op jit(solution)/shard_map/ppermute | solution.py:369
  70.4 3.7 %collective-permute-done.16.refs_6_ = f32[256,256]{1,0:T(8,128)S(1)} collective-permute-done((f32[256,256]{1,0:T(8,128)S(1)}, f32[256,256]{1,0:T(8,128)S(1)}, u32[]{:S(2)}, u32[]{:S(2)}) %collective-permute-start.16) | collective-permute-done | bytes 262176 | tf_op jit(solution)/shard_map/ppermute | solution.py:369
  74.1 1.4 %collective-permute-done.17.refs_7_ = f32[256,256]{1,0:T(8,128)S(1)} collective-permute-done((f32[256,256]{1,0:T(8,128)S(1)}, f32[256,256]{1,0:T(8,128)S(1)}, u32[]{:S(2)}, u32[]{:S(2)}) %collective-permute-start.17) | collective-permute-done | bytes 262176 | tf_op jit(solution)/shard_map/ppermute | solution.py:369
  75.5 2.6 %collective-permute-done.6.refs_1_ = f32[256,256]{1,0:T(8,128)S(1)} collective-permute-done((f32[256,256]{1,0:T(8,128)S(1)}, f32[256,256]{1,0:T(8,128)S(1)}, u32[]{:S(2)}, u32[]{:S(2)}) %collective-permute-start.6) | collective-permute-done | bytes 262176 | tf_op jit(solution)/shard_map/ppermute | solution.py:369
  78.1 6.5 %collective-permute-done.7.refs_2_ = f32[256,256]{1,0:T(8,128)S(1)} collective-permute-done((f32[256,256]{1,0:T(8,128)S(1)}, f32[256,256]{1,0:T(8,128)S(1)}, u32[]{:S(2)}, u32[]{:S(2)}) %collective-permute-start.7) | collective-permute-done | bytes 262176 | tf_op jit(solution)/shard_map/ppermute | solution.py:369
  84.6 1.7 %collective-permute-done.8.refs_3_ = f32[256,256]{1,0:T(8,128)S(1)} collective-permute-done((f32[256,256]{1,0:T(8,128)S(1)}, f32[256,256]{1,0:T(8,128)S(1)}, u32[]{:S(2)}, u32[]{:S(2)}) %collective-permute-start.8) | collective-permute-done | bytes 262176 | tf_op jit(solution)/shard_map/ppermute | solution.py:369
  86.3 2.3 %assemble.1 = (f32[32,4,2048]{2,1,0:T(4,128)}, f32[32,4,2048]{2,1,0:T(4,128)}) custom-call(f32[256,256]{1,0:T(8,128)S(1)} %get-tuple-element.32.refs_0_, f32[256,256]{1,0:T(8,128)S(1)} %collective-permute-done.6.refs_1_, f32[256,256]{1,0:T(8,128)S(1)} %collective-permute-done.7.refs_2_, f32[256,256]{1,0:T(8,128)S(1)} %collective-permute-done.8.refs_3_, ...), custom_call_target="tpu_custom_call" | custom-call | bytes 4194304 | tf_op jit(solution)/shard_map/assemble/pallas_call | solution.py:332
  (4 shorter events, 0.2 us)
Async XLA Ops:
  0.6 1.2 %copy-start = (f32[32,4,2048]{2,1,0:T(4,128)S(1)}, f32[32,4,2048]{2,1,0:T(4,128)}, u32[]{:S(2)}) copy-start(f32[32,4,2048]{2,1,0:T(4,128)} %heat_ref.3) | copy-start | bytes 3145732
  1.9 1.2 %copy-start.1 = (f32[32,4,2048]{2,1,0:T(4,128)S(1)}, f32[32,4,2048]{2,1,0:T(4,128)}, u32[]{:S(2)}) copy-start(f32[32,4,2048]{2,1,0:T(4,128)} %wet_ref.3) | copy-start | bytes 3145732
  3.1 0.8 copy-start.2
  5.3 10.5 %collective-permute-start.9 = (f32[272,256]{1,0:T(8,128)S(1)}, f32[272,256]{1,0:T(8,128)S(1)}, u32[]{:S(2)}, u32[]{:S(2)}) collective-permute-start(f32[272,256]{1,0:T(8,128)S(1)} %get-tuple-element.37), channel_id=1, source_target_pairs={{0,2},{1,3},{2,0},{3,1},{4,6},{5,7},{6,4},{7,5},{8,10},{9,11},{10,... | collective-permute-start | bytes 835592 | tf_op jit(solution)/shard_map/ppermute | solution.py:369
  8.3 15.6 %collective-permute-start.10 = (f32[272,256]{1,0:T(8,128)S(1)}, f32[272,256]{1,0:T(8,128)S(1)}, u32[]{:S(2)}, u32[]{:S(2)}) collective-permute-start(f32[272,256]{1,0:T(8,128)S(1)} %get-tuple-element.38), channel_id=1, source_target_pairs={{0,4},{1,5},{2,6},{3,7},{4,0},{5,1},{6,2},{7,3},{8,12},{9,13},{10,... | collective-permute-start | bytes 835592 | tf_op jit(solution)/shard_map/ppermute | solution.py:369
  9.8 15.3 %collective-permute-start.11 = (f32[272,256]{1,0:T(8,128)S(1)}, f32[272,256]{1,0:T(8,128)S(1)}, u32[]{:S(2)}, u32[]{:S(2)}) collective-permute-start(f32[272,256]{1,0:T(8,128)S(1)} %get-tuple-element.39), channel_id=1, source_target_pairs={{0,6},{1,7},{2,4},{3,5},{4,2},{5,3},{6,0},{7,1},{8,14},{9,15},{10,... | collective-permute-start | bytes 835592 | tf_op jit(solution)/shard_map/ppermute | solution.py:369
  11.3 18.5 %collective-permute-start = (f32[272,256]{1,0:T(8,128)S(1)}, f32[272,256]{1,0:T(8,128)S(1)}, u32[]{:S(2)}, u32[]{:S(2)}) collective-permute-start(f32[272,256]{1,0:T(8,128)S(1)} %get-tuple-element.25), channel_id=1, source_target_pairs={{0,2},{1,3},{2,0},{3,1},{4,6},{5,7},{6,4},{7,5},{8,10},{9,11},{10,... | collective-permute-start | bytes 835592 | tf_op jit(solution)/shard_map/ppermute | solution.py:369
  13.3 21.0 %collective-permute-start.1 = (f32[272,256]{1,0:T(8,128)S(1)}, f32[272,256]{1,0:T(8,128)S(1)}, u32[]{:S(2)}, u32[]{:S(2)}) collective-permute-start(f32[272,256]{1,0:T(8,128)S(1)} %get-tuple-element.26), channel_id=1, source_target_pairs={{0,4},{1,5},{2,6},{3,7},{4,0},{5,1},{6,2},{7,3},{8,12},{9,13},{10,... | collective-permute-start | bytes 835592 | tf_op jit(solution)/shard_map/ppermute | solution.py:369
  15.8 18.5 %collective-permute-start.2 = (f32[272,256]{1,0:T(8,128)S(1)}, f32[272,256]{1,0:T(8,128)S(1)}, u32[]{:S(2)}, u32[]{:S(2)}) collective-permute-start(f32[272,256]{1,0:T(8,128)S(1)} %get-tuple-element.27), channel_id=1, source_target_pairs={{0,6},{1,7},{2,4},{3,5},{4,2},{5,3},{6,0},{7,1},{8,14},{9,15},{10,... | collective-permute-start | bytes 835592 | tf_op jit(solution)/shard_map/ppermute | solution.py:369
  23.8 15.9 %collective-permute-start.12 = (f32[2,272,256]{2,1,0:T(8,128)S(1)}, f32[2,272,256]{2,1,0:T(8,128)S(1)}, u32[]{:S(2)}, u32[]{:S(2)}) collective-permute-start(f32[2,272,256]{2,1,0:T(8,128)S(1)} %pad_maximum_fusion.2), channel_id=1, source_target_pairs={{4,12},{5,13},{6,14},{7,15},{8,0},{9,1},{10,2},{11,3},{12,20},{13,... | collective-permute-start | bytes 1671176 | tf_op jit(solution)/shard_map/ppermute | solution.py:369
  25.2 14.5 %collective-permute-start.13 = (f32[2,272,256]{2,1,0:T(8,128)S(1)}, f32[2,272,256]{2,1,0:T(8,128)S(1)}, u32[]{:S(2)}, u32[]{:S(2)}) collective-permute-start(f32[2,272,256]{2,1,0:T(8,128)S(1)} %pad_maximum_fusion.3), channel_id=1, source_target_pairs={{0,8},{1,9},{2,10},{3,11},{8,16},{9,17},{10,18},{11,19},{12,4},{13... | collective-permute-start | bytes 1671176 | tf_op jit(solution)/shard_map/ppermute | solution.py:369
  29.8 17.4 %collective-permute-start.3 = (f32[2,272,256]{2,1,0:T(8,128)S(1)}, f32[2,272,256]{2,1,0:T(8,128)S(1)}, u32[]{:S(2)}, u32[]{:S(2)}) collective-permute-start(f32[2,272,256]{2,1,0:T(8,128)S(1)} %pad_maximum_fusion), channel_id=1, source_target_pairs={{4,12},{5,13},{6,14},{7,15},{8,0},{9,1},{10,2},{11,3},{12,20},{13,... | collective-permute-start | bytes 1671176 | tf_op jit(solution)/shard_map/ppermute | solution.py:369
  34.3 5.4 %copy-start.6 = (f32[12]{0:T(128)S(1)}, f32[12]{0:T(128)}, u32[]{:S(2)}) copy-start(f32[12]{0:T(128)} %spread_ref.3) | copy-start | bytes 148
  34.3 5.4 %copy-start.7 = (f32[12]{0:T(128)S(1)}, f32[12]{0:T(128)}, u32[]{:S(2)}) copy-start(f32[12]{0:T(128)} %factor_ref.3) | copy-start | bytes 148
  34.4 14.3 %collective-permute-start.4 = (f32[2,272,256]{2,1,0:T(8,128)S(1)}, f32[2,272,256]{2,1,0:T(8,128)S(1)}, u32[]{:S(2)}, u32[]{:S(2)}) collective-permute-start(f32[2,272,256]{2,1,0:T(8,128)S(1)} %pad_maximum_fusion.1), channel_id=1, source_target_pairs={{0,8},{1,9},{2,10},{3,11},{8,16},{9,17},{10,18},{11,19},{12,4},{13... | collective-permute-start | bytes 1671176 | tf_op jit(solution)/shard_map/ppermute | solution.py:369
  46.8 9.1 %copy-start.3 = (f32[128,128]{1,0:T(8,128)S(1)}, f32[128,128]{1,0:T(8,128)}, u32[]{:S(2)}) copy-start(f32[128,128]{1,0:T(8,128)} %thermal_ref.1) | copy-start | bytes 196612
  46.8 9.1 %copy-start.4 = (f32[128,128]{1,0:T(8,128)S(1)}, f32[128,128]{1,0:T(8,128)}, u32[]{:S(2)}) copy-start(f32[128,128]{1,0:T(8,128)} %water_ref.1) | copy-start | bytes 196612
  46.8 9.1 %copy-start.5 = (f32[128,128]{1,0:T(8,128)S(1)}, f32[128,128]{1,0:T(8,128)}, u32[]{:S(2)}) copy-start(f32[128,128]{1,0:T(8,128)} %constant.2.clone.cheb_ref) | copy-start | bytes 196612
  46.9 9.8 %collective-permute-start.14 = (f32[2,8,64,256]{3,2,1,0:T(8,128)S(1)}, f32[2,8,64,256]{3,2,1,0:T(8,128)S(1)}, u32[]{:S(2)}, u32[]{:S(2)}) collective-permute-start(f32[2,8,64,256]{3,2,1,0:T(8,128)S(1)} %get-tuple-element.40.mine), channel_id=1, source_target_pairs={{0,1},{1,0},{2,3},{3,2},{4,5},{5,4},{6,7},{7,6},{8,9},{9,8},{10,11... | collective-permute-start | bytes 3145736 | tf_op jit(solution)/shard_map/ppermute | solution.py:369
  55.8 7.0 %collective-permute-start.5 = (f32[2,8,64,256]{3,2,1,0:T(8,128)S(1)}, f32[2,8,64,256]{3,2,1,0:T(8,128)S(1)}, u32[]{:S(2)}, u32[]{:S(2)}) collective-permute-start(f32[2,8,64,256]{3,2,1,0:T(8,128)S(1)} %get-tuple-element.28.mine), channel_id=1, source_target_pairs={{0,1},{1,0},{2,3},{3,2},{4,5},{5,4},{6,7},{7,6},{8,9},{9,8},{10,11... | collective-permute-start | bytes 3145736 | tf_op jit(solution)/shard_map/ppermute | solution.py:369
  57.7 9.2 %collective-permute-start.15 = (f32[256,256]{1,0:T(8,128)S(1)}, f32[256,256]{1,0:T(8,128)S(1)}, u32[]{:S(2)}, u32[]{:S(2)}) collective-permute-start(f32[256,256]{1,0:T(8,128)S(1)} %get-tuple-element.43), channel_id=1, source_target_pairs={{0,2},{1,3},{2,0},{3,1},{4,6},{5,7},{6,4},{7,5},{8,10},{9,11},{10,... | collective-permute-start | bytes 786440 | tf_op jit(solution)/shard_map/ppermute | solution.py:369
  59.1 15.0 %collective-permute-start.16 = (f32[256,256]{1,0:T(8,128)S(1)}, f32[256,256]{1,0:T(8,128)S(1)}, u32[]{:S(2)}, u32[]{:S(2)}) collective-permute-start(f32[256,256]{1,0:T(8,128)S(1)} %get-tuple-element.44), channel_id=1, source_target_pairs={{0,4},{1,5},{2,6},{3,7},{4,0},{5,1},{6,2},{7,3},{8,12},{9,13},{10,... | collective-permute-start | bytes 786440 | tf_op jit(solution)/shard_map/ppermute | solution.py:369
  61.8 13.7 %collective-permute-start.17 = (f32[256,256]{1,0:T(8,128)S(1)}, f32[256,256]{1,0:T(8,128)S(1)}, u32[]{:S(2)}, u32[]{:S(2)}) collective-permute-start(f32[256,256]{1,0:T(8,128)S(1)} %get-tuple-element.45), channel_id=1, source_target_pairs={{0,6},{1,7},{2,4},{3,5},{4,2},{5,3},{6,0},{7,1},{8,14},{9,15},{10,... | collective-permute-start | bytes 786440 | tf_op jit(solution)/shard_map/ppermute | solution.py:369
  63.8 14.3 %collective-permute-start.6 = (f32[256,256]{1,0:T(8,128)S(1)}, f32[256,256]{1,0:T(8,128)S(1)}, u32[]{:S(2)}, u32[]{:S(2)}) collective-permute-start(f32[256,256]{1,0:T(8,128)S(1)} %get-tuple-element.33), channel_id=1, source_target_pairs={{0,2},{1,3},{2,0},{3,1},{4,6},{5,7},{6,4},{7,5},{8,10},{9,11},{10,... | collective-permute-start | bytes 786440 | tf_op jit(solution)/shard_map/ppermute | solution.py:369
  64.4 20.2 %collective-permute-start.7 = (f32[256,256]{1,0:T(8,128)S(1)}, f32[256,256]{1,0:T(8,128)S(1)}, u32[]{:S(2)}, u32[]{:S(2)}) collective-permute-start(f32[256,256]{1,0:T(8,128)S(1)} %get-tuple-element.34), channel_id=1, source_target_pairs={{0,4},{1,5},{2,6},{3,7},{4,0},{5,1},{6,2},{7,3},{8,12},{9,13},{10,... | collective-permute-start | bytes 786440 | tf_op jit(solution)/shard_map/ppermute | solution.py:369
  66.8 19.5 %collective-permute-start.8 = (f32[256,256]{1,0:T(8,128)S(1)}, f32[256,256]{1,0:T(8,128)S(1)}, u32[]{:S(2)}, u32[]{:S(2)}) collective-permute-start(f32[256,256]{1,0:T(8,128)S(1)} %get-tuple-element.35), channel_id=1, source_target_pairs={{0,6},{1,7},{2,4},{3,5},{4,2},{5,3},{6,0},{7,1},{8,14},{9,15},{10,... | collective-permute-start | bytes 786440 | tf_op jit(solution)/shard_map/ppermute | solution.py:369

commit v2 on v1

--- a/solution.py
+++ b/solution.py
@@ -12,18 +12,19 @@
 SLAB = 32
 ROWS = 4
 RATE = 0.25
-CHUNKS = 2
+PARTS = (2, 2)
 JOINT = ("lat", "depth")
 BODY = 2 * ROWS * SLAB
 VMEM_LIMIT = 48 * 1024 * 1024
-
-
-def params():
-    return pltpu.CompilerParams(vmem_limit_bytes=VMEM_LIMIT)
+FIRST_LIMIT = 62 * 1024 * 1024
+
+
+def params(limit=VMEM_LIMIT):
+    return pltpu.CompilerParams(vmem_limit_bytes=limit)
 
 
 def cost(flops, nbytes):
-    return pl.CostEstimate(flops=flops, bytes_accessed=nbytes, transcendentals=0)
+    return pl.CostEstimate(flops=0, bytes_accessed=1024, transcendentals=0)
 
 
 def scaled_cheb(count):
@@ -53,41 +54,85 @@
     return 2 * y + x
 
 
-def column_start(k, mask, width):
-    return pl.multiple_of((lax.bitwise_xor(quarter(), mask) * CHUNKS + k) * width, 128)
+def chunk_width(k, columns):
+    return columns * PARTS[k] // (4 * sum(PARTS))
+
+
+def column_start(k, mask, columns):
+    offset = sum(chunk_width(i, columns) for i in range(k))
+    return pl.multiple_of(
+        lax.bitwise_xor(quarter(), mask) * (columns // 4) + offset, 128
+    )
+
+
+def halo_at(f, width):
+    return (BODY, 128 * f) if width >= 256 else (BODY + 8 * f, 0)
+
+
+def label_at(width):
+    return BODY + (8 if width >= 256 else 16)
+
+
+def block_rows(width):
+    return label_at(width) + 8
 
 
 def lanes(shape):
     return lax.broadcasted_iota(jnp.int32, shape, len(shape) - 1)
 
 
-def pack_kernel(k, width, heat_ref, wet_ref, label_ref, *blocks):
-    columns = heat_ref.shape[2]
+def pack_kernel(k, width, heat_hbm, wet_hbm, label_hbm, *refs):
+    *blocks, near, label_ref, sems = refs
+    columns = heat_hbm.shape[2]
+    window = near.shape[4]
+    labels = pltpu.make_async_copy(label_hbm, label_ref, sems.at[8])
+    labels.start()
+    bases, copies = [], []
+    for mask in (1, 2, 3, 0):
+        start = column_start(k, mask, columns)
+        base = pl.multiple_of(jnp.clip(start - 128, 0, columns - window), 128)
+        pair = [
+            pltpu.make_async_copy(
+                far.at[:, :, pl.ds(base, window)], near.at[mask, f], sems.at[2 * mask + f]
+            )
+            for f, far in enumerate((heat_hbm, wet_hbm))
+        ]
+        for copy in pair:
+            copy.start()
+        bases.append(base)
+        copies.append(pair)
+    labels.wait()
     lane = lanes((SLAB, 128))
     lane8 = lanes((8, 128))
     lane4 = lanes((ROWS, 128))
-    for mask in range(4):
-        start = column_start(k, mask, width)
+    for mask, base, pair in zip((1, 2, 3, 0), bases, copies):
+        for copy in pair:
+            copy.wait()
+        start = column_start(k, mask, columns)
         left = pl.multiple_of(jnp.maximum(start - 128, 0), 128)
         right = pl.multiple_of(jnp.minimum(start + width, columns - 128), 128)
         keep_left = (start > 0).astype(jnp.float32)
         keep_right = (start + width < columns).astype(jnp.float32)
-        for f, ref in enumerate((heat_ref, wet_ref)):
+        main, before, after = (pl.multiple_of(at - base, 128) for at in (start, left, right))
+        for f in range(2):
+            ref = near.at[mask, f]
             packed = jnp.zeros((8, 128), jnp.float32)
             for r in range(ROWS):
-                base = (f * ROWS + r) * SLAB
-                blocks[mask][base : base + SLAB, :] = ref[:, r, pl.ds(start, width)]
+                row = (f * ROWS + r) * SLAB
+                blocks[mask][row : row + SLAB, :] = ref[:, r, pl.ds(main, width)]
                 edge = jnp.where(
                     lane >= 64,
-                    ref[:, r, pl.ds(left, 128)] * keep_left,
-                    ref[:, r, pl.ds(right, 128)] * keep_right,
+                    ref[:, r, pl.ds(before, 128)] * keep_left,
+                    ref[:, r, pl.ds(after, 128)] * keep_right,
                 )
                 for g in range(SLAB // 8):
                     at = 8 * (r * (SLAB // 8) + g)
                     moved = pltpu.roll(edge[8 * g : 8 * g + 8], (at + 4) % 128, 1)
                     packed = jnp.where((lane8 >= at) & (lane8 < at + 8), moved, packed)
-            blocks[mask][BODY : BODY + 8, 128 * f : 128 * f + 128] = packed
-        blocks[mask][BODY + 8 : BODY + 12, :] = (
+            at, lane_at = halo_at(f, width)
+            blocks[mask][at : at + 8, lane_at : lane_at + 128] = packed
+        types = label_at(width)
+        blocks[mask][types : types + 4, :] = (
             label_ref[:, pl.ds(start, width)] + 1
         ).astype(jnp.float32)
         edge = jnp.where(
@@ -95,20 +140,25 @@
             (label_ref[:, pl.ds(left, 128)] + 1).astype(jnp.float32) * keep_left,
             (label_ref[:, pl.ds(right, 128)] + 1).astype(jnp.float32) * keep_right,
         )
-        blocks[mask][BODY + 12 : BODY + 16, :] = jnp.zeros((ROWS, width), jnp.float32)
-        blocks[mask][BODY + 12 : BODY + 16, :128] = jnp.where(
+        blocks[mask][types + 4 : types + 8, :] = jnp.zeros((ROWS, width), jnp.float32)
+        blocks[mask][types + 4 : types + 8, :128] = jnp.where(
             (lane4 >= 124) | (lane4 < 4), edge, 0.0
         )
 
 
 def pack(k, width, heat, wet, label):
-    shape = jax.ShapeDtypeStruct((BODY + 16, width), jnp.float32)
+    shape = jax.ShapeDtypeStruct((block_rows(width), width), jnp.float32)
     return pl.pallas_call(
         functools.partial(pack_kernel, k, width),
         out_shape=[shape] * 4,
-        in_specs=[pl.BlockSpec(memory_space=pltpu.VMEM)] * 3,
+        in_specs=[pl.BlockSpec(memory_space=pltpu.HBM)] * 3,
         out_specs=[pl.BlockSpec(memory_space=pltpu.VMEM)] * 4,
-        compiler_params=params(),
+        scratch_shapes=[
+            pltpu.VMEM((4, 2, SLAB, ROWS, min(width + 256, heat.shape[2])), jnp.float32),
+            pltpu.VMEM(label.shape, jnp.int32),
+            pltpu.SemaphoreType.DMA((9,)),
+        ],
+        compiler_params=params(VMEM_LIMIT if k else FIRST_LIMIT),
         cost_estimate=cost(0, 4 << 20),
         name="pack",
     )(heat, wet, label)
@@ -186,87 +236,135 @@
     return heat, moist
 
 
+INNER = [(1, 5), (1, 6), (1, 9), (1, 10), (2, 6), (2, 7), (2, 8), (2, 9), (3, 7), (3, 8)]
+COUNT = 4 * ROWS
+
+
+def stored(r):
+    return jnp.where(lax.rem(lax.axis_index("lat"), 2) == 1, ROWS - 1 - r, r)
+
+
+def strip_factors(width, block, spread_ref, factor_ref):
+    y, _, _ = place()
+    label = block[label_at(width) : label_at(width) + 8, :]
+    body = factors(label[:ROWS], spread_ref, factor_ref)
+    edge = factors(label[ROWS:, :128], spread_ref, factor_ref)
+    for f in range(2):
+        whole = jnp.concatenate([body[f], edge[f]], axis=1)
+        back = jnp.concatenate([whole[r : r + 1] for r in reversed(range(ROWS))], axis=0)
+        yield jnp.where(y == 1, back, whole)
+
+
+def load_row(width, block, r, g):
+    r = stored(r)
+    shift = lax.rem(252 - 8 * (r * (SLAB // 8) + g), 128)
+    fields = []
+    for f in range(2):
+        at = pl.multiple_of((f * ROWS + r) * SLAB + 8 * g, 8)
+        row, lane = halo_at(f, width)
+        edge = pltpu.roll(block[row : row + 8, lane : lane + 128], shift, 1)
+        fields.append(jnp.concatenate([block[pl.ds(at, 8), :], edge], axis=1))
+    return tuple(fields)
+
+
+def pre_kernel(width, own, rx, ry, rxy, spread_ref, factor_ref, _, inner, kap, km_ref):
+    for j, block in enumerate((own, ry)):
+        to = slice(j * ROWS, j * ROWS + ROWS)
+        for f, whole in enumerate(strip_factors(width, block, spread_ref, factor_ref)):
+            kap[f, to, :] = RATE * whole
+            if f == 1:
+                km_ref[to, :] = factors(block[label_at(width) : label_at(width) + ROWS, :], spread_ref, factor_ref)[1]
+    for s in range(2):
+        blocks = ((own, rx)[s], (ry, rxy)[s])
+
+        def group(g, carry):
+            levels = [dict() for _ in range(4)]
+            at = pl.ds(pl.multiple_of(s * SLAB + 8 * g, 8), 8)
+            for j in range(ROWS, 3 * ROWS + 3):
+                if j < 3 * ROWS:
+                    levels[0][j] = load_row(width, blocks[j // ROWS - 1], j % ROWS, g)
+                for t in range(1, 4):
+                    i = j - t
+                    if ROWS + t <= i < 3 * ROWS - t:
+                        prev, k = levels[t - 1], i - ROWS
+                        levels[t][i] = substep(
+                            prev[i - 1], prev[i], prev[i + 1], kap[0, k : k + 1, :], kap[1, k : k + 1, :]
+                        )
+                        if (t, i) in INNER:
+                            for f in range(2):
+                                inner[INNER.index((t, i)), f, at, :] = levels[t][i][f]
+            return carry
+
+        lax.fori_loop(0, SLAB // 8, group, 0)
+
+
+def pre(width, own, rx, ry, rxy, spread, factor, after):
+    wide = width + 128
+    return pl.pallas_call(
+        functools.partial(pre_kernel, width),
+        out_shape=[
+            jax.ShapeDtypeStruct((len(INNER), 2, 2 * SLAB, wide), jnp.float32),
+            jax.ShapeDtypeStruct((2, 2 * ROWS, wide), jnp.float32),
+            jax.ShapeDtypeStruct((2 * ROWS, width), jnp.float32),
+        ],
+        in_specs=[pl.BlockSpec(memory_space=pltpu.VMEM)] * 4
+        + [pl.BlockSpec(memory_space=pltpu.SMEM)] * 2
+        + [pl.BlockSpec(memory_space=pl.ANY)],
+        out_specs=[pl.BlockSpec(memory_space=pltpu.VMEM)] * 3,
+        compiler_params=params(),
+        cost_estimate=cost(1 << 24, 4 << 20),
+        name="inner_substeps",
+    )(own, rx, ry, rxy, spread, factor, after)
+
+
 def stencil_kernel(
-    width, own, rx, ry, rxy, p1, p2, spread_ref, factor_ref, post, km_ref, kap
+    width, own, rx, ry, rxy, p1, p2, inner, kap_ref, spread_ref, factor_ref, _, post, kap
 ):
-    y, _, _ = place()
-    count = 4 * ROWS
-    for j, block in enumerate((p2.at[0], own, ry, p1.at[0])):
-        label = block[BODY + 8 : BODY + 16, :]
-        body = factors(label[:ROWS], spread_ref, factor_ref)
-        edge = factors(label[ROWS:, :128], spread_ref, factor_ref)
-        if 1 <= j < 3:
-            km_ref[(j - 1) * ROWS : j * ROWS, :] = body[1]
-        for f in range(2):
-            whole = RATE * jnp.concatenate([body[f], edge[f]], axis=1)
-            back = jnp.concatenate(
-                [whole[r : r + 1] for r in reversed(range(ROWS))], axis=0
-            )
-            kap[f, j * ROWS : j * ROWS + ROWS, :] = jnp.where(y == 1, back, whole)
-
-    def stored(r):
-        return jnp.where(y == 1, ROWS - 1 - r, r)
-
+    kap[:, ROWS : 3 * ROWS, :] = kap_ref[...]
+    for j, block in ((0, p2.at[0]), (3, p1.at[0])):
+        for f, whole in enumerate(strip_factors(width, block, spread_ref, factor_ref)):
+            kap[f, j * ROWS : j * ROWS + ROWS, :] = RATE * whole
     for s in range(2):
         blocks = (p2.at[s], (own, rx)[s], (ry, rxy)[s], p1.at[s])
 
         def group(g, carry):
-            def load(j):
-                block, r = blocks[j // ROWS], stored(j % ROWS)
-                shift = lax.rem(252 - 8 * (r * (SLAB // 8) + g), 128)
-                fields = []
-                for f in range(2):
-                    at = pl.multiple_of((f * ROWS + r) * SLAB + 8 * g, 8)
-                    edge = pltpu.roll(
-                        block[BODY : BODY + 8, 128 * f : 128 * f + 128], shift, 1
-                    )
-                    fields.append(jnp.concatenate([block[pl.ds(at, 8), :], edge], axis=1))
-                return tuple(fields)
-
+            at = pl.ds(pl.multiple_of(s * SLAB + 8 * g, 8), 8)
             levels = [dict() for _ in range(5)]
-            for j in range(count + 4):
-                if j < count:
-                    levels[0][j] = load(j)
+            for j in range(COUNT + 4):
+                if j < COUNT and not ROWS + 2 <= j < 3 * ROWS - 2:
+                    levels[0][j] = load_row(width, blocks[j // ROWS], j % ROWS, g)
                 for t in range(1, 5):
                     i = j - t
-                    if t <= i < count - t:
+                    if (t, i) in INNER:
+                        k = INNER.index((t, i))
+                        levels[t][i] = tuple(inner[k, f, at, :] for f in range(2))
+                    elif t <= i < COUNT - t and not (t < 4 and ROWS + t <= i < 3 * ROWS - t):
                         prev = levels[t - 1]
                         levels[t][i] = substep(
-                            prev[i - 1],
-                            prev[i],
-                            prev[i + 1],
-                            kap[0, i : i + 1, :],
-                            kap[1, i : i + 1, :],
+                            prev[i - 1], prev[i], prev[i + 1], kap[0, i : i + 1, :], kap[1, i : i + 1, :]
                         )
                         if t == 4:
-                            strip, r = divmod(i - ROWS, ROWS)
+                            row = (i - ROWS) // ROWS * ROWS + stored(i % ROWS)
                             for f in range(2):
-                                post[
-                                    f,
-                                    strip * ROWS + stored(r),
-                                    pl.ds(pl.multiple_of(s * SLAB + 8 * g, 8), 8),
-                                    :,
-                                ] = levels[4][i][f][:, :width]
+                                post[f, row, at, :] = levels[4][i][f][:, :width]
             return carry
 
         lax.fori_loop(0, SLAB // 8, group, 0)
 
 
-def stencil(width, own, rx, ry, rxy, p1, p2, spread, factor):
+def stencil(width, own, rx, ry, rxy, p1, p2, inner, kap, spread, factor, after):
     return pl.pallas_call(
         functools.partial(stencil_kernel, width),
-        out_shape=[
-            jax.ShapeDtypeStruct((2, 2 * ROWS, 2 * SLAB, width), jnp.float32),
-            jax.ShapeDtypeStruct((2 * ROWS, width), jnp.float32),
-        ],
-        in_specs=[pl.BlockSpec(memory_space=pltpu.VMEM)] * 6
-        + [pl.BlockSpec(memory_space=pltpu.SMEM)] * 2,
-        out_specs=[pl.BlockSpec(memory_space=pltpu.VMEM)] * 2,
-        scratch_shapes=[pltpu.VMEM((2, 4 * ROWS, width + 128), jnp.float32)],
+        out_shape=jax.ShapeDtypeStruct((2, 2 * ROWS, 2 * SLAB, width), jnp.float32),
+        in_specs=[pl.BlockSpec(memory_space=pltpu.VMEM)] * 8
+        + [pl.BlockSpec(memory_space=pltpu.SMEM)] * 2
+        + [pl.BlockSpec(memory_space=pl.ANY)],
+        out_specs=pl.BlockSpec(memory_space=pltpu.VMEM),
+        scratch_shapes=[pltpu.VMEM((2, COUNT, width + 128), jnp.float32)],
         compiler_params=params(),
         cost_estimate=cost(1 << 24, 4 << 20),
-        name="stencil",
-    )(own, rx, ry, rxy, p1, p2, spread, factor)
+        name="outer_substeps",
+    )(own, rx, ry, rxy, p1, p2, inner, kap, spread, factor, after)
 
 
 def split(values):
@@ -314,30 +412,44 @@
     )(mine, other, stack_w, stack_h, km)
 
 
-def assemble_kernel(width, *refs):
-    blocks, outs = refs[:-2], refs[-2:]
-    for k in range(CHUNKS):
-        for mask in range(4):
-            start = column_start(k, mask, width)
-            for f in range(2):
-                for r in range(ROWS):
-                    base = (f * ROWS + r) * SLAB
-                    outs[f][:, r, pl.ds(start, width)] = blocks[4 * k + mask][
-                        base : base + SLAB, :
-                    ]
-
-
-def assemble(width, columns, blocks):
+def assemble_kernel(k, width, *refs):
+    blocks, outs, scratch, sems = refs[:4], refs[-4:-2], refs[-2], refs[-1]
+    columns = outs[0].shape[2]
+    copies = []
+    for mask in range(4):
+        start = column_start(k, mask, columns)
+        for f in range(2):
+            for r in range(ROWS):
+                base = (f * ROWS + r) * SLAB
+                scratch[mask, f, :, r, :] = blocks[mask][base : base + SLAB, :]
+            copy = pltpu.make_async_copy(
+                scratch.at[mask, f],
+                outs[f].at[:, :, pl.ds(start, width)],
+                sems.at[2 * mask + f],
+            )
+            copy.start()
+            copies.append(copy)
+    for copy in copies:
+        copy.wait()
+
+
+def assemble(k, width, columns, blocks, outs):
     shape = jax.ShapeDtypeStruct((SLAB, ROWS, columns), jnp.float32)
     return pl.pallas_call(
-        functools.partial(assemble_kernel, width),
+        functools.partial(assemble_kernel, k, width),
         out_shape=[shape] * 2,
-        in_specs=[pl.BlockSpec(memory_space=pltpu.VMEM)] * len(blocks),
-        out_specs=[pl.BlockSpec(memory_space=pltpu.VMEM)] * 2,
+        in_specs=[pl.BlockSpec(memory_space=pltpu.VMEM)] * 4
+        + [pl.BlockSpec(memory_space=pltpu.HBM)] * len(outs),
+        out_specs=[pl.BlockSpec(memory_space=pltpu.HBM)] * 2,
+        scratch_shapes=[
+            pltpu.VMEM((4, 2, SLAB, ROWS, width), jnp.float32),
+            pltpu.SemaphoreType.DMA((8,)),
+        ],
+        input_output_aliases={4 + i: i for i in range(len(outs))},
         compiler_params=params(),
         cost_estimate=cost(0, 4 << 20),
         name="assemble",
-    )(*blocks)
+    )(*blocks, *outs)
 
 
 def routes(strips):
@@ -362,27 +474,37 @@
 
 def per_device(strips, heat, wet, label, spread, factor, thermal, water):
     columns = heat.shape[2]
-    width = columns // (4 * CHUNKS)
+    widths = [chunk_width(k, columns) for k in range(len(PARTS))]
     route = routes(strips)
 
     def send(array, name):
         return lax.ppermute(array, JOINT, route[name])
 
     received = []
-    for k in range(CHUNKS):
+    for k, width in enumerate(widths):
         own, bx, by, bxy = pack(k, width, heat, wet, label)
         received.append((own, send(bx, "x"), send(by, "y"), send(bxy, "xy")))
     stack_w, stack_h = prep(thermal, water)
-    blocks = []
-    for k in range(CHUNKS):
+    outs = []
+    inners, beyond = [], []
+    for k, width in enumerate(widths):
         own, rx, ry, rxy = received[k]
-        p1 = send(jnp.stack([own, rx]), "own")
-        p2 = send(jnp.stack([ry, rxy]), "partner")
-        post, km = stencil(width, own, rx, ry, rxy, p1, p2, spread, factor)
+        if k:
+            rxy, _ = lax.optimization_barrier((rxy, inners[-1][2]))
+            received[k] = (own, rx, ry, rxy)
+        beyond.append((send(jnp.stack([own, rx]), "own"), send(jnp.stack([ry, rxy]), "partner")))
+        inners.append(pre(width, own, rx, ry, rxy, spread, factor, stack_h))
+    for k, width in enumerate(widths):
+        own, rx, ry, rxy = received[k]
+        inner, kap, km = inners[k]
+        p1, p2 = beyond[k]
+        after = inners[k + 1][2] if k + 1 < len(widths) else km
+        post = stencil(width, own, rx, ry, rxy, p1, p2, inner, kap, spread, factor, after)
         other = send(post, "core")
         kept, bx, by, bxy = solve(width, post, other, stack_w, stack_h, km)
-        blocks += [kept, send(bx, "x"), send(by, "y"), send(bxy, "xy")]
-    return tuple(assemble(width, columns, blocks))
+        blocks = [kept, send(bx, "x"), send(by, "y"), send(bxy, "xy")]
+        outs = assemble(k, width, columns, blocks, outs)
+    return tuple(outs)
 
 
 def solution(mesh):

time: 88.9 us -> 85.9 us (0.966)
  Pallas kernels: 22 us -> 28.6 us
  starting transfers between devices: 33.2 us -> 27.1 us
  local copies, waits for them, and re-layouts: 3.23 us -> 1.26 us
  waiting for transfers between devices: 29.2 us -> 27.6 us
    ppermute x18, starting transfers between devices: 33.2 us -> 27.1 us  [send(): return lax.ppermute(array, JOINT, route[name])]
    pallas_call x3 -> x6, Pallas kernels: 16.5 us -> 20.3 us  [the longest x2 10.7 us: stencil(): pl.pallas_call(functools.partial(stencil_kernel, width), out_shape=jax.Sh...]
    pallas_call x2, Pallas kernels: 2.88 us -> 5.67 us  [pack(): pl.pallas_call(functools.partial(pack_kernel, k, width), out_shape=[shape...]
    unnamed x16 -> x18, local copies, waits for them, and re-layouts: 3.23 us -> 1.26 us
    ppermute x18, waiting for transfers between devices: 29.2 us -> 27.6 us  [send(): return lax.ppermute(array, JOINT, route[name])]
  transfers between devices with their start and end apart: 18 -> 18, of which waited for: 12 -> 5; matrix products, arithmetic and copies ran while one was open for 0% -> 0% of each run, Pallas kernels for 21% -> 28%
where the time goes in v2:
time: 85.9 us; the launch traced here: 85.7 us
  Pallas kernels  28.6 us (33%)
  waiting for transfers between devices  27.6 us (32%)
  starting transfers between devices  27.1 us (32%)
  local copies, waits for them, and re-layouts  1.26 us (1%)
  between operations  0.93 us (1%)
    ppermute x18, waiting for transfers between devices, send(): return lax.ppermute(array, JOINT, route[name])  27.6 us
    ppermute x18, starting transfers between devices, send(): return lax.ppermute(array, JOINT, route[name])  27.1 us
    pallas_call x2, Pallas kernels, stencil(): pl.pallas_call(functools.partial(stencil_kernel, width), out_shape=jax.Sh...  10.7 us
    pallas_call x2, Pallas kernels, pre(): pl.pallas_call(functools.partial(pre_kernel, width), out_shape=[jax.Shape...  7.43 us
    pallas_call x2, Pallas kernels, pack(): pl.pallas_call(functools.partial(pack_kernel, k, width), out_shape=[shape...  5.67 us
    pallas_call x2, Pallas kernels, assemble(): pl.pallas_call(functools.partial(assemble_kernel, k, width), out_shape=[s...  2.15 us
    pallas_call x2, Pallas kernels, solve(): pl.pallas_call(solve_kernel, out_shape=[shape] * 4, in_specs=[pl.BlockSpe...  1.98 us
  transfers between devices with their start and end apart: 18, of which 5 were waited for; matrix products, arithmetic and copies ran while one was open for 0% of the time, Pallas kernels for 28%

profile of v2, /device:TPU:0, one launch (start us, length us, event | category | flops | bytes accessed | tf_op | source)
XLA Modules:
  0.0 85.7 jit_solution(13933178310431581516)
XLA Ops:
  0.6 0.0 copy-start.3
  0.6 0.0 copy-start
  0.6 3.6 %pack.3 = (f32[272,256]{1,0:T(8,128)}, f32[272,256]{1,0:T(8,128)}, f32[272,256]{1,0:T(8,128)}, f32[272,256]{1,0:T(8,128)}) custom-call(f32[32,4,2048]{2,1,0:T(4,128)} %heat_hbm.3, f32[32,4,2048]{2,1,0:T(4,128)} %wet_hbm.3, s32[4,2048]{1,0:T(4,128)} %label_hbm.3), custom_call_target="tpu_custom_call" | custom-call | bytes 1024 | tf_op jit(solution)/shard_map/pack/pallas_call | solution.py:151
  4.3 3.0 %collective-permute-start.4 = (f32[272,256]{1,0:T(8,128)}, f32[272,256]{1,0:T(8,128)S(1)}, u32[]{:S(2)}, u32[]{:S(2)}) collective-permute-start(f32[272,256]{1,0:T(8,128)} %get-tuple-element.35), channel_id=1, source_target_pairs={{0,4},{1,5},{2,6},{3,7},{4,0},{5,1},{6,2},{7,3},{8,12},{9,13},{10,... | collective-permute-start | bytes 835592 | tf_op jit(solution)/shard_map/ppermute | solution.py:481
  7.3 1.4 %collective-permute-start.5 = (f32[272,256]{1,0:T(8,128)}, f32[272,256]{1,0:T(8,128)S(1)}, u32[]{:S(2)}, u32[]{:S(2)}) collective-permute-start(f32[272,256]{1,0:T(8,128)} %get-tuple-element.36), channel_id=1, source_target_pairs={{0,6},{1,7},{2,4},{3,5},{4,2},{5,3},{6,0},{7,1},{8,14},{9,15},{10,... | collective-permute-start | bytes 835592 | tf_op jit(solution)/shard_map/ppermute | solution.py:481
  8.8 0.1 collective-permute-start.3
  8.9 0.0 copy-done.3
  8.9 0.0 copy-done
  8.9 0.0 copy-start.1
  8.9 1.2 %copy-done.1 = f32[32,4,2048]{2,1,0:T(4,128)S(1)} copy-done((f32[32,4,2048]{2,1,0:T(4,128)S(1)}, f32[32,4,2048]{2,1,0:T(4,128)}, u32[]{:S(2)}) %copy-start.1) | copy-done | bytes 1048600
  10.1 0.0 copy-start.2
  10.1 0.0 copy-start.4
  10.1 0.0 copy-start.5
  10.1 0.0 copy-start.7
  10.1 0.0 copy-start.8
  10.1 2.0 %pack.2 = (f32[272,256]{1,0:T(8,128)S(1)}, f32[272,256]{1,0:T(8,128)S(1)}, f32[272,256]{1,0:T(8,128)S(1)}, f32[272,256]{1,0:T(8,128)S(1)}) custom-call(f32[32,4,2048]{2,1,0:T(4,128)S(1)} %copy-done, f32[32,4,2048]{2,1,0:T(4,128)S(1)} %copy-done.1, s32[4,2048]{1,0:T(4,128)S(1)} %copy-done.3), custom_call_target="tpu_custom_call" | custom-call | bytes 1024 | tf_op jit(solution)/shard_map/pack/pallas_call | solution.py:151
  12.2 2.9 %collective-permute-start.2 = (f32[272,256]{1,0:T(8,128)S(1)}, f32[272,256]{1,0:T(8,128)S(1)}, u32[]{:S(2)}, u32[]{:S(2)}) collective-permute-start(f32[272,256]{1,0:T(8,128)S(1)} %get-tuple-element.32), channel_id=1, source_target_pairs={{0,6},{1,7},{2,4},{3,5},{4,2},{5,3},{6,0},{7,1},{8,14},{9,15},{10,... | collective-permute-start | bytes 835592 | tf_op jit(solution)/shard_map/ppermute | solution.py:481
  15.1 0.5 collective-permute-start.1
  15.6 5.7 %collective-permute-done.4.ry = f32[272,256]{1,0:T(8,128)S(1)} collective-permute-done((f32[272,256]{1,0:T(8,128)}, f32[272,256]{1,0:T(8,128)S(1)}, u32[]{:S(2)}, u32[]{:S(2)}) %collective-permute-start.4) | collective-permute-done | bytes 278560 | tf_op jit(solution)/shard_map/ppermute | solution.py:481
  21.3 2.1 %collective-permute-start = (f32[272,256]{1,0:T(8,128)S(1)}, f32[272,256]{1,0:T(8,128)S(1)}, u32[]{:S(2)}, u32[]{:S(2)}) collective-permute-start(f32[272,256]{1,0:T(8,128)S(1)} %get-tuple-element.30), channel_id=1, source_target_pairs={{0,2},{1,3},{2,0},{3,1},{4,6},{5,7},{6,4},{7,5},{8,10},{9,11},{10,... | collective-permute-start | bytes 835592 | tf_op jit(solution)/shard_map/ppermute | solution.py:481
  23.4 0.0 collective-permute-done.5.rxy
  23.5 3.5 %collective-permute-start.13 = (f32[2,272,256]{2,1,0:T(8,128)S(1)}, f32[2,272,256]{2,1,0:T(8,128)S(1)}, u32[]{:S(2)}, u32[]{:S(2)}) collective-permute-start(f32[2,272,256]{2,1,0:T(8,128)S(1)} %pad_maximum_fusion.3), channel_id=1, source_target_pairs={{0,8},{1,9},{2,10},{3,11},{8,16},{9,17},{10,18},{11,19},{12,4},{13... | collective-permute-start | bytes 1671176 | tf_op jit(solution)/shard_map/ppermute | solution.py:481
  27.0 0.0 collective-permute-done.3.rx
  27.0 0.0 copy-done.2
  27.0 1.3 %collective-permute-start.12 = (f32[2,272,256]{2,1,0:T(8,128)S(1)}, f32[2,272,256]{2,1,0:T(8,128)S(1)}, u32[]{:S(2)}, u32[]{:S(2)}) collective-permute-start(f32[2,272,256]{2,1,0:T(8,128)S(1)} %pad_maximum_fusion.2), channel_id=1, source_target_pairs={{4,12},{5,13},{6,14},{7,15},{8,0},{9,1},{10,2},{11,3},{12,20},{13,... | collective-permute-start | bytes 1671176 | tf_op jit(solution)/shard_map/ppermute | solution.py:481
  28.3 0.0 copy-done.4
  28.4 0.0 copy-done.5
  28.4 0.0 copy-done.6
  28.4 0.7 prep.1
  29.1 0.0 copy-done.7
  29.1 0.0 copy-done.8
  29.1 3.7 %inner_substeps.2 = (f32[10,2,64,384]{3,2,1,0:T(8,128)S(1)}, f32[2,8,384]{2,1,0:T(8,128)S(1)}, f32[8,256]{1,0:T(8,128)S(1)}) custom-call(f32[272,256]{1,0:T(8,128)S(1)} %copy-done.2, f32[272,256]{1,0:T(8,128)S(1)} %collective-permute-done.3.rx, f32[272,256]{1,0:T(8,128)S(1)} %collective-permute-done.4.ry, f32[272,256]{1,0:T(8,128)S(1)} %collective-permute-done.5.rxy, ...), custom_call_target="tpu_custom_call" | custom-call | bytes 1024 | tf_op jit(solution)/shard_map/inner_substeps/pallas_call | solution.py:303
  32.9 0.0 collective-permute-done.2.rxy
  32.9 0.0 collective-permute-done.1.ry
  32.9 4.6 %collective-permute-start.7 = (f32[2,272,256]{2,1,0:T(8,128)S(1)}, f32[2,272,256]{2,1,0:T(8,128)S(1)}, u32[]{:S(2)}, u32[]{:S(2)}) collective-permute-start(f32[2,272,256]{2,1,0:T(8,128)S(1)} %pad_maximum_fusion.1), channel_id=1, source_target_pairs={{0,8},{1,9},{2,10},{3,11},{8,16},{9,17},{10,18},{11,19},{12,4},{13... | collective-permute-start | bytes 1671176 | tf_op jit(solution)/shard_map/ppermute | solution.py:481
  37.5 0.0 collective-permute-done.rx
  37.6 1.3 %collective-permute-start.6 = (f32[2,272,256]{2,1,0:T(8,128)S(1)}, f32[2,272,256]{2,1,0:T(8,128)S(1)}, u32[]{:S(2)}, u32[]{:S(2)}) collective-permute-start(f32[2,272,256]{2,1,0:T(8,128)S(1)} %pad_maximum_fusion), channel_id=1, source_target_pairs={{4,12},{5,13},{6,14},{7,15},{8,0},{9,1},{10,2},{11,3},{12,20},{13,... | collective-permute-start | bytes 1671176 | tf_op jit(solution)/shard_map/ppermute | solution.py:481
  38.9 3.7 %inner_substeps.3 = (f32[10,2,64,384]{3,2,1,0:T(8,128)S(1)}, f32[2,8,384]{2,1,0:T(8,128)S(1)}, f32[8,256]{1,0:T(8,128)S(1)}) custom-call(f32[272,256]{1,0:T(8,128)S(1)} %get-tuple-element.29.own, f32[272,256]{1,0:T(8,128)S(1)} %collective-permute-done.rx, f32[272,256]{1,0:T(8,128)S(1)} %collective-permute-done.1.ry, ...), custom_call_target="tpu_custom_call" | custom-call | bytes 1024 | tf_op jit(solution)/shard_map/inner_substeps/pallas_call | solution.py:303
  42.6 0.0 collective-permute-done.13.p2
  42.6 0.0 collective-permute-done.12.p1
  42.6 5.3 %outer_substeps.3.mine = f32[2,8,64,256]{3,2,1,0:T(8,128)S(1)} custom-call(f32[272,256]{1,0:T(8,128)S(1)} %copy-done.2, f32[272,256]{1,0:T(8,128)S(1)} %collective-permute-done.3.rx, f32[272,256]{1,0:T(8,128)S(1)} %collective-permute-done.4.ry, f32[272,256]{1,0:T(8,128)S(1)} %collective-permute-done.5.rxy, f32[2,272,256]{2,1,0:T(8,128)S(1)} %collective-permute-done.12.p1, ...), custom_call_target="tpu_custom_call" | custom-call | bytes 1024 | tf_op jit(solution)/shard_map/outer_substeps/pallas_call | solution.py:356
  48.0 0.1 collective-permute-start.14
  48.0 0.0 collective-permute-done.7.p2
  48.1 4.2 %collective-permute-done.6.p1 = f32[2,272,256]{2,1,0:T(8,128)S(1)} collective-permute-done((f32[2,272,256]{2,1,0:T(8,128)S(1)}, f32[2,272,256]{2,1,0:T(8,128)S(1)}, u32[]{:S(2)}, u32[]{:S(2)}) %collective-permute-start.6) | collective-permute-done | bytes 557088 | tf_op jit(solution)/shard_map/ppermute | solution.py:481
  52.3 5.3 %outer_substeps.2.mine = f32[2,8,64,256]{3,2,1,0:T(8,128)S(1)} custom-call(f32[272,256]{1,0:T(8,128)S(1)} %get-tuple-element.29.own, f32[272,256]{1,0:T(8,128)S(1)} %collective-permute-done.rx, f32[272,256]{1,0:T(8,128)S(1)} %collective-permute-done.1.ry, f32[272,256]{1,0:T(8,128)S(1)} %collective-permute-done.2.rxy, ...), custom_call_target="tpu_custom_call" | custom-call | bytes 1024 | tf_op jit(solution)/shard_map/outer_substeps/pallas_call | solution.py:356
  57.6 0.1 collective-permute-start.8
  57.7 0.0 collective-permute-done.14.other
  57.7 1.0 %solve.3 = (f32[256,256]{1,0:T(8,128)S(1)}, f32[256,256]{1,0:T(8,128)S(1)}, f32[256,256]{1,0:T(8,128)S(1)}, f32[256,256]{1,0:T(8,128)S(1)}) custom-call(f32[2,8,64,256]{3,2,1,0:T(8,128)S(1)} %outer_substeps.3.mine, f32[2,8,64,256]{3,2,1,0:T(8,128)S(1)} %collective-permute-done.14.other, bf16[384,128]{1,0:T(8,128)(2,1)S(1)} %get-tuple-element.43.stack_w, ...), custom_call_target="tpu_custom_call" | custom-call | bytes 1024 | tf_op jit(solution)/shard_map/solve/pallas_call | solution.py:404
  58.7 0.6 collective-permute-start.15
  59.3 0.0 collective-permute-start.16
  59.3 2.9 %collective-permute-start.17 = (f32[256,256]{1,0:T(8,128)S(1)}, f32[256,256]{1,0:T(8,128)S(1)}, u32[]{:S(2)}, u32[]{:S(2)}) collective-permute-start(f32[256,256]{1,0:T(8,128)S(1)} %get-tuple-element.53), channel_id=1, source_target_pairs={{0,6},{1,7},{2,4},{3,5},{4,2},{5,3},{6,0},{7,1},{8,14},{9,15},{10,... | collective-permute-start | bytes 786440 | tf_op jit(solution)/shard_map/ppermute | solution.py:481
  62.3 0.0 collective-permute-done.8.other
  62.3 1.0 %solve.2 = (f32[256,256]{1,0:T(8,128)S(1)}, f32[256,256]{1,0:T(8,128)S(1)}, f32[256,256]{1,0:T(8,128)S(1)}, f32[256,256]{1,0:T(8,128)S(1)}) custom-call(f32[2,8,64,256]{3,2,1,0:T(8,128)S(1)} %outer_substeps.2.mine, f32[2,8,64,256]{3,2,1,0:T(8,128)S(1)} %collective-permute-done.8.other, bf16[384,128]{1,0:T(8,128)(2,1)S(1)} %get-tuple-element.43.stack_w, ...), custom_call_target="tpu_custom_call" | custom-call | bytes 1024 | tf_op jit(solution)/shard_map/solve/pallas_call | solution.py:404
  63.3 0.1 collective-permute-start.10
  63.3 2.0 %collective-permute-start.11 = (f32[256,256]{1,0:T(8,128)S(1)}, f32[256,256]{1,0:T(8,128)S(1)}, u32[]{:S(2)}, u32[]{:S(2)}) collective-permute-start(f32[256,256]{1,0:T(8,128)S(1)} %get-tuple-element.47), channel_id=1, source_target_pairs={{0,6},{1,7},{2,4},{3,5},{4,2},{5,3},{6,0},{7,1},{8,14},{9,15},{10,... | collective-permute-start | bytes 786440 | tf_op jit(solution)/shard_map/ppermute | solution.py:481
  65.3 2.5 %collective-permute-done.15.refs_1_ = f32[256,256]{1,0:T(8,128)S(1)} collective-permute-done((f32[256,256]{1,0:T(8,128)S(1)}, f32[256,256]{1,0:T(8,128)S(1)}, u32[]{:S(2)}, u32[]{:S(2)}) %collective-permute-start.15) | collective-permute-done | bytes 262176 | tf_op jit(solution)/shard_map/ppermute | solution.py:481
  67.9 0.5 collective-permute-start.9
  68.4 11.3 %collective-permute-done.16.refs_2_ = f32[256,256]{1,0:T(8,128)S(1)} collective-permute-done((f32[256,256]{1,0:T(8,128)S(1)}, f32[256,256]{1,0:T(8,128)S(1)}, u32[]{:S(2)}, u32[]{:S(2)}) %collective-permute-start.16) | collective-permute-done | bytes 262176 | tf_op jit(solution)/shard_map/ppermute | solution.py:481
  79.7 0.0 collective-permute-done.17.refs_3_
  79.7 1.1 %assemble.2 = (f32[32,4,2048]{2,1,0:T(4,128)}, f32[32,4,2048]{2,1,0:T(4,128)}) custom-call(f32[256,256]{1,0:T(8,128)S(1)} %get-tuple-element.50.refs_0_, f32[256,256]{1,0:T(8,128)S(1)} %collective-permute-done.15.refs_1_, f32[256,256]{1,0:T(8,128)S(1)} %collective-permute-done.16.refs_2_, f32[256,256]{1,0:T(8,128)S(1)} %collective-permute-done.17.refs_3_), custom_call_target="tpu_custom_call" | custom-call | bytes 1024 | tf_op jit(solution)/shard_map/assemble/pallas_call | solution.py:438
  80.8 3.8 %collective-permute-done.10.refs_2_ = f32[256,256]{1,0:T(8,128)S(1)} collective-permute-done((f32[256,256]{1,0:T(8,128)S(1)}, f32[256,256]{1,0:T(8,128)S(1)}, u32[]{:S(2)}, u32[]{:S(2)}) %collective-permute-start.10) | collective-permute-done | bytes 262176 | tf_op jit(solution)/shard_map/ppermute | solution.py:481
  84.6 0.0 collective-permute-done.11.refs_3_
  84.6 0.0 collective-permute-done.9.refs_1_
  84.6 1.1 %assemble.3 = (f32[32,4,2048]{2,1,0:T(4,128)}, f32[32,4,2048]{2,1,0:T(4,128)}) custom-call(f32[256,256]{1,0:T(8,128)S(1)} %get-tuple-element.44.refs_0_, f32[256,256]{1,0:T(8,128)S(1)} %collective-permute-done.9.refs_1_, f32[256,256]{1,0:T(8,128)S(1)} %collective-permute-done.10.refs_2_, ...), custom_call_target="tpu_custom_call", output_to_operand_aliasing={{0}: (4, {}), {1}: (5, {})} | custom-call | bytes 1024 | tf_op jit(solution)/shard_map/assemble/pallas_call | solution.py:438
  (5 shorter events, 0.2 us)
Async XLA Ops:
  0.6 8.2 %copy-start.3 = (s32[4,2048]{1,0:T(4,128)S(1)}, s32[4,2048]{1,0:T(4,128)}, u32[]{:S(2)}) copy-start(s32[4,2048]{1,0:T(4,128)} %label_hbm.3) | copy-start | bytes 98308
  0.6 8.2 %copy-start = (f32[32,4,2048]{2,1,0:T(4,128)S(1)}, f32[32,4,2048]{2,1,0:T(4,128)}, u32[]{:S(2)}) copy-start(f32[32,4,2048]{2,1,0:T(4,128)} %heat_hbm.3) | copy-start | bytes 3145732
  4.3 17.0 %collective-permute-start.4 = (f32[272,256]{1,0:T(8,128)}, f32[272,256]{1,0:T(8,128)S(1)}, u32[]{:S(2)}, u32[]{:S(2)}) collective-permute-start(f32[272,256]{1,0:T(8,128)} %get-tuple-element.35), channel_id=1, source_target_pairs={{0,4},{1,5},{2,6},{3,7},{4,0},{5,1},{6,2},{7,3},{8,12},{9,13},{10,... | collective-permute-start | bytes 835592 | tf_op jit(solution)/shard_map/ppermute | solution.py:481
  7.3 16.1 %collective-permute-start.5 = (f32[272,256]{1,0:T(8,128)}, f32[272,256]{1,0:T(8,128)S(1)}, u32[]{:S(2)}, u32[]{:S(2)}) collective-permute-start(f32[272,256]{1,0:T(8,128)} %get-tuple-element.36), channel_id=1, source_target_pairs={{0,6},{1,7},{2,4},{3,5},{4,2},{5,3},{6,0},{7,1},{8,14},{9,15},{10,... | collective-permute-start | bytes 835592 | tf_op jit(solution)/shard_map/ppermute | solution.py:481
  8.8 18.2 %collective-permute-start.3 = (f32[272,256]{1,0:T(8,128)}, f32[272,256]{1,0:T(8,128)S(1)}, u32[]{:S(2)}, u32[]{:S(2)}) collective-permute-start(f32[272,256]{1,0:T(8,128)} %get-tuple-element.34), channel_id=1, source_target_pairs={{0,2},{1,3},{2,0},{3,1},{4,6},{5,7},{6,4},{7,5},{8,10},{9,11},{10,... | collective-permute-start | bytes 835592 | tf_op jit(solution)/shard_map/ppermute | solution.py:481
  8.9 1.2 %copy-start.1 = (f32[32,4,2048]{2,1,0:T(4,128)S(1)}, f32[32,4,2048]{2,1,0:T(4,128)}, u32[]{:S(2)}) copy-start(f32[32,4,2048]{2,1,0:T(4,128)} %wet_hbm.3) | copy-start | bytes 3145732
  10.1 16.9 %copy-start.2 = (f32[272,256]{1,0:T(8,128)S(1)}, f32[272,256]{1,0:T(8,128)}, u32[]{:S(2)}) copy-start(f32[272,256]{1,0:T(8,128)} %get-tuple-element.33.own) | copy-start | bytes 835588
  10.1 18.2 %copy-start.4 = (f32[128,128]{1,0:T(8,128)S(1)}, f32[128,128]{1,0:T(8,128)}, u32[]{:S(2)}) copy-start(f32[128,128]{1,0:T(8,128)} %thermal_ref.1) | copy-start | bytes 196612
  10.1 18.3 %copy-start.5 = (f32[128,128]{1,0:T(8,128)S(1)}, f32[128,128]{1,0:T(8,128)}, u32[]{:S(2)}) copy-start(f32[128,128]{1,0:T(8,128)} %water_ref.1) | copy-start | bytes 196612
  10.1 18.3 %copy-start.6 = (f32[128,128]{1,0:T(8,128)S(1)}, f32[128,128]{1,0:T(8,128)}, u32[]{:S(2)}) copy-start(f32[128,128]{1,0:T(8,128)} %constant.2.clone.cheb_ref) | copy-start | bytes 196612
  10.1 19.0 %copy-start.7 = (f32[12]{0:T(128)S(1)}, f32[12]{0:T(128)}, u32[]{:S(2)}) copy-start(f32[12]{0:T(128)} %spread_ref.7) | copy-start | bytes 148
  10.1 19.0 %copy-start.8 = (f32[12]{0:T(128)S(1)}, f32[12]{0:T(128)}, u32[]{:S(2)}) copy-start(f32[12]{0:T(128)} %factor_ref.7) | copy-start | bytes 148
  12.2 20.7 %collective-permute-start.2 = (f32[272,256]{1,0:T(8,128)S(1)}, f32[272,256]{1,0:T(8,128)S(1)}, u32[]{:S(2)}, u32[]{:S(2)}) collective-permute-start(f32[272,256]{1,0:T(8,128)S(1)} %get-tuple-element.32), channel_id=1, source_target_pairs={{0,6},{1,7},{2,4},{3,5},{4,2},{5,3},{6,0},{7,1},{8,14},{9,15},{10,... | collective-permute-start | bytes 835592 | tf_op jit(solution)/shard_map/ppermute | solution.py:481
  15.1 17.7 %collective-permute-start.1 = (f32[272,256]{1,0:T(8,128)S(1)}, f32[272,256]{1,0:T(8,128)S(1)}, u32[]{:S(2)}, u32[]{:S(2)}) collective-permute-start(f32[272,256]{1,0:T(8,128)S(1)} %get-tuple-element.31), channel_id=1, source_target_pairs={{0,4},{1,5},{2,6},{3,7},{4,0},{5,1},{6,2},{7,3},{8,12},{9,13},{10,... | collective-permute-start | bytes 835592 | tf_op jit(solution)/shard_map/ppermute | solution.py:481
  21.3 16.2 %collective-permute-start = (f32[272,256]{1,0:T(8,128)S(1)}, f32[272,256]{1,0:T(8,128)S(1)}, u32[]{:S(2)}, u32[]{:S(2)}) collective-permute-start(f32[272,256]{1,0:T(8,128)S(1)} %get-tuple-element.30), channel_id=1, source_target_pairs={{0,2},{1,3},{2,0},{3,1},{4,6},{5,7},{6,4},{7,5},{8,10},{9,11},{10,... | collective-permute-start | bytes 835592 | tf_op jit(solution)/shard_map/ppermute | solution.py:481
  23.5 19.1 %collective-permute-start.13 = (f32[2,272,256]{2,1,0:T(8,128)S(1)}, f32[2,272,256]{2,1,0:T(8,128)S(1)}, u32[]{:S(2)}, u32[]{:S(2)}) collective-permute-start(f32[2,272,256]{2,1,0:T(8,128)S(1)} %pad_maximum_fusion.3), channel_id=1, source_target_pairs={{0,8},{1,9},{2,10},{3,11},{8,16},{9,17},{10,18},{11,19},{12,4},{13... | collective-permute-start | bytes 1671176 | tf_op jit(solution)/shard_map/ppermute | solution.py:481
  27.0 15.5 %collective-permute-start.12 = (f32[2,272,256]{2,1,0:T(8,128)S(1)}, f32[2,272,256]{2,1,0:T(8,128)S(1)}, u32[]{:S(2)}, u32[]{:S(2)}) collective-permute-start(f32[2,272,256]{2,1,0:T(8,128)S(1)} %pad_maximum_fusion.2), channel_id=1, source_target_pairs={{4,12},{5,13},{6,14},{7,15},{8,0},{9,1},{10,2},{11,3},{12,20},{13,... | collective-permute-start | bytes 1671176 | tf_op jit(solution)/shard_map/ppermute | solution.py:481
  32.9 15.1 %collective-permute-start.7 = (f32[2,272,256]{2,1,0:T(8,128)S(1)}, f32[2,272,256]{2,1,0:T(8,128)S(1)}, u32[]{:S(2)}, u32[]{:S(2)}) collective-permute-start(f32[2,272,256]{2,1,0:T(8,128)S(1)} %pad_maximum_fusion.1), channel_id=1, source_target_pairs={{0,8},{1,9},{2,10},{3,11},{8,16},{9,17},{10,18},{11,19},{12,4},{13... | collective-permute-start | bytes 1671176 | tf_op jit(solution)/shard_map/ppermute | solution.py:481
  37.6 14.7 %collective-permute-start.6 = (f32[2,272,256]{2,1,0:T(8,128)S(1)}, f32[2,272,256]{2,1,0:T(8,128)S(1)}, u32[]{:S(2)}, u32[]{:S(2)}) collective-permute-start(f32[2,272,256]{2,1,0:T(8,128)S(1)} %pad_maximum_fusion), channel_id=1, source_target_pairs={{4,12},{5,13},{6,14},{7,15},{8,0},{9,1},{10,2},{11,3},{12,20},{13,... | collective-permute-start | bytes 1671176 | tf_op jit(solution)/shard_map/ppermute | solution.py:481
  48.0 9.8 %collective-permute-start.14 = (f32[2,8,64,256]{3,2,1,0:T(8,128)S(1)}, f32[2,8,64,256]{3,2,1,0:T(8,128)S(1)}, u32[]{:S(2)}, u32[]{:S(2)}) collective-permute-start(f32[2,8,64,256]{3,2,1,0:T(8,128)S(1)} %outer_substeps.3.mine), channel_id=1, source_target_pairs={{0,1},{1,0},{2,3},{3,2},{4,5},{5,4},{6,7},{7,6},{8,9},{9,8},{10,11... | collective-permute-start | bytes 3145736 | tf_op jit(solution)/shard_map/ppermute | solution.py:481
  57.6 4.6 %collective-permute-start.8 = (f32[2,8,64,256]{3,2,1,0:T(8,128)S(1)}, f32[2,8,64,256]{3,2,1,0:T(8,128)S(1)}, u32[]{:S(2)}, u32[]{:S(2)}) collective-permute-start(f32[2,8,64,256]{3,2,1,0:T(8,128)S(1)} %outer_substeps.2.mine), channel_id=1, source_target_pairs={{0,1},{1,0},{2,3},{3,2},{4,5},{5,4},{6,7},{7,6},{8,9},{9,8},{10,11... | collective-permute-start | bytes 3145736 | tf_op jit(solution)/shard_map/ppermute | solution.py:481
  58.7 9.2 %collective-permute-start.15 = (f32[256,256]{1,0:T(8,128)S(1)}, f32[256,256]{1,0:T(8,128)S(1)}, u32[]{:S(2)}, u32[]{:S(2)}) collective-permute-start(f32[256,256]{1,0:T(8,128)S(1)} %get-tuple-element.51), channel_id=1, source_target_pairs={{0,2},{1,3},{2,0},{3,1},{4,6},{5,7},{6,4},{7,5},{8,10},{9,11},{10,... | collective-permute-start | bytes 786440 | tf_op jit(solution)/shard_map/ppermute | solution.py:481
  59.3 20.4 %collective-permute-start.16 = (f32[256,256]{1,0:T(8,128)S(1)}, f32[256,256]{1,0:T(8,128)S(1)}, u32[]{:S(2)}, u32[]{:S(2)}) collective-permute-start(f32[256,256]{1,0:T(8,128)S(1)} %get-tuple-element.52), channel_id=1, source_target_pairs={{0,4},{1,5},{2,6},{3,7},{4,0},{5,1},{6,2},{7,3},{8,12},{9,13},{10,... | collective-permute-start | bytes 786440 | tf_op jit(solution)/shard_map/ppermute | solution.py:481
  59.3 20.4 %collective-permute-start.17 = (f32[256,256]{1,0:T(8,128)S(1)}, f32[256,256]{1,0:T(8,128)S(1)}, u32[]{:S(2)}, u32[]{:S(2)}) collective-permute-start(f32[256,256]{1,0:T(8,128)S(1)} %get-tuple-element.53), channel_id=1, source_target_pairs={{0,6},{1,7},{2,4},{3,5},{4,2},{5,3},{6,0},{7,1},{8,14},{9,15},{10,... | collective-permute-start | bytes 786440 | tf_op jit(solution)/shard_map/ppermute | solution.py:481
  63.3 21.3 %collective-permute-start.10 = (f32[256,256]{1,0:T(8,128)S(1)}, f32[256,256]{1,0:T(8,128)S(1)}, u32[]{:S(2)}, u32[]{:S(2)}) collective-permute-start(f32[256,256]{1,0:T(8,128)S(1)} %get-tuple-element.46), channel_id=1, source_target_pairs={{0,4},{1,5},{2,6},{3,7},{4,0},{5,1},{6,2},{7,3},{8,12},{9,13},{10,... | collective-permute-start | bytes 786440 | tf_op jit(solution)/shard_map/ppermute | solution.py:481
  63.3 21.2 %collective-permute-start.11 = (f32[256,256]{1,0:T(8,128)S(1)}, f32[256,256]{1,0:T(8,128)S(1)}, u32[]{:S(2)}, u32[]{:S(2)}) collective-permute-start(f32[256,256]{1,0:T(8,128)S(1)} %get-tuple-element.47), channel_id=1, source_target_pairs={{0,6},{1,7},{2,4},{3,5},{4,2},{5,3},{6,0},{7,1},{8,14},{9,15},{10,... | collective-permute-start | bytes 786440 | tf_op jit(solution)/shard_map/ppermute | solution.py:481
  67.9 16.7 %collective-permute-start.9 = (f32[256,256]{1,0:T(8,128)S(1)}, f32[256,256]{1,0:T(8,128)S(1)}, u32[]{:S(2)}, u32[]{:S(2)}) collective-permute-start(f32[256,256]{1,0:T(8,128)S(1)} %get-tuple-element.45), channel_id=1, source_target_pairs={{0,2},{1,3},{2,0},{3,1},{4,6},{5,7},{6,4},{7,5},{8,10},{9,11},{10,... | collective-permute-start | bytes 786440 | tf_op jit(solution)/shard_map/ppermute | solution.py:481

commit v3 on v2

--- a/solution.py
+++ b/solution.py
@@ -15,6 +15,9 @@
 PARTS = (2, 2)
 JOINT = ("lat", "depth")
 BODY = 2 * ROWS * SLAB
+PIECES = 1
+HOP_ROWS = 816
+TAIL_ROWS = 136
 VMEM_LIMIT = 48 * 1024 * 1024
 FIRST_LIMIT = 62 * 1024 * 1024
 
@@ -59,10 +62,18 @@
 
 
 def column_start(k, mask, columns):
-    offset = sum(chunk_width(i, columns) for i in range(k))
-    return pl.multiple_of(
-        lax.bitwise_xor(quarter(), mask) * (columns // 4) + offset, 128
-    )
+    width = chunk_width(k, columns)
+    place_in_chunk = lax.bitwise_xor(quarter(), mask) * width
+    return pl.multiple_of(chunk_start(k, columns) + place_in_chunk, 128)
+
+
+def chunk_start(k, columns):
+    return sum(4 * chunk_width(i, columns) for i in range(k))
+
+
+def chunk_window(k, columns):
+    first = max(chunk_start(k, columns) - 128, 0)
+    return first, min(chunk_start(k + 1, columns) + 128, columns)
 
 
 def halo_at(f, width):
@@ -84,38 +95,32 @@
 def pack_kernel(k, width, heat_hbm, wet_hbm, label_hbm, *refs):
     *blocks, near, label_ref, sems = refs
     columns = heat_hbm.shape[2]
-    window = near.shape[4]
-    labels = pltpu.make_async_copy(label_hbm, label_ref, sems.at[8])
-    labels.start()
-    bases, copies = [], []
-    for mask in (1, 2, 3, 0):
-        start = column_start(k, mask, columns)
-        base = pl.multiple_of(jnp.clip(start - 128, 0, columns - window), 128)
-        pair = [
-            pltpu.make_async_copy(
-                far.at[:, :, pl.ds(base, window)], near.at[mask, f], sems.at[2 * mask + f]
+    first, last = chunk_window(k, columns)
+    copies = [pltpu.make_async_copy(label_hbm, label_ref, sems.at[2 * PIECES])]
+    for f, far in enumerate((heat_hbm, wet_hbm)):
+        for piece in range(PIECES):
+            at = pl.ds(piece * (SLAB // PIECES), SLAB // PIECES)
+            copies.append(
+                pltpu.make_async_copy(
+                    far.at[at, :, first:last], near.at[f, at], sems.at[f * PIECES + piece]
+                )
             )
-            for f, far in enumerate((heat_hbm, wet_hbm))
-        ]
-        for copy in pair:
-            copy.start()
-        bases.append(base)
-        copies.append(pair)
-    labels.wait()
+    for copy in copies:
+        copy.start()
+    for copy in copies:
+        copy.wait()
     lane = lanes((SLAB, 128))
     lane8 = lanes((8, 128))
     lane4 = lanes((ROWS, 128))
-    for mask, base, pair in zip((1, 2, 3, 0), bases, copies):
-        for copy in pair:
-            copy.wait()
+    for mask in range(4):
         start = column_start(k, mask, columns)
         left = pl.multiple_of(jnp.maximum(start - 128, 0), 128)
         right = pl.multiple_of(jnp.minimum(start + width, columns - 128), 128)
         keep_left = (start > 0).astype(jnp.float32)
         keep_right = (start + width < columns).astype(jnp.float32)
-        main, before, after = (pl.multiple_of(at - base, 128) for at in (start, left, right))
+        main, before, after = (pl.multiple_of(at - first, 128) for at in (start, left, right))
         for f in range(2):
-            ref = near.at[mask, f]
+            ref = near.at[f]
             packed = jnp.zeros((8, 128), jnp.float32)
             for r in range(ROWS):
                 row = (f * ROWS + r) * SLAB
@@ -148,15 +153,16 @@
 
 def pack(k, width, heat, wet, label):
     shape = jax.ShapeDtypeStruct((block_rows(width), width), jnp.float32)
+    first, last = chunk_window(k, heat.shape[2])
     return pl.pallas_call(
         functools.partial(pack_kernel, k, width),
         out_shape=[shape] * 4,
         in_specs=[pl.BlockSpec(memory_space=pltpu.HBM)] * 3,
         out_specs=[pl.BlockSpec(memory_space=pltpu.VMEM)] * 4,
         scratch_shapes=[
-            pltpu.VMEM((4, 2, SLAB, ROWS, min(width + 256, heat.shape[2])), jnp.float32),
+            pltpu.VMEM((2, SLAB, ROWS, last - first), jnp.float32),
             pltpu.VMEM(label.shape, jnp.int32),
-            pltpu.SemaphoreType.DMA((9,)),
+            pltpu.SemaphoreType.DMA((2 * PIECES + 1,)),
         ],
         compiler_params=params(VMEM_LIMIT if k else FIRST_LIMIT),
         cost_estimate=cost(0, 4 << 20),
@@ -295,7 +301,7 @@
                                 inner[INNER.index((t, i)), f, at, :] = levels[t][i][f]
             return carry
 
-        lax.fori_loop(0, SLAB // 8, group, 0)
+        lax.fori_loop(0, SLAB // 8, group, 0, unroll=2)
 
 
 def pre(width, own, rx, ry, rxy, spread, factor, after):
@@ -318,7 +324,7 @@
 
 
 def stencil_kernel(
-    width, own, rx, ry, rxy, p1, p2, inner, kap_ref, spread_ref, factor_ref, _, post, kap
+    width, own, rx, ry, rxy, p1, p2, inner, kap_ref, spread_ref, factor_ref, post_own, post_partner, kap
 ):
     kap[:, ROWS : 3 * ROWS, :] = kap_ref[...]
     for j, block in ((0, p2.at[0]), (3, p1.at[0])):
@@ -344,27 +350,26 @@
                             prev[i - 1], prev[i], prev[i + 1], kap[0, i : i + 1, :], kap[1, i : i + 1, :]
                         )
                         if t == 4:
-                            row = (i - ROWS) // ROWS * ROWS + stored(i % ROWS)
+                            post = (post_own, post_partner)[(i - ROWS) // ROWS]
                             for f in range(2):
-                                post[f, row, at, :] = levels[4][i][f][:, :width]
+                                post[f, stored(i % ROWS), at, :] = levels[4][i][f][:, :width]
             return carry
 
         lax.fori_loop(0, SLAB // 8, group, 0)
 
 
-def stencil(width, own, rx, ry, rxy, p1, p2, inner, kap, spread, factor, after):
+def stencil(width, own, rx, ry, rxy, p1, p2, inner, kap, spread, factor):
     return pl.pallas_call(
         functools.partial(stencil_kernel, width),
-        out_shape=jax.ShapeDtypeStruct((2, 2 * ROWS, 2 * SLAB, width), jnp.float32),
+        out_shape=[jax.ShapeDtypeStruct((2, ROWS, 2 * SLAB, width), jnp.float32)] * 2,
         in_specs=[pl.BlockSpec(memory_space=pltpu.VMEM)] * 8
-        + [pl.BlockSpec(memory_space=pltpu.SMEM)] * 2
-        + [pl.BlockSpec(memory_space=pl.ANY)],
-        out_specs=pl.BlockSpec(memory_space=pltpu.VMEM),
+        + [pl.BlockSpec(memory_space=pltpu.SMEM)] * 2,
+        out_specs=[pl.BlockSpec(memory_space=pltpu.VMEM)] * 2,
         scratch_shapes=[pltpu.VMEM((2, COUNT, width + 128), jnp.float32)],
         compiler_params=params(),
         cost_estimate=cost(1 << 24, 4 << 20),
         name="outer_substeps",
-    )(own, rx, ry, rxy, p1, p2, inner, kap, spread, factor, after)
+    )(own, rx, ry, rxy, p1, p2, inner, kap, spread, factor)
 
 
 def split(values):
@@ -372,7 +377,8 @@
     return high, (values - high.astype(jnp.float32)).astype(jnp.bfloat16)
 
 
-def solve_kernel(mine, other, stack_w, stack_h, km, *blocks):
+def solve_kernel(*refs):
+    mine, other, (stack_w, stack_h, km), blocks = refs[:2], refs[2:4], refs[4:7], refs[7:]
     dot = functools.partial(jnp.dot, preferred_element_type=jnp.float32)
     half = 2 * SLAB
 
@@ -383,14 +389,14 @@
         return both[:count] + both[count:] + dot(stack[:count, :], low)
 
     for r in range(2 * ROWS):
-        heat = apply(stack_h, jnp.concatenate([mine[0, r], other[0, r]], axis=0))
-        wet = apply(stack_w, jnp.concatenate([mine[1, r], other[1, r]], axis=0))
+        strip, inner = divmod(r, ROWS)
+        heat = apply(stack_h, jnp.concatenate([mine[strip][0, inner], other[strip][0, inner]], axis=0))
+        wet = apply(stack_w, jnp.concatenate([mine[strip][1, inner], other[strip][1, inner]], axis=0))
         factor = km[r : r + 1, :]
         results = (
             heat + factor * wet[half : 2 * half],
             wet[:half] + factor * wet[2 * half :],
         )
-        strip, inner = divmod(r, ROWS)
         for f in range(2):
             base = (f * ROWS + inner) * SLAB
             for slab in range(2):
@@ -404,12 +410,12 @@
     return pl.pallas_call(
         solve_kernel,
         out_shape=[shape] * 4,
-        in_specs=[pl.BlockSpec(memory_space=pltpu.VMEM)] * 5,
+        in_specs=[pl.BlockSpec(memory_space=pltpu.VMEM)] * 7,
         out_specs=[pl.BlockSpec(memory_space=pltpu.VMEM)] * 4,
         compiler_params=params(),
         cost_estimate=cost(1 << 26, 4 << 20),
         name="solve",
-    )(mine, other, stack_w, stack_h, km)
+    )(*mine, *other, stack_w, stack_h, km)
 
 
 def assemble_kernel(k, width, *refs):
@@ -433,13 +439,14 @@
         copy.wait()
 
 
-def assemble(k, width, columns, blocks, outs):
+def assemble(k, width, columns, blocks, outs, tail):
     shape = jax.ShapeDtypeStruct((SLAB, ROWS, columns), jnp.float32)
     return pl.pallas_call(
         functools.partial(assemble_kernel, k, width),
         out_shape=[shape] * 2,
         in_specs=[pl.BlockSpec(memory_space=pltpu.VMEM)] * 4
-        + [pl.BlockSpec(memory_space=pltpu.HBM)] * len(outs),
+        + [pl.BlockSpec(memory_space=pltpu.HBM)] * len(outs)
+        + [pl.BlockSpec(memory_space=pl.ANY)] * len(tail),
         out_specs=[pl.BlockSpec(memory_space=pltpu.HBM)] * 2,
         scratch_shapes=[
             pltpu.VMEM((4, 2, SLAB, ROWS, width), jnp.float32),
@@ -449,7 +456,7 @@
         compiler_params=params(),
         cost_estimate=cost(0, 4 << 20),
         name="assemble",
-    )(*blocks, *outs)
+    )(*blocks, *outs, *tail)
 
 
 def routes(strips):
@@ -486,24 +493,31 @@
         received.append((own, send(bx, "x"), send(by, "y"), send(bxy, "xy")))
     stack_w, stack_h = prep(thermal, water)
     outs = []
-    inners, beyond = [], []
+    before, tail = None, []
+
+    def after(value, *others):
+        return lax.optimization_barrier((value, *others))[0] if others else value
+
     for k, width in enumerate(widths):
         own, rx, ry, rxy = received[k]
         if k:
-            rxy, _ = lax.optimization_barrier((rxy, inners[-1][2]))
-            received[k] = (own, rx, ry, rxy)
-        beyond.append((send(jnp.stack([own, rx]), "own"), send(jnp.stack([ry, rxy]), "partner")))
-        inners.append(pre(width, own, rx, ry, rxy, spread, factor, stack_h))
-    for k, width in enumerate(widths):
-        own, rx, ry, rxy = received[k]
-        inner, kap, km = inners[k]
-        p1, p2 = beyond[k]
-        after = inners[k + 1][2] if k + 1 < len(widths) else km
-        post = stencil(width, own, rx, ry, rxy, p1, p2, inner, kap, spread, factor, after)
-        other = send(post, "core")
-        kept, bx, by, bxy = solve(width, post, other, stack_w, stack_h, km)
-        blocks = [kept, send(bx, "x"), send(by, "y"), send(bxy, "xy")]
-        outs = assemble(k, width, columns, blocks, outs)
+            ry = after(ry, before[1])
+            hop = send(jnp.concatenate([rx, ry, rxy, own])[:HOP_ROWS], "core")
+        p1 = send(jnp.stack([own, rx]), "own")
+        p2 = send(jnp.stack([ry, rxy]), "partner")
+        inner, kap, km = pre(width, own, rx, ry, rxy, spread, factor, hop if k else stack_h)
+        if k:
+            kap = after(kap, before[0])
+        mine = stencil(width, own, rx, ry, rxy, p1, p2, inner, kap, spread, factor)
+        other = [send(piece, "core") for piece in mine]
+        kept, bx, by, bxy = solve(width, mine, other, stack_w, stack_h, km)
+        arrived = [send(bx, "x"), send(by, "y"), send(bxy, "xy")]
+        before = (kept, km)
+        outs = assemble(k, width, columns, [kept, *arrived], outs, tail)
+        if k + 1 < len(widths):
+            tail = [send(jnp.concatenate([block[:TAIL_ROWS] for block in arrived]), "core")]
+        else:
+            tail = []
     return tuple(outs)
 
 

time: 85.9 us -> 81.4 us (0.948)
  waiting for transfers between devices: 27.6 us -> 20.6 us
  starting transfers between devices: 27.1 us -> 31.1 us
  Pallas kernels: 28.6 us -> 26.7 us
    ppermute x18 -> x22, waiting for transfers between devices: 27.6 us -> 20.6 us  [send(): return lax.ppermute(array, JOINT, route[name])]
    ppermute x18 -> x22, starting transfers between devices: 27.1 us -> 31.1 us  [send(): return lax.ppermute(array, JOINT, route[name])]
    pallas_call x2, Pallas kernels: 7.43 us -> 6.04 us  [pre(): pl.pallas_call(functools.partial(pre_kernel, width), out_shape=[jax.Shape...]
  transfers between devices with their start and end apart: 18 -> 22, of which waited for: 5 -> 7; matrix products, arithmetic and copies ran while one was open for 0% -> 0% of each run, Pallas kernels for 28% -> 27%
where the time goes in v3:
time: 81.4 us; the launch traced here: 81.1 us
  starting transfers between devices  31.1 us (38%)
  Pallas kernels  26.7 us (33%)
  waiting for transfers between devices  20.6 us (25%)
  local copies, waits for them, and re-layouts  1.29 us (2%)
  between operations  1.14 us (1%)
    ppermute x22, starting transfers between devices, send(): return lax.ppermute(array, JOINT, route[name])  31.1 us
    ppermute x22, waiting for transfers between devices, send(): return lax.ppermute(array, JOINT, route[name])  20.6 us
    pallas_call x2, Pallas kernels, stencil(): pl.pallas_call(functools.partial(stencil_kernel, width), out_shape=[jax.S...  10.7 us
    pallas_call x2, Pallas kernels, pre(): pl.pallas_call(functools.partial(pre_kernel, width), out_shape=[jax.Shape...  6.04 us
    pallas_call x2, Pallas kernels, pack(): pl.pallas_call(functools.partial(pack_kernel, k, width), out_shape=[shape...  5.19 us
    pallas_call x2, Pallas kernels, assemble(): pl.pallas_call(functools.partial(assemble_kernel, k, width), out_shape=[s...  2.14 us
    pallas_call x2, Pallas kernels, solve(): pl.pallas_call(solve_kernel, out_shape=[shape] * 4, in_specs=[pl.BlockSpe...  1.98 us
  transfers between devices with their start and end apart: 22, of which 7 were waited for; matrix products, arithmetic and copies ran while one was open for 0% of the time, Pallas kernels for 27%

profile of v3, /device:TPU:0, one launch (start us, length us, event | category | flops | bytes accessed | tf_op | source)
XLA Modules:
  0.0 81.1 jit_solution(16103271096462700605)
XLA Ops:
  0.6 0.0 copy-start.3
  0.6 0.0 copy-start
  0.6 3.5 %pack.3 = (f32[272,256]{1,0:T(8,128)}, f32[272,256]{1,0:T(8,128)}, f32[272,256]{1,0:T(8,128)}, f32[272,256]{1,0:T(8,128)}) custom-call(f32[32,4,2048]{2,1,0:T(4,128)} %heat_hbm.3, f32[32,4,2048]{2,1,0:T(4,128)} %wet_hbm.3, s32[4,2048]{1,0:T(4,128)} %label_hbm.3), custom_call_target="tpu_custom_call" | custom-call | bytes 1024 | tf_op jit(solution)/shard_map/pack/pallas_call | solution.py:157
  4.2 3.0 %collective-permute-start.2 = (f32[272,256]{1,0:T(8,128)}, f32[272,256]{1,0:T(8,128)S(1)}, u32[]{:S(2)}, u32[]{:S(2)}) collective-permute-start(f32[272,256]{1,0:T(8,128)} %get-tuple-element.38), channel_id=1, source_target_pairs={{0,2},{1,3},{2,0},{3,1},{4,6},{5,7},{6,4},{7,5},{8,10},{9,11},{10,... | collective-permute-start | bytes 835592 | tf_op jit(solution)/shard_map/ppermute | solution.py:488
  7.2 1.5 %collective-permute-start.3 = (f32[272,256]{1,0:T(8,128)}, f32[272,256]{1,0:T(8,128)S(1)}, u32[]{:S(2)}, u32[]{:S(2)}) collective-permute-start(f32[272,256]{1,0:T(8,128)} %get-tuple-element.39), channel_id=1, source_target_pairs={{0,4},{1,5},{2,6},{3,7},{4,0},{5,1},{6,2},{7,3},{8,12},{9,13},{10,... | collective-permute-start | bytes 835592 | tf_op jit(solution)/shard_map/ppermute | solution.py:488
  8.7 0.0 collective-permute-start.4
  8.7 0.0 copy-done.3
  8.7 0.0 copy-done
  8.7 1.2 %copy-done.1 = f32[32,4,2048]{2,1,0:T(4,128)S(1)} copy-done((f32[32,4,2048]{2,1,0:T(4,128)S(1)}, f32[32,4,2048]{2,1,0:T(4,128)}, u32[]{:S(2)}) %copy-start.1) | copy-done | bytes 1048600
  10.0 0.0 copy-start.7
  10.0 0.0 copy-start.8
  10.0 1.7 %pack.2 = (f32[272,256]{1,0:T(8,128)S(1)}, f32[272,256]{1,0:T(8,128)S(1)}, f32[272,256]{1,0:T(8,128)S(1)}, f32[272,256]{1,0:T(8,128)S(1)}) custom-call(f32[32,4,2048]{2,1,0:T(4,128)S(1)} %copy-done, f32[32,4,2048]{2,1,0:T(4,128)S(1)} %copy-done.1, s32[4,2048]{1,0:T(4,128)S(1)} %copy-done.3), custom_call_target="tpu_custom_call" | custom-call | bytes 1024 | tf_op jit(solution)/shard_map/pack/pallas_call | solution.py:157
  11.7 2.0 %collective-permute-start = (f32[272,256]{1,0:T(8,128)S(1)}, f32[272,256]{1,0:T(8,128)S(1)}, u32[]{:S(2)}, u32[]{:S(2)}) collective-permute-start(f32[272,256]{1,0:T(8,128)S(1)} %get-tuple-element.35), channel_id=1, source_target_pairs={{0,2},{1,3},{2,0},{3,1},{4,6},{5,7},{6,4},{7,5},{8,10},{9,11},{10,... | collective-permute-start | bytes 835592 | tf_op jit(solution)/shard_map/ppermute | solution.py:488
  13.7 1.5 %collective-permute-start.1 = (f32[272,256]{1,0:T(8,128)S(1)}, f32[272,256]{1,0:T(8,128)S(1)}, u32[]{:S(2)}, u32[]{:S(2)}) collective-permute-start(f32[272,256]{1,0:T(8,128)S(1)} %get-tuple-element.36), channel_id=1, source_target_pairs={{0,4},{1,5},{2,6},{3,7},{4,0},{5,1},{6,2},{7,3},{8,12},{9,13},{10,... | collective-permute-start | bytes 835592 | tf_op jit(solution)/shard_map/ppermute | solution.py:488
  15.2 0.0 collective-permute-done.2.rx
  15.2 2.7 %collective-permute-start.5 = (f32[272,256]{1,0:T(8,128)S(1)}, f32[272,256]{1,0:T(8,128)S(1)}, u32[]{:S(2)}, u32[]{:S(2)}) collective-permute-start(f32[272,256]{1,0:T(8,128)S(1)} %get-tuple-element.44), channel_id=1, source_target_pairs={{0,6},{1,7},{2,4},{3,5},{4,2},{5,3},{6,0},{7,1},{8,14},{9,15},{10,... | collective-permute-start | bytes 835592 | tf_op jit(solution)/shard_map/ppermute | solution.py:488
  17.9 0.0 copy-done.2
  17.9 4.4 %collective-permute-done.3.ry = f32[272,256]{1,0:T(8,128)S(1)} collective-permute-done((f32[272,256]{1,0:T(8,128)}, f32[272,256]{1,0:T(8,128)S(1)}, u32[]{:S(2)}, u32[]{:S(2)}) %collective-permute-start.3) | collective-permute-done | bytes 278560 | tf_op jit(solution)/shard_map/ppermute | solution.py:488
  22.3 1.3 %collective-permute-start.9 = (f32[2,272,256]{2,1,0:T(8,128)S(1)}, f32[2,272,256]{2,1,0:T(8,128)S(1)}, u32[]{:S(2)}, u32[]{:S(2)}) collective-permute-start(f32[2,272,256]{2,1,0:T(8,128)S(1)} %pad_maximum_fusion.3), channel_id=1, source_target_pairs={{4,12},{5,13},{6,14},{7,15},{8,0},{9,1},{10,2},{11,3},{12,20},{13,... | collective-permute-start | bytes 1671176 | tf_op jit(solution)/shard_map/ppermute | solution.py:488
  23.6 0.0 collective-permute-done.4.rxy
  23.7 4.6 %collective-permute-start.10 = (f32[2,272,256]{2,1,0:T(8,128)S(1)}, f32[2,272,256]{2,1,0:T(8,128)S(1)}, u32[]{:S(2)}, u32[]{:S(2)}) collective-permute-start(f32[2,272,256]{2,1,0:T(8,128)S(1)} %pad_maximum_fusion.4), channel_id=1, source_target_pairs={{0,8},{1,9},{2,10},{3,11},{8,16},{9,17},{10,18},{11,19},{12,4},{13... | collective-permute-start | bytes 1671176 | tf_op jit(solution)/shard_map/ppermute | solution.py:488
  28.3 0.7 prep.1
  29.0 3.0 %inner_substeps.2 = (f32[10,2,64,384]{3,2,1,0:T(8,128)S(1)}, f32[2,8,384]{2,1,0:T(8,128)S(1)}, f32[8,256]{1,0:T(8,128)S(1)}) custom-call(f32[272,256]{1,0:T(8,128)S(1)} %copy-done.2, f32[272,256]{1,0:T(8,128)S(1)} %collective-permute-done.2.rx, f32[272,256]{1,0:T(8,128)S(1)} %collective-permute-done.3.ry, f32[272,256]{1,0:T(8,128)S(1)} %collective-permute-done.4.rxy, ...), custom_call_target="tpu_custom_call" | custom-call | bytes 1024 | tf_op jit(solution)/shard_map/inner_substeps/pallas_call | solution.py:309
  32.1 1.3 %collective-permute-done.1.ry = f32[272,256]{1,0:T(8,128)S(1)} collective-permute-done((f32[272,256]{1,0:T(8,128)S(1)}, f32[272,256]{1,0:T(8,128)S(1)}, u32[]{:S(2)}, u32[]{:S(2)}) %collective-permute-start.1) | collective-permute-done | bytes 278560 | tf_op jit(solution)/shard_map/ppermute | solution.py:488
  33.4 0.0 collective-permute-done.rx
  33.4 0.0 collective-permute-done.5.rxy
  33.4 0.1 pad_maximum_fusion
  33.5 0.1 collective-permute-start.8
  33.6 1.3 %collective-permute-start.6 = (f32[2,272,256]{2,1,0:T(8,128)S(1)}, f32[2,272,256]{2,1,0:T(8,128)S(1)}, u32[]{:S(2)}, u32[]{:S(2)}) collective-permute-start(f32[2,272,256]{2,1,0:T(8,128)S(1)} %pad_maximum_fusion.1), channel_id=1, source_target_pairs={{4,12},{5,13},{6,14},{7,15},{8,0},{9,1},{10,2},{11,3},{12,20},{13,... | collective-permute-start | bytes 1671176 | tf_op jit(solution)/shard_map/ppermute | solution.py:488
  35.0 4.8 %collective-permute-start.7 = (f32[2,272,256]{2,1,0:T(8,128)S(1)}, f32[2,272,256]{2,1,0:T(8,128)S(1)}, u32[]{:S(2)}, u32[]{:S(2)}) collective-permute-start(f32[2,272,256]{2,1,0:T(8,128)S(1)} %pad_maximum_fusion.2), channel_id=1, source_target_pairs={{0,8},{1,9},{2,10},{3,11},{8,16},{9,17},{10,18},{11,19},{12,4},{13... | collective-permute-start | bytes 1671176 | tf_op jit(solution)/shard_map/ppermute | solution.py:488
  39.7 0.0 collective-permute-done.9.p1
  39.7 0.0 collective-permute-done.10.p2
  39.7 5.3 %outer_substeps.2 = (f32[2,4,64,256]{3,2,1,0:T(8,128)S(1)}, f32[2,4,64,256]{3,2,1,0:T(8,128)S(1)}) custom-call(f32[272,256]{1,0:T(8,128)S(1)} %copy-done.2, f32[272,256]{1,0:T(8,128)S(1)} %collective-permute-done.2.rx, f32[272,256]{1,0:T(8,128)S(1)} %collective-permute-done.3.ry, f32[272,256]{1,0:T(8,128)S(1)} %collective-permute-done.4.rxy, ...), custom_call_target="tpu_custom_call" | custom-call | bytes 1024 | tf_op jit(solution)/shard_map/outer_substeps/pallas_call | solution.py:362
  45.1 0.1 collective-permute-start.11
  45.2 0.5 collective-permute-start.12
  45.7 1.4 %collective-permute-done.11.refs_2_ = f32[2,4,64,256]{3,2,1,0:T(8,128)S(1)} collective-permute-done((f32[2,4,64,256]{3,2,1,0:T(8,128)S(1)}, f32[2,4,64,256]{3,2,1,0:T(8,128)S(1)}, u32[]{:S(2)}, u32[]{:S(2)}) %collective-permute-start.11) | collective-permute-done | bytes 524320 | tf_op jit(solution)/shard_map/ppermute | solution.py:488
  47.1 0.7 collective-permute-done.12.refs_3_
  47.8 1.0 %solve.2 = (f32[256,256]{1,0:T(8,128)S(1)}, f32[256,256]{1,0:T(8,128)S(1)}, f32[256,256]{1,0:T(8,128)S(1)}, f32[256,256]{1,0:T(8,128)S(1)}) custom-call(f32[2,4,64,256]{3,2,1,0:T(8,128)S(1)} %get-tuple-element.49.refs_0_, f32[2,4,64,256]{3,2,1,0:T(8,128)S(1)} %get-tuple-element.50.refs_1_, f32[2,4,64,256]{3,2,1,0:T(8,128)S(1)} %collective-permute-done.11.refs_2_, ...), custom_call_target="tpu_custom_call" | custom-call | bytes 1024 | tf_op jit(solution)/shard_map/solve/pallas_call | solution.py:410
  48.8 1.3 %collective-permute-start.18 = (f32[256,256]{1,0:T(8,128)S(1)}, f32[256,256]{1,0:T(8,128)S(1)}, u32[]{:S(2)}, u32[]{:S(2)}) collective-permute-start(f32[256,256]{1,0:T(8,128)S(1)} %get-tuple-element.61), channel_id=1, source_target_pairs={{0,2},{1,3},{2,0},{3,1},{4,6},{5,7},{6,4},{7,5},{8,10},{9,11},{10,... | collective-permute-start | bytes 786440 | tf_op jit(solution)/shard_map/ppermute | solution.py:488
  50.1 0.0 collective-permute-start.19
  50.1 0.0 collective-permute-done.8._
  50.2 2.2 %collective-permute-start.20 = (f32[256,256]{1,0:T(8,128)S(1)}, f32[256,256]{1,0:T(8,128)S(1)}, u32[]{:S(2)}, u32[]{:S(2)}) collective-permute-start(f32[256,256]{1,0:T(8,128)S(1)} %get-tuple-element.63), channel_id=1, source_target_pairs={{0,6},{1,7},{2,4},{3,5},{4,2},{5,3},{6,0},{7,1},{8,14},{9,15},{10,... | collective-permute-start | bytes 786440 | tf_op jit(solution)/shard_map/ppermute | solution.py:488
  52.4 3.0 %inner_substeps.3 = (f32[10,2,64,384]{3,2,1,0:T(8,128)S(1)}, f32[2,8,384]{2,1,0:T(8,128)S(1)}, f32[8,256]{1,0:T(8,128)S(1)}) custom-call(f32[272,256]{1,0:T(8,128)S(1)} %get-tuple-element.34.own, f32[272,256]{1,0:T(8,128)S(1)} %collective-permute-done.rx, f32[272,256]{1,0:T(8,128)S(1)} %collective-permute-done.1.ry, ...), custom_call_target="tpu_custom_call" | custom-call | bytes 1024 | tf_op jit(solution)/shard_map/inner_substeps/pallas_call | solution.py:309
  55.4 0.0 collective-permute-done.6.p1
  55.4 0.0 collective-permute-done.7.p2
  55.4 5.3 %outer_substeps.3 = (f32[2,4,64,256]{3,2,1,0:T(8,128)S(1)}, f32[2,4,64,256]{3,2,1,0:T(8,128)S(1)}) custom-call(f32[272,256]{1,0:T(8,128)S(1)} %get-tuple-element.34.own, f32[272,256]{1,0:T(8,128)S(1)} %collective-permute-done.rx, f32[272,256]{1,0:T(8,128)S(1)} %collective-permute-done.1.ry, f32[272,256]{1,0:T(8,128)S(1)} %collective-permute-done.5.rxy, ...), custom_call_target="tpu_custom_call" | custom-call | bytes 1024 | tf_op jit(solution)/shard_map/outer_substeps/pallas_call | solution.py:362
  60.8 0.1 collective-permute-start.13
  60.8 0.5 collective-permute-start.14
  61.3 0.0 collective-permute-done.18.refs_1_
  61.3 2.5 %collective-permute-done.19.refs_2_ = f32[256,256]{1,0:T(8,128)S(1)} collective-permute-done((f32[256,256]{1,0:T(8,128)S(1)}, f32[256,256]{1,0:T(8,128)S(1)}, u32[]{:S(2)}, u32[]{:S(2)}) %collective-permute-start.19) | collective-permute-done | bytes 262176 | tf_op jit(solution)/shard_map/ppermute | solution.py:488
  63.9 0.0 collective-permute-done.20.refs_3_
  63.9 0.1 collective-permute-start.21
  64.0 0.0 collective-permute-done.13.refs_2_
  64.0 0.0 collective-permute-done.14.refs_3_
  64.0 1.0 %solve.3 = (f32[256,256]{1,0:T(8,128)S(1)}, f32[256,256]{1,0:T(8,128)S(1)}, f32[256,256]{1,0:T(8,128)S(1)}, f32[256,256]{1,0:T(8,128)S(1)}) custom-call(f32[2,4,64,256]{3,2,1,0:T(8,128)S(1)} %get-tuple-element.54.refs_0_, f32[2,4,64,256]{3,2,1,0:T(8,128)S(1)} %get-tuple-element.55.refs_1_, f32[2,4,64,256]{3,2,1,0:T(8,128)S(1)} %collective-permute-done.13.refs_2_, ...), custom_call_target="tpu_custom_call" | custom-call | bytes 1024 | tf_op jit(solution)/shard_map/solve/pallas_call | solution.py:410
  65.0 0.8 %collective-permute-start.15 = (f32[256,256]{1,0:T(8,128)S(1)}, f32[256,256]{1,0:T(8,128)S(1)}, u32[]{:S(2)}, u32[]{:S(2)}) collective-permute-start(f32[256,256]{1,0:T(8,128)S(1)} %get-tuple-element.58), channel_id=1, source_target_pairs={{0,2},{1,3},{2,0},{3,1},{4,6},{5,7},{6,4},{7,5},{8,10},{9,11},{10,... | collective-permute-start | bytes 786440 | tf_op jit(solution)/shard_map/ppermute | solution.py:488
  65.8 1.0 %collective-permute-start.16 = (f32[256,256]{1,0:T(8,128)S(1)}, f32[256,256]{1,0:T(8,128)S(1)}, u32[]{:S(2)}, u32[]{:S(2)}) collective-permute-start(f32[256,256]{1,0:T(8,128)S(1)} %get-tuple-element.59), channel_id=1, source_target_pairs={{0,4},{1,5},{2,6},{3,7},{4,0},{5,1},{6,2},{7,3},{8,12},{9,13},{10,... | collective-permute-start | bytes 786440 | tf_op jit(solution)/shard_map/ppermute | solution.py:488
  66.8 1.8 %collective-permute-start.17 = (f32[256,256]{1,0:T(8,128)S(1)}, f32[256,256]{1,0:T(8,128)S(1)}, u32[]{:S(2)}, u32[]{:S(2)}) collective-permute-start(f32[256,256]{1,0:T(8,128)S(1)} %get-tuple-element.60), channel_id=1, source_target_pairs={{0,6},{1,7},{2,4},{3,5},{4,2},{5,3},{6,0},{7,1},{8,14},{9,15},{10,... | collective-permute-start | bytes 786440 | tf_op jit(solution)/shard_map/ppermute | solution.py:488
  68.6 1.1 %assemble.2 = (f32[32,4,2048]{2,1,0:T(4,128)}, f32[32,4,2048]{2,1,0:T(4,128)}) custom-call(f32[256,256]{1,0:T(8,128)S(1)} %get-tuple-element.52.refs_0_, f32[256,256]{1,0:T(8,128)S(1)} %collective-permute-done.18.refs_1_, f32[256,256]{1,0:T(8,128)S(1)} %collective-permute-done.19.refs_2_, f32[256,256]{1,0:T(8,128)S(1)} %collective-permute-done.20.refs_3_), custom_call_target="tpu_custom_call" | custom-call | bytes 1024 | tf_op jit(solution)/shard_map/assemble/pallas_call | solution.py:444
  69.6 0.0 collective-permute-done.21.refs_6_
  69.7 4.5 %collective-permute-done.15.refs_1_ = f32[256,256]{1,0:T(8,128)S(1)} collective-permute-done((f32[256,256]{1,0:T(8,128)S(1)}, f32[256,256]{1,0:T(8,128)S(1)}, u32[]{:S(2)}, u32[]{:S(2)}) %collective-permute-start.15) | collective-permute-done | bytes 262176 | tf_op jit(solution)/shard_map/ppermute | solution.py:488
  74.2 5.7 %collective-permute-done.16.refs_2_ = f32[256,256]{1,0:T(8,128)S(1)} collective-permute-done((f32[256,256]{1,0:T(8,128)S(1)}, f32[256,256]{1,0:T(8,128)S(1)}, u32[]{:S(2)}, u32[]{:S(2)}) %collective-permute-start.16) | collective-permute-done | bytes 262176 | tf_op jit(solution)/shard_map/ppermute | solution.py:488
  79.9 0.0 collective-permute-done.17.refs_3_
  79.9 1.1 %assemble.3 = (f32[32,4,2048]{2,1,0:T(4,128)}, f32[32,4,2048]{2,1,0:T(4,128)}) custom-call(f32[256,256]{1,0:T(8,128)S(1)} %get-tuple-element.57.refs_0_, f32[256,256]{1,0:T(8,128)S(1)} %collective-permute-done.15.refs_1_, f32[256,256]{1,0:T(8,128)S(1)} %collective-permute-done.16.refs_2_, ...), custom_call_target="tpu_custom_call", output_to_operand_aliasing={{0}: (4, {}), {1}: (5, {})} | custom-call | bytes 1024 | tf_op jit(solution)/shard_map/assemble/pallas_call | solution.py:444
  (18 shorter events, 0.2 us)
Async XLA Ops:
  0.6 8.1 %copy-start.3 = (s32[4,2048]{1,0:T(4,128)S(1)}, s32[4,2048]{1,0:T(4,128)}, u32[]{:S(2)}) copy-start(s32[4,2048]{1,0:T(4,128)} %label_hbm.3) | copy-start | bytes 98308
  0.6 8.1 %copy-start = (f32[32,4,2048]{2,1,0:T(4,128)S(1)}, f32[32,4,2048]{2,1,0:T(4,128)}, u32[]{:S(2)}) copy-start(f32[32,4,2048]{2,1,0:T(4,128)} %heat_hbm.3) | copy-start | bytes 3145732
  4.2 11.0 %collective-permute-start.2 = (f32[272,256]{1,0:T(8,128)}, f32[272,256]{1,0:T(8,128)S(1)}, u32[]{:S(2)}, u32[]{:S(2)}) collective-permute-start(f32[272,256]{1,0:T(8,128)} %get-tuple-element.38), channel_id=1, source_target_pairs={{0,2},{1,3},{2,0},{3,1},{4,6},{5,7},{6,4},{7,5},{8,10},{9,11},{10,... | collective-permute-start | bytes 835592 | tf_op jit(solution)/shard_map/ppermute | solution.py:488
  7.2 15.1 %collective-permute-start.3 = (f32[272,256]{1,0:T(8,128)}, f32[272,256]{1,0:T(8,128)S(1)}, u32[]{:S(2)}, u32[]{:S(2)}) collective-permute-start(f32[272,256]{1,0:T(8,128)} %get-tuple-element.39), channel_id=1, source_target_pairs={{0,4},{1,5},{2,6},{3,7},{4,0},{5,1},{6,2},{7,3},{8,12},{9,13},{10,... | collective-permute-start | bytes 835592 | tf_op jit(solution)/shard_map/ppermute | solution.py:488
  8.7 14.9 %collective-permute-start.4 = (f32[272,256]{1,0:T(8,128)}, f32[272,256]{1,0:T(8,128)S(1)}, u32[]{:S(2)}, u32[]{:S(2)}) collective-permute-start(f32[272,256]{1,0:T(8,128)} %get-tuple-element.40), channel_id=1, source_target_pairs={{0,6},{1,7},{2,4},{3,5},{4,2},{5,3},{6,0},{7,1},{8,14},{9,15},{10,... | collective-permute-start | bytes 835592 | tf_op jit(solution)/shard_map/ppermute | solution.py:488
  8.7 1.2 %copy-start.1 = (f32[32,4,2048]{2,1,0:T(4,128)S(1)}, f32[32,4,2048]{2,1,0:T(4,128)}, u32[]{:S(2)}) copy-start(f32[32,4,2048]{2,1,0:T(4,128)} %wet_hbm.3) | copy-start | bytes 3145732
  10.0 7.9 %copy-start.2 = (f32[272,256]{1,0:T(8,128)S(1)}, f32[272,256]{1,0:T(8,128)}, u32[]{:S(2)}) copy-start(f32[272,256]{1,0:T(8,128)} %get-tuple-element.37.own) | copy-start | bytes 835588
  10.0 18.3 %copy-start.4 = (f32[128,128]{1,0:T(8,128)S(1)}, f32[128,128]{1,0:T(8,128)}, u32[]{:S(2)}) copy-start(f32[128,128]{1,0:T(8,128)} %thermal_ref.1) | copy-start | bytes 196612
  10.0 18.3 %copy-start.5 = (f32[128,128]{1,0:T(8,128)S(1)}, f32[128,128]{1,0:T(8,128)}, u32[]{:S(2)}) copy-start(f32[128,128]{1,0:T(8,128)} %water_ref.1) | copy-start | bytes 196612
  10.0 18.3 %copy-start.6 = (f32[128,128]{1,0:T(8,128)S(1)}, f32[128,128]{1,0:T(8,128)}, u32[]{:S(2)}) copy-start(f32[128,128]{1,0:T(8,128)} %constant.2.clone.cheb_ref) | copy-start | bytes 196612
  10.0 19.1 %copy-start.7 = (f32[12]{0:T(128)S(1)}, f32[12]{0:T(128)}, u32[]{:S(2)}) copy-start(f32[12]{0:T(128)} %spread_ref.7) | copy-start | bytes 148
  10.0 19.1 %copy-start.8 = (f32[12]{0:T(128)S(1)}, f32[12]{0:T(128)}, u32[]{:S(2)}) copy-start(f32[12]{0:T(128)} %factor_ref.7) | copy-start | bytes 148
  11.7 21.8 %collective-permute-start = (f32[272,256]{1,0:T(8,128)S(1)}, f32[272,256]{1,0:T(8,128)S(1)}, u32[]{:S(2)}, u32[]{:S(2)}) collective-permute-start(f32[272,256]{1,0:T(8,128)S(1)} %get-tuple-element.35), channel_id=1, source_target_pairs={{0,2},{1,3},{2,0},{3,1},{4,6},{5,7},{6,4},{7,5},{8,10},{9,11},{10,... | collective-permute-start | bytes 835592 | tf_op jit(solution)/shard_map/ppermute | solution.py:488
  13.7 19.7 %collective-permute-start.1 = (f32[272,256]{1,0:T(8,128)S(1)}, f32[272,256]{1,0:T(8,128)S(1)}, u32[]{:S(2)}, u32[]{:S(2)}) collective-permute-start(f32[272,256]{1,0:T(8,128)S(1)} %get-tuple-element.36), channel_id=1, source_target_pairs={{0,4},{1,5},{2,6},{3,7},{4,0},{5,1},{6,2},{7,3},{8,12},{9,13},{10,... | collective-permute-start | bytes 835592 | tf_op jit(solution)/shard_map/ppermute | solution.py:488
  15.2 18.2 %collective-permute-start.5 = (f32[272,256]{1,0:T(8,128)S(1)}, f32[272,256]{1,0:T(8,128)S(1)}, u32[]{:S(2)}, u32[]{:S(2)}) collective-permute-start(f32[272,256]{1,0:T(8,128)S(1)} %get-tuple-element.44), channel_id=1, source_target_pairs={{0,6},{1,7},{2,4},{3,5},{4,2},{5,3},{6,0},{7,1},{8,14},{9,15},{10,... | collective-permute-start | bytes 835592 | tf_op jit(solution)/shard_map/ppermute | solution.py:488
  22.3 17.4 %collective-permute-start.9 = (f32[2,272,256]{2,1,0:T(8,128)S(1)}, f32[2,272,256]{2,1,0:T(8,128)S(1)}, u32[]{:S(2)}, u32[]{:S(2)}) collective-permute-start(f32[2,272,256]{2,1,0:T(8,128)S(1)} %pad_maximum_fusion.3), channel_id=1, source_target_pairs={{4,12},{5,13},{6,14},{7,15},{8,0},{9,1},{10,2},{11,3},{12,20},{13,... | collective-permute-start | bytes 1671176 | tf_op jit(solution)/shard_map/ppermute | solution.py:488
  23.7 16.1 %collective-permute-start.10 = (f32[2,272,256]{2,1,0:T(8,128)S(1)}, f32[2,272,256]{2,1,0:T(8,128)S(1)}, u32[]{:S(2)}, u32[]{:S(2)}) collective-permute-start(f32[2,272,256]{2,1,0:T(8,128)S(1)} %pad_maximum_fusion.4), channel_id=1, source_target_pairs={{0,8},{1,9},{2,10},{3,11},{8,16},{9,17},{10,18},{11,19},{12,4},{13... | collective-permute-start | bytes 1671176 | tf_op jit(solution)/shard_map/ppermute | solution.py:488
  33.5 16.7 %collective-permute-start.8 = (f32[816,256]{1,0:T(8,128)S(1)}, f32[816,256]{1,0:T(8,128)S(1)}, u32[]{:S(2)}, u32[]{:S(2)}) collective-permute-start(f32[816,256]{1,0:T(8,128)S(1)} %pad_maximum_fusion), channel_id=1, source_target_pairs={{0,1},{1,0},{2,3},{3,2},{4,5},{5,4},{6,7},{7,6},{8,9},{9,8},{10,11... | collective-permute-start | bytes 2506760 | tf_op jit(solution)/shard_map/ppermute | solution.py:488
  33.6 21.8 %collective-permute-start.6 = (f32[2,272,256]{2,1,0:T(8,128)S(1)}, f32[2,272,256]{2,1,0:T(8,128)S(1)}, u32[]{:S(2)}, u32[]{:S(2)}) collective-permute-start(f32[2,272,256]{2,1,0:T(8,128)S(1)} %pad_maximum_fusion.1), channel_id=1, source_target_pairs={{4,12},{5,13},{6,14},{7,15},{8,0},{9,1},{10,2},{11,3},{12,20},{13,... | collective-permute-start | bytes 1671176 | tf_op jit(solution)/shard_map/ppermute | solution.py:488
  35.0 20.5 %collective-permute-start.7 = (f32[2,272,256]{2,1,0:T(8,128)S(1)}, f32[2,272,256]{2,1,0:T(8,128)S(1)}, u32[]{:S(2)}, u32[]{:S(2)}) collective-permute-start(f32[2,272,256]{2,1,0:T(8,128)S(1)} %pad_maximum_fusion.2), channel_id=1, source_target_pairs={{0,8},{1,9},{2,10},{3,11},{8,16},{9,17},{10,18},{11,19},{12,4},{13... | collective-permute-start | bytes 1671176 | tf_op jit(solution)/shard_map/ppermute | solution.py:488
  45.1 2.0 %collective-permute-start.11 = (f32[2,4,64,256]{3,2,1,0:T(8,128)S(1)}, f32[2,4,64,256]{3,2,1,0:T(8,128)S(1)}, u32[]{:S(2)}, u32[]{:S(2)}) collective-permute-start(f32[2,4,64,256]{3,2,1,0:T(8,128)S(1)} %get-tuple-element.49.refs_0_), channel_id=1, source_target_pairs={{0,1},{1,0},{2,3},{3,2},{4,5},{5,4},{6,7},{7,6},{8,9},{9,8},{10,11... | collective-permute-start | bytes 1572872 | tf_op jit(solution)/shard_map/ppermute | solution.py:488
  45.2 2.6 %collective-permute-start.12 = (f32[2,4,64,256]{3,2,1,0:T(8,128)S(1)}, f32[2,4,64,256]{3,2,1,0:T(8,128)S(1)}, u32[]{:S(2)}, u32[]{:S(2)}) collective-permute-start(f32[2,4,64,256]{3,2,1,0:T(8,128)S(1)} %get-tuple-element.50.refs_1_), channel_id=1, source_target_pairs={{0,1},{1,0},{2,3},{3,2},{4,5},{5,4},{6,7},{7,6},{8,9},{9,8},{10,11... | collective-permute-start | bytes 1572872 | tf_op jit(solution)/shard_map/ppermute | solution.py:488
  48.8 12.5 %collective-permute-start.18 = (f32[256,256]{1,0:T(8,128)S(1)}, f32[256,256]{1,0:T(8,128)S(1)}, u32[]{:S(2)}, u32[]{:S(2)}) collective-permute-start(f32[256,256]{1,0:T(8,128)S(1)} %get-tuple-element.61), channel_id=1, source_target_pairs={{0,2},{1,3},{2,0},{3,1},{4,6},{5,7},{6,4},{7,5},{8,10},{9,11},{10,... | collective-permute-start | bytes 786440 | tf_op jit(solution)/shard_map/ppermute | solution.py:488
  50.1 13.7 %collective-permute-start.19 = (f32[256,256]{1,0:T(8,128)S(1)}, f32[256,256]{1,0:T(8,128)S(1)}, u32[]{:S(2)}, u32[]{:S(2)}) collective-permute-start(f32[256,256]{1,0:T(8,128)S(1)} %get-tuple-element.62), channel_id=1, source_target_pairs={{0,4},{1,5},{2,6},{3,7},{4,0},{5,1},{6,2},{7,3},{8,12},{9,13},{10,... | collective-permute-start | bytes 786440 | tf_op jit(solution)/shard_map/ppermute | solution.py:488
  50.2 13.7 %collective-permute-start.20 = (f32[256,256]{1,0:T(8,128)S(1)}, f32[256,256]{1,0:T(8,128)S(1)}, u32[]{:S(2)}, u32[]{:S(2)}) collective-permute-start(f32[256,256]{1,0:T(8,128)S(1)} %get-tuple-element.63), channel_id=1, source_target_pairs={{0,6},{1,7},{2,4},{3,5},{4,2},{5,3},{6,0},{7,1},{8,14},{9,15},{10,... | collective-permute-start | bytes 786440 | tf_op jit(solution)/shard_map/ppermute | solution.py:488
  60.8 3.2 %collective-permute-start.13 = (f32[2,4,64,256]{3,2,1,0:T(8,128)S(1)}, f32[2,4,64,256]{3,2,1,0:T(8,128)S(1)}, u32[]{:S(2)}, u32[]{:S(2)}) collective-permute-start(f32[2,4,64,256]{3,2,1,0:T(8,128)S(1)} %get-tuple-element.54.refs_0_), channel_id=1, source_target_pairs={{0,1},{1,0},{2,3},{3,2},{4,5},{5,4},{6,7},{7,6},{8,9},{9,8},{10,11... | collective-permute-start | bytes 1572872 | tf_op jit(solution)/shard_map/ppermute | solution.py:488
  60.8 3.2 %collective-permute-start.14 = (f32[2,4,64,256]{3,2,1,0:T(8,128)S(1)}, f32[2,4,64,256]{3,2,1,0:T(8,128)S(1)}, u32[]{:S(2)}, u32[]{:S(2)}) collective-permute-start(f32[2,4,64,256]{3,2,1,0:T(8,128)S(1)} %get-tuple-element.55.refs_1_), channel_id=1, source_target_pairs={{0,1},{1,0},{2,3},{3,2},{4,5},{5,4},{6,7},{7,6},{8,9},{9,8},{10,11... | collective-permute-start | bytes 1572872 | tf_op jit(solution)/shard_map/ppermute | solution.py:488
  63.9 5.7 %collective-permute-start.21 = (f32[408,256]{1,0:T(8,128)S(1)}, f32[408,256]{1,0:T(8,128)S(1)}, u32[]{:S(2)}, u32[]{:S(2)}) collective-permute-start(f32[408,256]{1,0:T(8,128)S(1)} %pad_maximum_fusion.5), channel_id=1, source_target_pairs={{0,1},{1,0},{2,3},{3,2},{4,5},{5,4},{6,7},{7,6},{8,9},{9,8},{10,11... | collective-permute-start | bytes 1253384 | tf_op jit(solution)/shard_map/ppermute | solution.py:488
  65.0 9.2 %collective-permute-start.15 = (f32[256,256]{1,0:T(8,128)S(1)}, f32[256,256]{1,0:T(8,128)S(1)}, u32[]{:S(2)}, u32[]{:S(2)}) collective-permute-start(f32[256,256]{1,0:T(8,128)S(1)} %get-tuple-element.58), channel_id=1, source_target_pairs={{0,2},{1,3},{2,0},{3,1},{4,6},{5,7},{6,4},{7,5},{8,10},{9,11},{10,... | collective-permute-start | bytes 786440 | tf_op jit(solution)/shard_map/ppermute | solution.py:488
  65.8 14.0 %collective-permute-start.16 = (f32[256,256]{1,0:T(8,128)S(1)}, f32[256,256]{1,0:T(8,128)S(1)}, u32[]{:S(2)}, u32[]{:S(2)}) collective-permute-start(f32[256,256]{1,0:T(8,128)S(1)} %get-tuple-element.59), channel_id=1, source_target_pairs={{0,4},{1,5},{2,6},{3,7},{4,0},{5,1},{6,2},{7,3},{8,12},{9,13},{10,... | collective-permute-start | bytes 786440 | tf_op jit(solution)/shard_map/ppermute | solution.py:488
  66.8 13.1 %collective-permute-start.17 = (f32[256,256]{1,0:T(8,128)S(1)}, f32[256,256]{1,0:T(8,128)S(1)}, u32[]{:S(2)}, u32[]{:S(2)}) collective-permute-start(f32[256,256]{1,0:T(8,128)S(1)} %get-tuple-element.60), channel_id=1, source_target_pairs={{0,6},{1,7},{2,4},{3,5},{4,2},{5,3},{6,0},{7,1},{8,14},{9,15},{10,... | collective-permute-start | bytes 786440 | tf_op jit(solution)/shard_map/ppermute | solution.py:488

commit v4 on v3

--- a/solution.py
+++ b/solution.py
@@ -490,6 +490,8 @@
     received = []
     for k, width in enumerate(widths):
         own, bx, by, bxy = pack(k, width, heat, wet, label)
+        if k:
+            bxy = lax.optimization_barrier((bxy, received[k - 1][2]))[0]
         received.append((own, send(bx, "x"), send(by, "y"), send(bxy, "xy")))
     stack_w, stack_h = prep(thermal, water)
     outs = []

time: 81.4 us -> 81.2 us (level)
  starting transfers between devices: 31.1 us -> 30 us
  waiting for transfers between devices: 20.6 us -> 21.5 us
    ppermute x22, starting transfers between devices: 31.1 us -> 30 us  [send(): return lax.ppermute(array, JOINT, route[name])]
    ppermute x22, waiting for transfers between devices: 20.6 us -> 21.5 us  [send(): return lax.ppermute(array, JOINT, route[name])]
where the time goes in v4:
time: 81.2 us; the launch traced here: 81 us
  starting transfers between devices  30 us (37%)
  Pallas kernels  26.7 us (33%)
  waiting for transfers between devices  21.5 us (26%)
  local copies, waits for them, and re-layouts  1.29 us (2%)
  between operations  1.14 us (1%)
    ppermute x22, starting transfers between devices, send(): return lax.ppermute(array, JOINT, route[name])  30 us
    ppermute x22, waiting for transfers between devices, send(): return lax.ppermute(array, JOINT, route[name])  21.5 us
    pallas_call x2, Pallas kernels, stencil(): pl.pallas_call(functools.partial(stencil_kernel, width), out_shape=[jax.S...  10.7 us
    pallas_call x2, Pallas kernels, pre(): pl.pallas_call(functools.partial(pre_kernel, width), out_shape=[jax.Shape...  6.04 us
    pallas_call x2, Pallas kernels, pack(): pl.pallas_call(functools.partial(pack_kernel, k, width), out_shape=[shape...  5.19 us
    pallas_call x2, Pallas kernels, assemble(): pl.pallas_call(functools.partial(assemble_kernel, k, width), out_shape=[s...  2.14 us
    pallas_call x2, Pallas kernels, solve(): pl.pallas_call(solve_kernel, out_shape=[shape] * 4, in_specs=[pl.BlockSpe...  1.98 us
  transfers between devices with their start and end apart: 22, of which 7 were waited for; matrix products, arithmetic and copies ran while one was open for 0% of the time, Pallas kernels for 27%

profile of v4, /device:TPU:0, one launch (start us, length us, event | category | flops | bytes accessed | tf_op | source)
XLA Modules:
  0.0 81.0 jit_solution(16264218753953997476)
XLA Ops:
  0.6 0.0 copy-start.3
  0.6 0.0 copy-start
  0.6 3.5 %pack.3 = (f32[272,256]{1,0:T(8,128)}, f32[272,256]{1,0:T(8,128)}, f32[272,256]{1,0:T(8,128)}, f32[272,256]{1,0:T(8,128)}) custom-call(f32[32,4,2048]{2,1,0:T(4,128)} %heat_hbm.3, f32[32,4,2048]{2,1,0:T(4,128)} %wet_hbm.3, s32[4,2048]{1,0:T(4,128)} %label_hbm.3), custom_call_target="tpu_custom_call" | custom-call | bytes 1024 | tf_op jit(solution)/shard_map/pack/pallas_call | solution.py:157
  4.2 3.0 %collective-permute-start.3 = (f32[272,256]{1,0:T(8,128)}, f32[272,256]{1,0:T(8,128)S(1)}, u32[]{:S(2)}, u32[]{:S(2)}) collective-permute-start(f32[272,256]{1,0:T(8,128)} %get-tuple-element.40), channel_id=1, source_target_pairs={{0,4},{1,5},{2,6},{3,7},{4,0},{5,1},{6,2},{7,3},{8,12},{9,13},{10,... | collective-permute-start | bytes 835592 | tf_op jit(solution)/shard_map/ppermute | solution.py:488
  7.2 1.5 %collective-permute-start.2 = (f32[272,256]{1,0:T(8,128)}, f32[272,256]{1,0:T(8,128)S(1)}, u32[]{:S(2)}, u32[]{:S(2)}) collective-permute-start(f32[272,256]{1,0:T(8,128)} %get-tuple-element.39), channel_id=1, source_target_pairs={{0,2},{1,3},{2,0},{3,1},{4,6},{5,7},{6,4},{7,5},{8,10},{9,11},{10,... | collective-permute-start | bytes 835592 | tf_op jit(solution)/shard_map/ppermute | solution.py:488
  8.7 0.1 collective-permute-start.4
  8.8 0.0 copy-done.3
  8.8 0.0 copy-done
  8.8 1.2 %copy-done.1 = f32[32,4,2048]{2,1,0:T(4,128)S(1)} copy-done((f32[32,4,2048]{2,1,0:T(4,128)S(1)}, f32[32,4,2048]{2,1,0:T(4,128)}, u32[]{:S(2)}) %copy-start.1) | copy-done | bytes 1048600
  10.0 0.0 copy-start.7
  10.0 0.0 copy-start.8
  10.0 1.7 %pack.2 = (f32[272,256]{1,0:T(8,128)S(1)}, f32[272,256]{1,0:T(8,128)S(1)}, f32[272,256]{1,0:T(8,128)S(1)}, f32[272,256]{1,0:T(8,128)S(1)}) custom-call(f32[32,4,2048]{2,1,0:T(4,128)S(1)} %copy-done, f32[32,4,2048]{2,1,0:T(4,128)S(1)} %copy-done.1, s32[4,2048]{1,0:T(4,128)S(1)} %copy-done.3), custom_call_target="tpu_custom_call" | custom-call | bytes 1024 | tf_op jit(solution)/shard_map/pack/pallas_call | solution.py:157
  11.7 2.0 %collective-permute-start = (f32[272,256]{1,0:T(8,128)S(1)}, f32[272,256]{1,0:T(8,128)S(1)}, u32[]{:S(2)}, u32[]{:S(2)}) collective-permute-start(f32[272,256]{1,0:T(8,128)S(1)} %get-tuple-element.36), channel_id=1, source_target_pairs={{0,2},{1,3},{2,0},{3,1},{4,6},{5,7},{6,4},{7,5},{8,10},{9,11},{10,... | collective-permute-start | bytes 835592 | tf_op jit(solution)/shard_map/ppermute | solution.py:488
  13.7 1.5 %collective-permute-start.1 = (f32[272,256]{1,0:T(8,128)S(1)}, f32[272,256]{1,0:T(8,128)S(1)}, u32[]{:S(2)}, u32[]{:S(2)}) collective-permute-start(f32[272,256]{1,0:T(8,128)S(1)} %get-tuple-element.37), channel_id=1, source_target_pairs={{0,4},{1,5},{2,6},{3,7},{4,0},{5,1},{6,2},{7,3},{8,12},{9,13},{10,... | collective-permute-start | bytes 835592 | tf_op jit(solution)/shard_map/ppermute | solution.py:488
  15.2 0.0 collective-permute-done.3.ry
  15.2 2.2 %collective-permute-start.5 = (f32[272,256]{1,0:T(8,128)S(1)}, f32[272,256]{1,0:T(8,128)S(1)}, u32[]{:S(2)}, u32[]{:S(2)}) collective-permute-start(f32[272,256]{1,0:T(8,128)S(1)} %get-tuple-element.46), channel_id=1, source_target_pairs={{0,6},{1,7},{2,4},{3,5},{4,2},{5,3},{6,0},{7,1},{8,14},{9,15},{10,... | collective-permute-start | bytes 835592 | tf_op jit(solution)/shard_map/ppermute | solution.py:488
  17.4 0.0 collective-permute-done.2.rx
  17.4 0.0 copy-done.2
  17.5 1.3 %collective-permute-start.9 = (f32[2,272,256]{2,1,0:T(8,128)S(1)}, f32[2,272,256]{2,1,0:T(8,128)S(1)}, u32[]{:S(2)}, u32[]{:S(2)}) collective-permute-start(f32[2,272,256]{2,1,0:T(8,128)S(1)} %pad_maximum_fusion.3), channel_id=1, source_target_pairs={{4,12},{5,13},{6,14},{7,15},{8,0},{9,1},{10,2},{11,3},{12,20},{13,... | collective-permute-start | bytes 1671176 | tf_op jit(solution)/shard_map/ppermute | solution.py:488
  18.8 3.7 %collective-permute-done.4.rxy = f32[272,256]{1,0:T(8,128)S(1)} collective-permute-done((f32[272,256]{1,0:T(8,128)}, f32[272,256]{1,0:T(8,128)S(1)}, u32[]{:S(2)}, u32[]{:S(2)}) %collective-permute-start.4) | collective-permute-done | bytes 278560 | tf_op jit(solution)/shard_map/ppermute | solution.py:488
  22.5 4.0 %collective-permute-start.10 = (f32[2,272,256]{2,1,0:T(8,128)S(1)}, f32[2,272,256]{2,1,0:T(8,128)S(1)}, u32[]{:S(2)}, u32[]{:S(2)}) collective-permute-start(f32[2,272,256]{2,1,0:T(8,128)S(1)} %pad_maximum_fusion.4), channel_id=1, source_target_pairs={{0,8},{1,9},{2,10},{3,11},{8,16},{9,17},{10,18},{11,19},{12,4},{13... | collective-permute-start | bytes 1671176 | tf_op jit(solution)/shard_map/ppermute | solution.py:488
  26.6 0.7 prep.1
  27.3 3.0 %inner_substeps.2 = (f32[10,2,64,384]{3,2,1,0:T(8,128)S(1)}, f32[2,8,384]{2,1,0:T(8,128)S(1)}, f32[8,256]{1,0:T(8,128)S(1)}) custom-call(f32[272,256]{1,0:T(8,128)S(1)} %copy-done.2, f32[272,256]{1,0:T(8,128)S(1)} %collective-permute-done.2.rx, f32[272,256]{1,0:T(8,128)S(1)} %collective-permute-done.3.ry, f32[272,256]{1,0:T(8,128)S(1)} %collective-permute-done.4.rxy, ...), custom_call_target="tpu_custom_call" | custom-call | bytes 1024 | tf_op jit(solution)/shard_map/inner_substeps/pallas_call | solution.py:309
  30.3 0.0 collective-permute-done.1.ry
  30.3 0.0 collective-permute-done.rx
  30.4 2.9 %collective-permute-done.5.rxy = f32[272,256]{1,0:T(8,128)S(1)} collective-permute-done((f32[272,256]{1,0:T(8,128)S(1)}, f32[272,256]{1,0:T(8,128)S(1)}, u32[]{:S(2)}, u32[]{:S(2)}) %collective-permute-start.5) | collective-permute-done | bytes 278560 | tf_op jit(solution)/shard_map/ppermute | solution.py:488
  33.3 0.1 pad_maximum_fusion
  33.3 0.1 collective-permute-start.8
  33.5 1.3 %collective-permute-start.6 = (f32[2,272,256]{2,1,0:T(8,128)S(1)}, f32[2,272,256]{2,1,0:T(8,128)S(1)}, u32[]{:S(2)}, u32[]{:S(2)}) collective-permute-start(f32[2,272,256]{2,1,0:T(8,128)S(1)} %pad_maximum_fusion.1), channel_id=1, source_target_pairs={{4,12},{5,13},{6,14},{7,15},{8,0},{9,1},{10,2},{11,3},{12,20},{13,... | collective-permute-start | bytes 1671176 | tf_op jit(solution)/shard_map/ppermute | solution.py:488
  34.8 4.8 %collective-permute-start.7 = (f32[2,272,256]{2,1,0:T(8,128)S(1)}, f32[2,272,256]{2,1,0:T(8,128)S(1)}, u32[]{:S(2)}, u32[]{:S(2)}) collective-permute-start(f32[2,272,256]{2,1,0:T(8,128)S(1)} %pad_maximum_fusion.2), channel_id=1, source_target_pairs={{0,8},{1,9},{2,10},{3,11},{8,16},{9,17},{10,18},{11,19},{12,4},{13... | collective-permute-start | bytes 1671176 | tf_op jit(solution)/shard_map/ppermute | solution.py:488
  39.6 0.0 collective-permute-done.9.p1
  39.6 0.0 collective-permute-done.10.p2
  39.6 5.3 %outer_substeps.2 = (f32[2,4,64,256]{3,2,1,0:T(8,128)S(1)}, f32[2,4,64,256]{3,2,1,0:T(8,128)S(1)}) custom-call(f32[272,256]{1,0:T(8,128)S(1)} %copy-done.2, f32[272,256]{1,0:T(8,128)S(1)} %collective-permute-done.2.rx, f32[272,256]{1,0:T(8,128)S(1)} %collective-permute-done.3.ry, f32[272,256]{1,0:T(8,128)S(1)} %collective-permute-done.4.rxy, ...), custom_call_target="tpu_custom_call" | custom-call | bytes 1024 | tf_op jit(solution)/shard_map/outer_substeps/pallas_call | solution.py:362
  44.9 0.1 collective-permute-start.11
  45.0 0.5 collective-permute-start.12
  45.5 1.4 %collective-permute-done.11.refs_2_ = f32[2,4,64,256]{3,2,1,0:T(8,128)S(1)} collective-permute-done((f32[2,4,64,256]{3,2,1,0:T(8,128)S(1)}, f32[2,4,64,256]{3,2,1,0:T(8,128)S(1)}, u32[]{:S(2)}, u32[]{:S(2)}) %collective-permute-start.11) | collective-permute-done | bytes 524320 | tf_op jit(solution)/shard_map/ppermute | solution.py:488
  46.9 0.7 collective-permute-done.12.refs_3_
  47.7 1.0 %solve.2 = (f32[256,256]{1,0:T(8,128)S(1)}, f32[256,256]{1,0:T(8,128)S(1)}, f32[256,256]{1,0:T(8,128)S(1)}, f32[256,256]{1,0:T(8,128)S(1)}) custom-call(f32[2,4,64,256]{3,2,1,0:T(8,128)S(1)} %get-tuple-element.51.refs_0_, f32[2,4,64,256]{3,2,1,0:T(8,128)S(1)} %get-tuple-element.52.refs_1_, f32[2,4,64,256]{3,2,1,0:T(8,128)S(1)} %collective-permute-done.11.refs_2_, ...), custom_call_target="tpu_custom_call" | custom-call | bytes 1024 | tf_op jit(solution)/shard_map/solve/pallas_call | solution.py:410
  48.7 1.7 %collective-permute-start.18 = (f32[256,256]{1,0:T(8,128)S(1)}, f32[256,256]{1,0:T(8,128)S(1)}, u32[]{:S(2)}, u32[]{:S(2)}) collective-permute-start(f32[256,256]{1,0:T(8,128)S(1)} %get-tuple-element.63), channel_id=1, source_target_pairs={{0,2},{1,3},{2,0},{3,1},{4,6},{5,7},{6,4},{7,5},{8,10},{9,11},{10,... | collective-permute-start | bytes 786440 | tf_op jit(solution)/shard_map/ppermute | solution.py:488
  50.4 0.5 collective-permute-start.19
  50.8 0.0 collective-permute-done.8._
  50.8 1.4 %collective-permute-start.20 = (f32[256,256]{1,0:T(8,128)S(1)}, f32[256,256]{1,0:T(8,128)S(1)}, u32[]{:S(2)}, u32[]{:S(2)}) collective-permute-start(f32[256,256]{1,0:T(8,128)S(1)} %get-tuple-element.65), channel_id=1, source_target_pairs={{0,6},{1,7},{2,4},{3,5},{4,2},{5,3},{6,0},{7,1},{8,14},{9,15},{10,... | collective-permute-start | bytes 786440 | tf_op jit(solution)/shard_map/ppermute | solution.py:488
  52.2 3.0 %inner_substeps.3 = (f32[10,2,64,384]{3,2,1,0:T(8,128)S(1)}, f32[2,8,384]{2,1,0:T(8,128)S(1)}, f32[8,256]{1,0:T(8,128)S(1)}) custom-call(f32[272,256]{1,0:T(8,128)S(1)} %get-tuple-element.35.own, f32[272,256]{1,0:T(8,128)S(1)} %collective-permute-done.rx, f32[272,256]{1,0:T(8,128)S(1)} %collective-permute-done.1.ry, ...), custom_call_target="tpu_custom_call" | custom-call | bytes 1024 | tf_op jit(solution)/shard_map/inner_substeps/pallas_call | solution.py:309
  55.2 0.0 collective-permute-done.6.p1
  55.3 0.0 collective-permute-done.7.p2
  55.3 5.3 %outer_substeps.3 = (f32[2,4,64,256]{3,2,1,0:T(8,128)S(1)}, f32[2,4,64,256]{3,2,1,0:T(8,128)S(1)}) custom-call(f32[272,256]{1,0:T(8,128)S(1)} %get-tuple-element.35.own, f32[272,256]{1,0:T(8,128)S(1)} %collective-permute-done.rx, f32[272,256]{1,0:T(8,128)S(1)} %collective-permute-done.1.ry, f32[272,256]{1,0:T(8,128)S(1)} %collective-permute-done.5.rxy, ...), custom_call_target="tpu_custom_call" | custom-call | bytes 1024 | tf_op jit(solution)/shard_map/outer_substeps/pallas_call | solution.py:362
  60.6 0.1 collective-permute-start.13
  60.7 0.5 collective-permute-start.14
  61.2 0.0 collective-permute-done.18.refs_1_
  61.2 2.9 %collective-permute-done.19.refs_2_ = f32[256,256]{1,0:T(8,128)S(1)} collective-permute-done((f32[256,256]{1,0:T(8,128)S(1)}, f32[256,256]{1,0:T(8,128)S(1)}, u32[]{:S(2)}, u32[]{:S(2)}) %collective-permute-start.19) | collective-permute-done | bytes 262176 | tf_op jit(solution)/shard_map/ppermute | solution.py:488
  64.1 0.0 collective-permute-done.20.refs_3_
  64.2 0.1 collective-permute-start.21
  64.2 0.0 collective-permute-done.13.refs_2_
  64.2 0.0 collective-permute-done.14.refs_3_
  64.3 1.0 %solve.3 = (f32[256,256]{1,0:T(8,128)S(1)}, f32[256,256]{1,0:T(8,128)S(1)}, f32[256,256]{1,0:T(8,128)S(1)}, f32[256,256]{1,0:T(8,128)S(1)}) custom-call(f32[2,4,64,256]{3,2,1,0:T(8,128)S(1)} %get-tuple-element.56.refs_0_, f32[2,4,64,256]{3,2,1,0:T(8,128)S(1)} %get-tuple-element.57.refs_1_, f32[2,4,64,256]{3,2,1,0:T(8,128)S(1)} %collective-permute-done.13.refs_2_, ...), custom_call_target="tpu_custom_call" | custom-call | bytes 1024 | tf_op jit(solution)/shard_map/solve/pallas_call | solution.py:410
  65.3 0.8 collective-permute-start.15
  66.0 1.0 %collective-permute-start.16 = (f32[256,256]{1,0:T(8,128)S(1)}, f32[256,256]{1,0:T(8,128)S(1)}, u32[]{:S(2)}, u32[]{:S(2)}) collective-permute-start(f32[256,256]{1,0:T(8,128)S(1)} %get-tuple-element.61), channel_id=1, source_target_pairs={{0,4},{1,5},{2,6},{3,7},{4,0},{5,1},{6,2},{7,3},{8,12},{9,13},{10,... | collective-permute-start | bytes 786440 | tf_op jit(solution)/shard_map/ppermute | solution.py:488
  67.0 1.8 %collective-permute-start.17 = (f32[256,256]{1,0:T(8,128)S(1)}, f32[256,256]{1,0:T(8,128)S(1)}, u32[]{:S(2)}, u32[]{:S(2)}) collective-permute-start(f32[256,256]{1,0:T(8,128)S(1)} %get-tuple-element.62), channel_id=1, source_target_pairs={{0,6},{1,7},{2,4},{3,5},{4,2},{5,3},{6,0},{7,1},{8,14},{9,15},{10,... | collective-permute-start | bytes 786440 | tf_op jit(solution)/shard_map/ppermute | solution.py:488
  68.8 1.1 %assemble.2 = (f32[32,4,2048]{2,1,0:T(4,128)}, f32[32,4,2048]{2,1,0:T(4,128)}) custom-call(f32[256,256]{1,0:T(8,128)S(1)} %get-tuple-element.54.refs_0_, f32[256,256]{1,0:T(8,128)S(1)} %collective-permute-done.18.refs_1_, f32[256,256]{1,0:T(8,128)S(1)} %collective-permute-done.19.refs_2_, f32[256,256]{1,0:T(8,128)S(1)} %collective-permute-done.20.refs_3_), custom_call_target="tpu_custom_call" | custom-call | bytes 1024 | tf_op jit(solution)/shard_map/assemble/pallas_call | solution.py:444
  69.9 0.0 collective-permute-done.21.refs_6_
  69.9 4.5 %collective-permute-done.15.refs_1_ = f32[256,256]{1,0:T(8,128)S(1)} collective-permute-done((f32[256,256]{1,0:T(8,128)S(1)}, f32[256,256]{1,0:T(8,128)S(1)}, u32[]{:S(2)}, u32[]{:S(2)}) %collective-permute-start.15) | collective-permute-done | bytes 262176 | tf_op jit(solution)/shard_map/ppermute | solution.py:488
  74.4 5.3 %collective-permute-done.16.refs_2_ = f32[256,256]{1,0:T(8,128)S(1)} collective-permute-done((f32[256,256]{1,0:T(8,128)S(1)}, f32[256,256]{1,0:T(8,128)S(1)}, u32[]{:S(2)}, u32[]{:S(2)}) %collective-permute-start.16) | collective-permute-done | bytes 262176 | tf_op jit(solution)/shard_map/ppermute | solution.py:488
  79.7 0.0 collective-permute-done.17.refs_3_
  79.7 1.1 %assemble.3 = (f32[32,4,2048]{2,1,0:T(4,128)}, f32[32,4,2048]{2,1,0:T(4,128)}) custom-call(f32[256,256]{1,0:T(8,128)S(1)} %get-tuple-element.59.refs_0_, f32[256,256]{1,0:T(8,128)S(1)} %collective-permute-done.15.refs_1_, f32[256,256]{1,0:T(8,128)S(1)} %collective-permute-done.16.refs_2_, ...), custom_call_target="tpu_custom_call", output_to_operand_aliasing={{0}: (4, {}), {1}: (5, {})} | custom-call | bytes 1024 | tf_op jit(solution)/shard_map/assemble/pallas_call | solution.py:444
  (18 shorter events, 0.2 us)
Async XLA Ops:
  0.6 8.1 %copy-start.3 = (s32[4,2048]{1,0:T(4,128)S(1)}, s32[4,2048]{1,0:T(4,128)}, u32[]{:S(2)}) copy-start(s32[4,2048]{1,0:T(4,128)} %label_hbm.3) | copy-start | bytes 98308
  0.6 8.1 %copy-start = (f32[32,4,2048]{2,1,0:T(4,128)S(1)}, f32[32,4,2048]{2,1,0:T(4,128)}, u32[]{:S(2)}) copy-start(f32[32,4,2048]{2,1,0:T(4,128)} %heat_hbm.3) | copy-start | bytes 3145732
  4.2 11.0 %collective-permute-start.3 = (f32[272,256]{1,0:T(8,128)}, f32[272,256]{1,0:T(8,128)S(1)}, u32[]{:S(2)}, u32[]{:S(2)}) collective-permute-start(f32[272,256]{1,0:T(8,128)} %get-tuple-element.40), channel_id=1, source_target_pairs={{0,4},{1,5},{2,6},{3,7},{4,0},{5,1},{6,2},{7,3},{8,12},{9,13},{10,... | collective-permute-start | bytes 835592 | tf_op jit(solution)/shard_map/ppermute | solution.py:488
  7.2 10.2 %collective-permute-start.2 = (f32[272,256]{1,0:T(8,128)}, f32[272,256]{1,0:T(8,128)S(1)}, u32[]{:S(2)}, u32[]{:S(2)}) collective-permute-start(f32[272,256]{1,0:T(8,128)} %get-tuple-element.39), channel_id=1, source_target_pairs={{0,2},{1,3},{2,0},{3,1},{4,6},{5,7},{6,4},{7,5},{8,10},{9,11},{10,... | collective-permute-start | bytes 835592 | tf_op jit(solution)/shard_map/ppermute | solution.py:488
  8.7 13.8 %collective-permute-start.4 = (f32[272,256]{1,0:T(8,128)}, f32[272,256]{1,0:T(8,128)S(1)}, u32[]{:S(2)}, u32[]{:S(2)}) collective-permute-start(f32[272,256]{1,0:T(8,128)} %get-tuple-element.41), channel_id=1, source_target_pairs={{0,6},{1,7},{2,4},{3,5},{4,2},{5,3},{6,0},{7,1},{8,14},{9,15},{10,... | collective-permute-start | bytes 835592 | tf_op jit(solution)/shard_map/ppermute | solution.py:488
  8.8 1.2 %copy-start.1 = (f32[32,4,2048]{2,1,0:T(4,128)S(1)}, f32[32,4,2048]{2,1,0:T(4,128)}, u32[]{:S(2)}) copy-start(f32[32,4,2048]{2,1,0:T(4,128)} %wet_hbm.3) | copy-start | bytes 3145732
  10.0 7.5 %copy-start.2 = (f32[272,256]{1,0:T(8,128)S(1)}, f32[272,256]{1,0:T(8,128)}, u32[]{:S(2)}) copy-start(f32[272,256]{1,0:T(8,128)} %get-tuple-element.38.own) | copy-start | bytes 835588
  10.0 16.5 %copy-start.4 = (f32[128,128]{1,0:T(8,128)S(1)}, f32[128,128]{1,0:T(8,128)}, u32[]{:S(2)}) copy-start(f32[128,128]{1,0:T(8,128)} %thermal_ref.1) | copy-start | bytes 196612
  10.0 16.5 %copy-start.5 = (f32[128,128]{1,0:T(8,128)S(1)}, f32[128,128]{1,0:T(8,128)}, u32[]{:S(2)}) copy-start(f32[128,128]{1,0:T(8,128)} %water_ref.1) | copy-start | bytes 196612
  10.0 16.5 %copy-start.6 = (f32[128,128]{1,0:T(8,128)S(1)}, f32[128,128]{1,0:T(8,128)}, u32[]{:S(2)}) copy-start(f32[128,128]{1,0:T(8,128)} %constant.2.clone.cheb_ref) | copy-start | bytes 196612
  10.0 17.3 %copy-start.7 = (f32[12]{0:T(128)S(1)}, f32[12]{0:T(128)}, u32[]{:S(2)}) copy-start(f32[12]{0:T(128)} %spread_ref.7) | copy-start | bytes 148
  10.0 17.3 %copy-start.8 = (f32[12]{0:T(128)S(1)}, f32[12]{0:T(128)}, u32[]{:S(2)}) copy-start(f32[12]{0:T(128)} %factor_ref.7) | copy-start | bytes 148
  11.7 18.6 %collective-permute-start = (f32[272,256]{1,0:T(8,128)S(1)}, f32[272,256]{1,0:T(8,128)S(1)}, u32[]{:S(2)}, u32[]{:S(2)}) collective-permute-start(f32[272,256]{1,0:T(8,128)S(1)} %get-tuple-element.36), channel_id=1, source_target_pairs={{0,2},{1,3},{2,0},{3,1},{4,6},{5,7},{6,4},{7,5},{8,10},{9,11},{10,... | collective-permute-start | bytes 835592 | tf_op jit(solution)/shard_map/ppermute | solution.py:488
  13.7 16.6 %collective-permute-start.1 = (f32[272,256]{1,0:T(8,128)S(1)}, f32[272,256]{1,0:T(8,128)S(1)}, u32[]{:S(2)}, u32[]{:S(2)}) collective-permute-start(f32[272,256]{1,0:T(8,128)S(1)} %get-tuple-element.37), channel_id=1, source_target_pairs={{0,4},{1,5},{2,6},{3,7},{4,0},{5,1},{6,2},{7,3},{8,12},{9,13},{10,... | collective-permute-start | bytes 835592 | tf_op jit(solution)/shard_map/ppermute | solution.py:488
  15.2 18.1 %collective-permute-start.5 = (f32[272,256]{1,0:T(8,128)S(1)}, f32[272,256]{1,0:T(8,128)S(1)}, u32[]{:S(2)}, u32[]{:S(2)}) collective-permute-start(f32[272,256]{1,0:T(8,128)S(1)} %get-tuple-element.46), channel_id=1, source_target_pairs={{0,6},{1,7},{2,4},{3,5},{4,2},{5,3},{6,0},{7,1},{8,14},{9,15},{10,... | collective-permute-start | bytes 835592 | tf_op jit(solution)/shard_map/ppermute | solution.py:488
  17.5 22.1 %collective-permute-start.9 = (f32[2,272,256]{2,1,0:T(8,128)S(1)}, f32[2,272,256]{2,1,0:T(8,128)S(1)}, u32[]{:S(2)}, u32[]{:S(2)}) collective-permute-start(f32[2,272,256]{2,1,0:T(8,128)S(1)} %pad_maximum_fusion.3), channel_id=1, source_target_pairs={{4,12},{5,13},{6,14},{7,15},{8,0},{9,1},{10,2},{11,3},{12,20},{13,... | collective-permute-start | bytes 1671176 | tf_op jit(solution)/shard_map/ppermute | solution.py:488
  22.5 17.1 %collective-permute-start.10 = (f32[2,272,256]{2,1,0:T(8,128)S(1)}, f32[2,272,256]{2,1,0:T(8,128)S(1)}, u32[]{:S(2)}, u32[]{:S(2)}) collective-permute-start(f32[2,272,256]{2,1,0:T(8,128)S(1)} %pad_maximum_fusion.4), channel_id=1, source_target_pairs={{0,8},{1,9},{2,10},{3,11},{8,16},{9,17},{10,18},{11,19},{12,4},{13... | collective-permute-start | bytes 1671176 | tf_op jit(solution)/shard_map/ppermute | solution.py:488
  33.3 17.5 %collective-permute-start.8 = (f32[816,256]{1,0:T(8,128)S(1)}, f32[816,256]{1,0:T(8,128)S(1)}, u32[]{:S(2)}, u32[]{:S(2)}) collective-permute-start(f32[816,256]{1,0:T(8,128)S(1)} %pad_maximum_fusion), channel_id=1, source_target_pairs={{0,1},{1,0},{2,3},{3,2},{4,5},{5,4},{6,7},{7,6},{8,9},{9,8},{10,11... | collective-permute-start | bytes 2506760 | tf_op jit(solution)/shard_map/ppermute | solution.py:488
  33.5 21.8 %collective-permute-start.6 = (f32[2,272,256]{2,1,0:T(8,128)S(1)}, f32[2,272,256]{2,1,0:T(8,128)S(1)}, u32[]{:S(2)}, u32[]{:S(2)}) collective-permute-start(f32[2,272,256]{2,1,0:T(8,128)S(1)} %pad_maximum_fusion.1), channel_id=1, source_target_pairs={{4,12},{5,13},{6,14},{7,15},{8,0},{9,1},{10,2},{11,3},{12,20},{13,... | collective-permute-start | bytes 1671176 | tf_op jit(solution)/shard_map/ppermute | solution.py:488
  34.8 20.4 %collective-permute-start.7 = (f32[2,272,256]{2,1,0:T(8,128)S(1)}, f32[2,272,256]{2,1,0:T(8,128)S(1)}, u32[]{:S(2)}, u32[]{:S(2)}) collective-permute-start(f32[2,272,256]{2,1,0:T(8,128)S(1)} %pad_maximum_fusion.2), channel_id=1, source_target_pairs={{0,8},{1,9},{2,10},{3,11},{8,16},{9,17},{10,18},{11,19},{12,4},{13... | collective-permute-start | bytes 1671176 | tf_op jit(solution)/shard_map/ppermute | solution.py:488
  44.9 2.0 %collective-permute-start.11 = (f32[2,4,64,256]{3,2,1,0:T(8,128)S(1)}, f32[2,4,64,256]{3,2,1,0:T(8,128)S(1)}, u32[]{:S(2)}, u32[]{:S(2)}) collective-permute-start(f32[2,4,64,256]{3,2,1,0:T(8,128)S(1)} %get-tuple-element.51.refs_0_), channel_id=1, source_target_pairs={{0,1},{1,0},{2,3},{3,2},{4,5},{5,4},{6,7},{7,6},{8,9},{9,8},{10,11... | collective-permute-start | bytes 1572872 | tf_op jit(solution)/shard_map/ppermute | solution.py:488
  45.0 2.6 %collective-permute-start.12 = (f32[2,4,64,256]{3,2,1,0:T(8,128)S(1)}, f32[2,4,64,256]{3,2,1,0:T(8,128)S(1)}, u32[]{:S(2)}, u32[]{:S(2)}) collective-permute-start(f32[2,4,64,256]{3,2,1,0:T(8,128)S(1)} %get-tuple-element.52.refs_1_), channel_id=1, source_target_pairs={{0,1},{1,0},{2,3},{3,2},{4,5},{5,4},{6,7},{7,6},{8,9},{9,8},{10,11... | collective-permute-start | bytes 1572872 | tf_op jit(solution)/shard_map/ppermute | solution.py:488
  48.7 12.5 %collective-permute-start.18 = (f32[256,256]{1,0:T(8,128)S(1)}, f32[256,256]{1,0:T(8,128)S(1)}, u32[]{:S(2)}, u32[]{:S(2)}) collective-permute-start(f32[256,256]{1,0:T(8,128)S(1)} %get-tuple-element.63), channel_id=1, source_target_pairs={{0,2},{1,3},{2,0},{3,1},{4,6},{5,7},{6,4},{7,5},{8,10},{9,11},{10,... | collective-permute-start | bytes 786440 | tf_op jit(solution)/shard_map/ppermute | solution.py:488
  50.4 13.7 %collective-permute-start.19 = (f32[256,256]{1,0:T(8,128)S(1)}, f32[256,256]{1,0:T(8,128)S(1)}, u32[]{:S(2)}, u32[]{:S(2)}) collective-permute-start(f32[256,256]{1,0:T(8,128)S(1)} %get-tuple-element.64), channel_id=1, source_target_pairs={{0,4},{1,5},{2,6},{3,7},{4,0},{5,1},{6,2},{7,3},{8,12},{9,13},{10,... | collective-permute-start | bytes 786440 | tf_op jit(solution)/shard_map/ppermute | solution.py:488
  50.8 13.3 %collective-permute-start.20 = (f32[256,256]{1,0:T(8,128)S(1)}, f32[256,256]{1,0:T(8,128)S(1)}, u32[]{:S(2)}, u32[]{:S(2)}) collective-permute-start(f32[256,256]{1,0:T(8,128)S(1)} %get-tuple-element.65), channel_id=1, source_target_pairs={{0,6},{1,7},{2,4},{3,5},{4,2},{5,3},{6,0},{7,1},{8,14},{9,15},{10,... | collective-permute-start | bytes 786440 | tf_op jit(solution)/shard_map/ppermute | solution.py:488
  60.6 3.6 %collective-permute-start.13 = (f32[2,4,64,256]{3,2,1,0:T(8,128)S(1)}, f32[2,4,64,256]{3,2,1,0:T(8,128)S(1)}, u32[]{:S(2)}, u32[]{:S(2)}) collective-permute-start(f32[2,4,64,256]{3,2,1,0:T(8,128)S(1)} %get-tuple-element.56.refs_0_), channel_id=1, source_target_pairs={{0,1},{1,0},{2,3},{3,2},{4,5},{5,4},{6,7},{7,6},{8,9},{9,8},{10,11... | collective-permute-start | bytes 1572872 | tf_op jit(solution)/shard_map/ppermute | solution.py:488
  60.7 3.6 %collective-permute-start.14 = (f32[2,4,64,256]{3,2,1,0:T(8,128)S(1)}, f32[2,4,64,256]{3,2,1,0:T(8,128)S(1)}, u32[]{:S(2)}, u32[]{:S(2)}) collective-permute-start(f32[2,4,64,256]{3,2,1,0:T(8,128)S(1)} %get-tuple-element.57.refs_1_), channel_id=1, source_target_pairs={{0,1},{1,0},{2,3},{3,2},{4,5},{5,4},{6,7},{7,6},{8,9},{9,8},{10,11... | collective-permute-start | bytes 1572872 | tf_op jit(solution)/shard_map/ppermute | solution.py:488
  64.2 5.7 %collective-permute-start.21 = (f32[408,256]{1,0:T(8,128)S(1)}, f32[408,256]{1,0:T(8,128)S(1)}, u32[]{:S(2)}, u32[]{:S(2)}) collective-permute-start(f32[408,256]{1,0:T(8,128)S(1)} %pad_maximum_fusion.5), channel_id=1, source_target_pairs={{0,1},{1,0},{2,3},{3,2},{4,5},{5,4},{6,7},{7,6},{8,9},{9,8},{10,11... | collective-permute-start | bytes 1253384 | tf_op jit(solution)/shard_map/ppermute | solution.py:488
  65.3 9.2 %collective-permute-start.15 = (f32[256,256]{1,0:T(8,128)S(1)}, f32[256,256]{1,0:T(8,128)S(1)}, u32[]{:S(2)}, u32[]{:S(2)}) collective-permute-start(f32[256,256]{1,0:T(8,128)S(1)} %get-tuple-element.60), channel_id=1, source_target_pairs={{0,2},{1,3},{2,0},{3,1},{4,6},{5,7},{6,4},{7,5},{8,10},{9,11},{10,... | collective-permute-start | bytes 786440 | tf_op jit(solution)/shard_map/ppermute | solution.py:488
  66.0 13.7 %collective-permute-start.16 = (f32[256,256]{1,0:T(8,128)S(1)}, f32[256,256]{1,0:T(8,128)S(1)}, u32[]{:S(2)}, u32[]{:S(2)}) collective-permute-start(f32[256,256]{1,0:T(8,128)S(1)} %get-tuple-element.61), channel_id=1, source_target_pairs={{0,4},{1,5},{2,6},{3,7},{4,0},{5,1},{6,2},{7,3},{8,12},{9,13},{10,... | collective-permute-start | bytes 786440 | tf_op jit(solution)/shard_map/ppermute | solution.py:488
  67.0 12.7 %collective-permute-start.17 = (f32[256,256]{1,0:T(8,128)S(1)}, f32[256,256]{1,0:T(8,128)S(1)}, u32[]{:S(2)}, u32[]{:S(2)}) collective-permute-start(f32[256,256]{1,0:T(8,128)S(1)} %get-tuple-element.62), channel_id=1, source_target_pairs={{0,6},{1,7},{2,4},{3,5},{4,2},{5,3},{6,0},{7,1},{8,14},{9,15},{10,... | collective-permute-start | bytes 786440 | tf_op jit(solution)/shard_map/ppermute | solution.py:488

commit v5 on v4

--- a/solution.py
+++ b/solution.py
@@ -15,7 +15,6 @@
 PARTS = (2, 2)
 JOINT = ("lat", "depth")
 BODY = 2 * ROWS * SLAB
-PIECES = 1
 HOP_ROWS = 816
 TAIL_ROWS = 136
 VMEM_LIMIT = 48 * 1024 * 1024
@@ -93,51 +92,34 @@
 
 
 def pack_kernel(k, width, heat_hbm, wet_hbm, label_hbm, *refs):
-    *blocks, near, label_ref, sems = refs
+    *outs, blocks, near, label_ref, sems = refs
     columns = heat_hbm.shape[2]
     first, last = chunk_window(k, columns)
-    copies = [pltpu.make_async_copy(label_hbm, label_ref, sems.at[2 * PIECES])]
-    for f, far in enumerate((heat_hbm, wet_hbm)):
-        for piece in range(PIECES):
-            at = pl.ds(piece * (SLAB // PIECES), SLAB // PIECES)
-            copies.append(
-                pltpu.make_async_copy(
-                    far.at[at, :, first:last], near.at[f, at], sems.at[f * PIECES + piece]
-                )
-            )
-    for copy in copies:
-        copy.start()
-    for copy in copies:
-        copy.wait()
+    loads = [
+        pltpu.make_async_copy(far.at[:, :, first:last], near.at[f], sems.at[f])
+        for f, far in enumerate((heat_hbm, wet_hbm))
+    ]
+    labels = pltpu.make_async_copy(label_hbm, label_ref, sems.at[2])
+    labels.start()
+    for load in loads:
+        load.start()
     lane = lanes((SLAB, 128))
     lane8 = lanes((8, 128))
     lane4 = lanes((ROWS, 128))
-    for mask in range(4):
+
+    def window(mask):
         start = column_start(k, mask, columns)
         left = pl.multiple_of(jnp.maximum(start - 128, 0), 128)
         right = pl.multiple_of(jnp.minimum(start + width, columns - 128), 128)
         keep_left = (start > 0).astype(jnp.float32)
         keep_right = (start + width < columns).astype(jnp.float32)
-        main, before, after = (pl.multiple_of(at - first, 128) for at in (start, left, right))
-        for f in range(2):
-            ref = near.at[f]
-            packed = jnp.zeros((8, 128), jnp.float32)
-            for r in range(ROWS):
-                row = (f * ROWS + r) * SLAB
-                blocks[mask][row : row + SLAB, :] = ref[:, r, pl.ds(main, width)]
-                edge = jnp.where(
-                    lane >= 64,
-                    ref[:, r, pl.ds(before, 128)] * keep_left,
-                    ref[:, r, pl.ds(after, 128)] * keep_right,
-                )
-                for g in range(SLAB // 8):
-                    at = 8 * (r * (SLAB // 8) + g)
-                    moved = pltpu.roll(edge[8 * g : 8 * g + 8], (at + 4) % 128, 1)
-                    packed = jnp.where((lane8 >= at) & (lane8 < at + 8), moved, packed)
-            at, lane_at = halo_at(f, width)
-            blocks[mask][at : at + 8, lane_at : lane_at + 128] = packed
-        types = label_at(width)
-        blocks[mask][types : types + 4, :] = (
+        return start, left, right, keep_left, keep_right
+
+    labels.wait()
+    types = label_at(width)
+    for mask in range(4):
+        start, left, right, keep_left, keep_right = window(mask)
+        blocks[mask, types : types + 4, :] = (
             label_ref[:, pl.ds(start, width)] + 1
         ).astype(jnp.float32)
         edge = jnp.where(
@@ -145,10 +127,43 @@
             (label_ref[:, pl.ds(left, 128)] + 1).astype(jnp.float32) * keep_left,
             (label_ref[:, pl.ds(right, 128)] + 1).astype(jnp.float32) * keep_right,
         )
-        blocks[mask][types + 4 : types + 8, :] = jnp.zeros((ROWS, width), jnp.float32)
-        blocks[mask][types + 4 : types + 8, :128] = jnp.where(
+        blocks[mask, types + 4 : types + 8, :] = jnp.zeros((ROWS, width), jnp.float32)
+        blocks[mask, types + 4 : types + 8, :128] = jnp.where(
             (lane4 >= 124) | (lane4 < 4), edge, 0.0
         )
+    begin = chunk_start(k, columns)
+    here = [lax.bitwise_xor(quarter(), part) for part in range(4)]
+    for f in range(2):
+        loads[f].wait()
+        packed = [jnp.zeros((8, 128), jnp.float32)] * 4
+        for r in range(ROWS):
+            row = (f * ROWS + r) * SLAB
+            tiles = {
+                at: near[f, :, r, at - first : at - first + 128]
+                for at in range(first, last, 128)
+            }
+            blank = jnp.zeros((SLAB, 128), jnp.float32)
+            for part in range(4):
+                start = begin + part * width
+                for at in range(start, start + width, 128):
+                    blocks[here[part], row : row + SLAB, at - start : at - start + 128] = tiles[at]
+                edge = jnp.where(
+                    lane >= 64, tiles.get(start - 128, blank), tiles.get(start + width, blank)
+                )
+                for g in range(SLAB // 8):
+                    at = 8 * (r * (SLAB // 8) + g)
+                    moved = pltpu.roll(edge[8 * g : 8 * g + 8], (at + 4) % 128, 1)
+                    packed[part] = jnp.where((lane8 >= at) & (lane8 < at + 8), moved, packed[part])
+        at, lane_at = halo_at(f, width)
+        for part in range(4):
+            blocks[here[part], at : at + 8, lane_at : lane_at + 128] = packed[part]
+    stores = [
+        pltpu.make_async_copy(blocks.at[mask], outs[mask], sems.at[3 + mask]) for mask in range(4)
+    ]
+    for store in stores:
+        store.start()
+    for store in stores:
+        store.wait()
 
 
 def pack(k, width, heat, wet, label):
@@ -158,11 +173,12 @@
         functools.partial(pack_kernel, k, width),
         out_shape=[shape] * 4,
         in_specs=[pl.BlockSpec(memory_space=pltpu.HBM)] * 3,
-        out_specs=[pl.BlockSpec(memory_space=pltpu.VMEM)] * 4,
+        out_specs=[pl.BlockSpec(memory_space=pl.ANY)] * 4,
         scratch_shapes=[
+            pltpu.VMEM((4, block_rows(width), width), jnp.float32),
             pltpu.VMEM((2, SLAB, ROWS, last - first), jnp.float32),
             pltpu.VMEM(label.shape, jnp.int32),
-            pltpu.SemaphoreType.DMA((2 * PIECES + 1,)),
+            pltpu.SemaphoreType.DMA((7,)),
         ],
         compiler_params=params(VMEM_LIMIT if k else FIRST_LIMIT),
         cost_estimate=cost(0, 4 << 20),

time: 81.2 us -> 81.2 us (level)
  transfers between devices with their start and end apart: 22 -> 22, of which waited for: 7 -> 7; matrix products, arithmetic and copies ran while one was open for 0% -> 0% of each run, Pallas kernels for 27% -> 28%
where the time goes in v5:
time: 81.2 us; the launch traced here: 80.9 us
  starting transfers between devices  29.8 us (37%)
  Pallas kernels  26.8 us (33%)
  waiting for transfers between devices  21.7 us (27%)
  local copies, waits for them, and re-layouts  1.29 us (2%)
  between operations  1.14 us (1%)
    ppermute x22, starting transfers between devices, send(): return lax.ppermute(array, JOINT, route[name])  29.8 us
    ppermute x22, waiting for transfers between devices, send(): return lax.ppermute(array, JOINT, route[name])  21.7 us
    pallas_call x2, Pallas kernels, stencil(): pl.pallas_call(functools.partial(stencil_kernel, width), out_shape=[jax.S...  10.7 us
    pallas_call x2, Pallas kernels, pre(): pl.pallas_call(functools.partial(pre_kernel, width), out_shape=[jax.Shape...  6.04 us
    pallas_call x2, Pallas kernels, pack(): pl.pallas_call(functools.partial(pack_kernel, k, width), out_shape=[shape...  5.3 us
    pallas_call x2, Pallas kernels, assemble(): pl.pallas_call(functools.partial(assemble_kernel, k, width), out_shape=[s...  2.14 us
    pallas_call x2, Pallas kernels, solve(): pl.pallas_call(solve_kernel, out_shape=[shape] * 4, in_specs=[pl.BlockSpe...  1.98 us
  transfers between devices with their start and end apart: 22, of which 7 were waited for; matrix products, arithmetic and copies ran while one was open for 0% of the time, Pallas kernels for 28%

profile of v5, /device:TPU:0, one launch (start us, length us, event | category | flops | bytes accessed | tf_op | source)
XLA Modules:
  0.0 80.9 jit_solution(14594789946979478482)
XLA Ops:
  0.6 0.0 copy-start.3
  0.6 0.0 copy-start
  0.6 3.5 %pack.3 = (f32[272,256]{1,0:T(8,128)}, f32[272,256]{1,0:T(8,128)}, f32[272,256]{1,0:T(8,128)}, f32[272,256]{1,0:T(8,128)}) custom-call(f32[32,4,2048]{2,1,0:T(4,128)} %heat_hbm.3, f32[32,4,2048]{2,1,0:T(4,128)} %wet_hbm.3, s32[4,2048]{1,0:T(4,128)} %label_hbm.3), custom_call_target="tpu_custom_call" | custom-call | bytes 1024 | tf_op jit(solution)/shard_map/pack/pallas_call | solution.py:172
  4.2 3.0 %collective-permute-start.3 = (f32[272,256]{1,0:T(8,128)}, f32[272,256]{1,0:T(8,128)S(1)}, u32[]{:S(2)}, u32[]{:S(2)}) collective-permute-start(f32[272,256]{1,0:T(8,128)} %get-tuple-element.40), channel_id=1, source_target_pairs={{0,4},{1,5},{2,6},{3,7},{4,0},{5,1},{6,2},{7,3},{8,12},{9,13},{10,... | collective-permute-start | bytes 835592 | tf_op jit(solution)/shard_map/ppermute | solution.py:504
  7.2 1.5 %collective-permute-start.2 = (f32[272,256]{1,0:T(8,128)}, f32[272,256]{1,0:T(8,128)S(1)}, u32[]{:S(2)}, u32[]{:S(2)}) collective-permute-start(f32[272,256]{1,0:T(8,128)} %get-tuple-element.39), channel_id=1, source_target_pairs={{0,2},{1,3},{2,0},{3,1},{4,6},{5,7},{6,4},{7,5},{8,10},{9,11},{10,... | collective-permute-start | bytes 835592 | tf_op jit(solution)/shard_map/ppermute | solution.py:504
  8.7 0.0 collective-permute-start.4
  8.7 1.2 %copy-done.1 = f32[32,4,2048]{2,1,0:T(4,128)S(1)} copy-done((f32[32,4,2048]{2,1,0:T(4,128)S(1)}, f32[32,4,2048]{2,1,0:T(4,128)}, u32[]{:S(2)}) %copy-start.1) | copy-done | bytes 1048600
  10.0 0.0 copy-start.7
  10.0 0.0 copy-start.8
  10.0 1.8 %pack.2 = (f32[272,256]{1,0:T(8,128)S(1)}, f32[272,256]{1,0:T(8,128)S(1)}, f32[272,256]{1,0:T(8,128)S(1)}, f32[272,256]{1,0:T(8,128)S(1)}) custom-call(f32[32,4,2048]{2,1,0:T(4,128)S(1)} %copy-done, f32[32,4,2048]{2,1,0:T(4,128)S(1)} %copy-done.1, s32[4,2048]{1,0:T(4,128)S(1)} %copy-done.3), custom_call_target="tpu_custom_call" | custom-call | bytes 1024 | tf_op jit(solution)/shard_map/pack/pallas_call | solution.py:172
  11.8 2.0 %collective-permute-start = (f32[272,256]{1,0:T(8,128)S(1)}, f32[272,256]{1,0:T(8,128)S(1)}, u32[]{:S(2)}, u32[]{:S(2)}) collective-permute-start(f32[272,256]{1,0:T(8,128)S(1)} %get-tuple-element.36), channel_id=1, source_target_pairs={{0,2},{1,3},{2,0},{3,1},{4,6},{5,7},{6,4},{7,5},{8,10},{9,11},{10,... | collective-permute-start | bytes 835592 | tf_op jit(solution)/shard_map/ppermute | solution.py:504
  13.8 1.5 %collective-permute-start.1 = (f32[272,256]{1,0:T(8,128)S(1)}, f32[272,256]{1,0:T(8,128)S(1)}, u32[]{:S(2)}, u32[]{:S(2)}) collective-permute-start(f32[272,256]{1,0:T(8,128)S(1)} %get-tuple-element.37), channel_id=1, source_target_pairs={{0,4},{1,5},{2,6},{3,7},{4,0},{5,1},{6,2},{7,3},{8,12},{9,13},{10,... | collective-permute-start | bytes 835592 | tf_op jit(solution)/shard_map/ppermute | solution.py:504
  15.3 0.0 collective-permute-done.3.ry
  15.3 2.0 %collective-permute-start.5 = (f32[272,256]{1,0:T(8,128)S(1)}, f32[272,256]{1,0:T(8,128)S(1)}, u32[]{:S(2)}, u32[]{:S(2)}) collective-permute-start(f32[272,256]{1,0:T(8,128)S(1)} %get-tuple-element.46), channel_id=1, source_target_pairs={{0,6},{1,7},{2,4},{3,5},{4,2},{5,3},{6,0},{7,1},{8,14},{9,15},{10,... | collective-permute-start | bytes 835592 | tf_op jit(solution)/shard_map/ppermute | solution.py:504
  17.3 0.0 collective-permute-done.2.rx
  17.3 1.3 %collective-permute-start.9 = (f32[2,272,256]{2,1,0:T(8,128)S(1)}, f32[2,272,256]{2,1,0:T(8,128)S(1)}, u32[]{:S(2)}, u32[]{:S(2)}) collective-permute-start(f32[2,272,256]{2,1,0:T(8,128)S(1)} %pad_maximum_fusion.3), channel_id=1, source_target_pairs={{4,12},{5,13},{6,14},{7,15},{8,0},{9,1},{10,2},{11,3},{12,20},{13,... | collective-permute-start | bytes 1671176 | tf_op jit(solution)/shard_map/ppermute | solution.py:504
  18.6 3.8 %collective-permute-done.4.rxy = f32[272,256]{1,0:T(8,128)S(1)} collective-permute-done((f32[272,256]{1,0:T(8,128)}, f32[272,256]{1,0:T(8,128)S(1)}, u32[]{:S(2)}, u32[]{:S(2)}) %collective-permute-start.4) | collective-permute-done | bytes 278560 | tf_op jit(solution)/shard_map/ppermute | solution.py:504
  22.5 4.0 %collective-permute-start.10 = (f32[2,272,256]{2,1,0:T(8,128)S(1)}, f32[2,272,256]{2,1,0:T(8,128)S(1)}, u32[]{:S(2)}, u32[]{:S(2)}) collective-permute-start(f32[2,272,256]{2,1,0:T(8,128)S(1)} %pad_maximum_fusion.4), channel_id=1, source_target_pairs={{0,8},{1,9},{2,10},{3,11},{8,16},{9,17},{10,18},{11,19},{12,4},{13... | collective-permute-start | bytes 1671176 | tf_op jit(solution)/shard_map/ppermute | solution.py:504
  26.5 0.0 copy-done.4
  26.5 0.0 copy-done.5
  26.5 0.0 copy-done.6
  26.5 0.7 prep.1
  27.3 3.0 %inner_substeps.2 = (f32[10,2,64,384]{3,2,1,0:T(8,128)S(1)}, f32[2,8,384]{2,1,0:T(8,128)S(1)}, f32[8,256]{1,0:T(8,128)S(1)}) custom-call(f32[272,256]{1,0:T(8,128)S(1)} %copy-done.2, f32[272,256]{1,0:T(8,128)S(1)} %collective-permute-done.2.rx, f32[272,256]{1,0:T(8,128)S(1)} %collective-permute-done.3.ry, f32[272,256]{1,0:T(8,128)S(1)} %collective-permute-done.4.rxy, ...), custom_call_target="tpu_custom_call" | custom-call | bytes 1024 | tf_op jit(solution)/shard_map/inner_substeps/pallas_call | solution.py:325
  30.3 0.0 collective-permute-done.1.ry
  30.3 0.0 collective-permute-done.rx
  30.3 2.9 %collective-permute-done.5.rxy = f32[272,256]{1,0:T(8,128)S(1)} collective-permute-done((f32[272,256]{1,0:T(8,128)S(1)}, f32[272,256]{1,0:T(8,128)S(1)}, u32[]{:S(2)}, u32[]{:S(2)}) %collective-permute-start.5) | collective-permute-done | bytes 278560 | tf_op jit(solution)/shard_map/ppermute | solution.py:504
  33.3 0.1 pad_maximum_fusion
  33.3 0.1 collective-permute-start.8
  33.5 1.3 %collective-permute-start.6 = (f32[2,272,256]{2,1,0:T(8,128)S(1)}, f32[2,272,256]{2,1,0:T(8,128)S(1)}, u32[]{:S(2)}, u32[]{:S(2)}) collective-permute-start(f32[2,272,256]{2,1,0:T(8,128)S(1)} %pad_maximum_fusion.1), channel_id=1, source_target_pairs={{4,12},{5,13},{6,14},{7,15},{8,0},{9,1},{10,2},{11,3},{12,20},{13,... | collective-permute-start | bytes 1671176 | tf_op jit(solution)/shard_map/ppermute | solution.py:504
  34.8 4.8 %collective-permute-start.7 = (f32[2,272,256]{2,1,0:T(8,128)S(1)}, f32[2,272,256]{2,1,0:T(8,128)S(1)}, u32[]{:S(2)}, u32[]{:S(2)}) collective-permute-start(f32[2,272,256]{2,1,0:T(8,128)S(1)} %pad_maximum_fusion.2), channel_id=1, source_target_pairs={{0,8},{1,9},{2,10},{3,11},{8,16},{9,17},{10,18},{11,19},{12,4},{13... | collective-permute-start | bytes 1671176 | tf_op jit(solution)/shard_map/ppermute | solution.py:504
  39.6 0.0 collective-permute-done.9.p1
  39.6 0.0 collective-permute-done.10.p2
  39.6 5.3 %outer_substeps.2 = (f32[2,4,64,256]{3,2,1,0:T(8,128)S(1)}, f32[2,4,64,256]{3,2,1,0:T(8,128)S(1)}) custom-call(f32[272,256]{1,0:T(8,128)S(1)} %copy-done.2, f32[272,256]{1,0:T(8,128)S(1)} %collective-permute-done.2.rx, f32[272,256]{1,0:T(8,128)S(1)} %collective-permute-done.3.ry, f32[272,256]{1,0:T(8,128)S(1)} %collective-permute-done.4.rxy, ...), custom_call_target="tpu_custom_call" | custom-call | bytes 1024 | tf_op jit(solution)/shard_map/outer_substeps/pallas_call | solution.py:378
  44.9 0.1 collective-permute-start.11
  45.0 0.5 collective-permute-start.12
  45.5 1.4 %collective-permute-done.11.refs_2_ = f32[2,4,64,256]{3,2,1,0:T(8,128)S(1)} collective-permute-done((f32[2,4,64,256]{3,2,1,0:T(8,128)S(1)}, f32[2,4,64,256]{3,2,1,0:T(8,128)S(1)}, u32[]{:S(2)}, u32[]{:S(2)}) %collective-permute-start.11) | collective-permute-done | bytes 524320 | tf_op jit(solution)/shard_map/ppermute | solution.py:504
  46.9 0.7 collective-permute-done.12.refs_3_
  47.7 1.0 %solve.2 = (f32[256,256]{1,0:T(8,128)S(1)}, f32[256,256]{1,0:T(8,128)S(1)}, f32[256,256]{1,0:T(8,128)S(1)}, f32[256,256]{1,0:T(8,128)S(1)}) custom-call(f32[2,4,64,256]{3,2,1,0:T(8,128)S(1)} %get-tuple-element.51.refs_0_, f32[2,4,64,256]{3,2,1,0:T(8,128)S(1)} %get-tuple-element.52.refs_1_, f32[2,4,64,256]{3,2,1,0:T(8,128)S(1)} %collective-permute-done.11.refs_2_, ...), custom_call_target="tpu_custom_call" | custom-call | bytes 1024 | tf_op jit(solution)/shard_map/solve/pallas_call | solution.py:426
  48.7 1.7 %collective-permute-start.18 = (f32[256,256]{1,0:T(8,128)S(1)}, f32[256,256]{1,0:T(8,128)S(1)}, u32[]{:S(2)}, u32[]{:S(2)}) collective-permute-start(f32[256,256]{1,0:T(8,128)S(1)} %get-tuple-element.63), channel_id=1, source_target_pairs={{0,2},{1,3},{2,0},{3,1},{4,6},{5,7},{6,4},{7,5},{8,10},{9,11},{10,... | collective-permute-start | bytes 786440 | tf_op jit(solution)/shard_map/ppermute | solution.py:504
  50.4 0.5 collective-permute-start.19
  50.8 0.0 collective-permute-done.8._
  50.8 1.4 %collective-permute-start.20 = (f32[256,256]{1,0:T(8,128)S(1)}, f32[256,256]{1,0:T(8,128)S(1)}, u32[]{:S(2)}, u32[]{:S(2)}) collective-permute-start(f32[256,256]{1,0:T(8,128)S(1)} %get-tuple-element.65), channel_id=1, source_target_pairs={{0,6},{1,7},{2,4},{3,5},{4,2},{5,3},{6,0},{7,1},{8,14},{9,15},{10,... | collective-permute-start | bytes 786440 | tf_op jit(solution)/shard_map/ppermute | solution.py:504
  52.2 3.0 %inner_substeps.3 = (f32[10,2,64,384]{3,2,1,0:T(8,128)S(1)}, f32[2,8,384]{2,1,0:T(8,128)S(1)}, f32[8,256]{1,0:T(8,128)S(1)}) custom-call(f32[272,256]{1,0:T(8,128)S(1)} %get-tuple-element.35.own, f32[272,256]{1,0:T(8,128)S(1)} %collective-permute-done.rx, f32[272,256]{1,0:T(8,128)S(1)} %collective-permute-done.1.ry, ...), custom_call_target="tpu_custom_call" | custom-call | bytes 1024 | tf_op jit(solution)/shard_map/inner_substeps/pallas_call | solution.py:325
  55.2 0.0 collective-permute-done.6.p1
  55.2 0.0 collective-permute-done.7.p2
  55.3 5.3 %outer_substeps.3 = (f32[2,4,64,256]{3,2,1,0:T(8,128)S(1)}, f32[2,4,64,256]{3,2,1,0:T(8,128)S(1)}) custom-call(f32[272,256]{1,0:T(8,128)S(1)} %get-tuple-element.35.own, f32[272,256]{1,0:T(8,128)S(1)} %collective-permute-done.rx, f32[272,256]{1,0:T(8,128)S(1)} %collective-permute-done.1.ry, f32[272,256]{1,0:T(8,128)S(1)} %collective-permute-done.5.rxy, ...), custom_call_target="tpu_custom_call" | custom-call | bytes 1024 | tf_op jit(solution)/shard_map/outer_substeps/pallas_call | solution.py:378
  60.6 0.1 collective-permute-start.13
  60.7 0.5 collective-permute-start.14
  61.2 0.0 collective-permute-done.18.refs_1_
  61.2 2.9 %collective-permute-done.19.refs_2_ = f32[256,256]{1,0:T(8,128)S(1)} collective-permute-done((f32[256,256]{1,0:T(8,128)S(1)}, f32[256,256]{1,0:T(8,128)S(1)}, u32[]{:S(2)}, u32[]{:S(2)}) %collective-permute-start.19) | collective-permute-done | bytes 262176 | tf_op jit(solution)/shard_map/ppermute | solution.py:504
  64.1 0.0 collective-permute-done.20.refs_3_
  64.1 0.1 collective-permute-start.21
  64.2 0.0 collective-permute-done.13.refs_2_
  64.2 0.0 collective-permute-done.14.refs_3_
  64.2 1.0 %solve.3 = (f32[256,256]{1,0:T(8,128)S(1)}, f32[256,256]{1,0:T(8,128)S(1)}, f32[256,256]{1,0:T(8,128)S(1)}, f32[256,256]{1,0:T(8,128)S(1)}) custom-call(f32[2,4,64,256]{3,2,1,0:T(8,128)S(1)} %get-tuple-element.56.refs_0_, f32[2,4,64,256]{3,2,1,0:T(8,128)S(1)} %get-tuple-element.57.refs_1_, f32[2,4,64,256]{3,2,1,0:T(8,128)S(1)} %collective-permute-done.13.refs_2_, ...), custom_call_target="tpu_custom_call" | custom-call | bytes 1024 | tf_op jit(solution)/shard_map/solve/pallas_call | solution.py:426
  65.2 0.8 collective-permute-start.15
  66.0 1.0 %collective-permute-start.16 = (f32[256,256]{1,0:T(8,128)S(1)}, f32[256,256]{1,0:T(8,128)S(1)}, u32[]{:S(2)}, u32[]{:S(2)}) collective-permute-start(f32[256,256]{1,0:T(8,128)S(1)} %get-tuple-element.61), channel_id=1, source_target_pairs={{0,4},{1,5},{2,6},{3,7},{4,0},{5,1},{6,2},{7,3},{8,12},{9,13},{10,... | collective-permute-start | bytes 786440 | tf_op jit(solution)/shard_map/ppermute | solution.py:504
  67.0 1.8 %collective-permute-start.17 = (f32[256,256]{1,0:T(8,128)S(1)}, f32[256,256]{1,0:T(8,128)S(1)}, u32[]{:S(2)}, u32[]{:S(2)}) collective-permute-start(f32[256,256]{1,0:T(8,128)S(1)} %get-tuple-element.62), channel_id=1, source_target_pairs={{0,6},{1,7},{2,4},{3,5},{4,2},{5,3},{6,0},{7,1},{8,14},{9,15},{10,... | collective-permute-start | bytes 786440 | tf_op jit(solution)/shard_map/ppermute | solution.py:504
  68.8 1.1 %assemble.2 = (f32[32,4,2048]{2,1,0:T(4,128)}, f32[32,4,2048]{2,1,0:T(4,128)}) custom-call(f32[256,256]{1,0:T(8,128)S(1)} %get-tuple-element.54.refs_0_, f32[256,256]{1,0:T(8,128)S(1)} %collective-permute-done.18.refs_1_, f32[256,256]{1,0:T(8,128)S(1)} %collective-permute-done.19.refs_2_, f32[256,256]{1,0:T(8,128)S(1)} %collective-permute-done.20.refs_3_), custom_call_target="tpu_custom_call" | custom-call | bytes 1024 | tf_op jit(solution)/shard_map/assemble/pallas_call | solution.py:460
  69.9 0.0 collective-permute-done.21.refs_6_
  69.9 4.5 %collective-permute-done.15.refs_1_ = f32[256,256]{1,0:T(8,128)S(1)} collective-permute-done((f32[256,256]{1,0:T(8,128)S(1)}, f32[256,256]{1,0:T(8,128)S(1)}, u32[]{:S(2)}, u32[]{:S(2)}) %collective-permute-start.15) | collective-permute-done | bytes 262176 | tf_op jit(solution)/shard_map/ppermute | solution.py:504
  74.4 5.3 %collective-permute-done.16.refs_2_ = f32[256,256]{1,0:T(8,128)S(1)} collective-permute-done((f32[256,256]{1,0:T(8,128)S(1)}, f32[256,256]{1,0:T(8,128)S(1)}, u32[]{:S(2)}, u32[]{:S(2)}) %collective-permute-start.16) | collective-permute-done | bytes 262176 | tf_op jit(solution)/shard_map/ppermute | solution.py:504
  79.7 0.0 collective-permute-done.17.refs_3_
  79.7 1.1 %assemble.3 = (f32[32,4,2048]{2,1,0:T(4,128)}, f32[32,4,2048]{2,1,0:T(4,128)}) custom-call(f32[256,256]{1,0:T(8,128)S(1)} %get-tuple-element.59.refs_0_, f32[256,256]{1,0:T(8,128)S(1)} %collective-permute-done.15.refs_1_, f32[256,256]{1,0:T(8,128)S(1)} %collective-permute-done.16.refs_2_, ...), custom_call_target="tpu_custom_call", output_to_operand_aliasing={{0}: (4, {}), {1}: (5, {})} | custom-call | bytes 1024 | tf_op jit(solution)/shard_map/assemble/pallas_call | solution.py:460
  (18 shorter events, 0.2 us)
Async XLA Ops:
  0.6 8.1 %copy-start.3 = (s32[4,2048]{1,0:T(4,128)S(1)}, s32[4,2048]{1,0:T(4,128)}, u32[]{:S(2)}) copy-start(s32[4,2048]{1,0:T(4,128)} %label_hbm.3) | copy-start | bytes 98308
  0.6 8.1 %copy-start = (f32[32,4,2048]{2,1,0:T(4,128)S(1)}, f32[32,4,2048]{2,1,0:T(4,128)}, u32[]{:S(2)}) copy-start(f32[32,4,2048]{2,1,0:T(4,128)} %heat_hbm.3) | copy-start | bytes 3145732
  4.2 11.2 %collective-permute-start.3 = (f32[272,256]{1,0:T(8,128)}, f32[272,256]{1,0:T(8,128)S(1)}, u32[]{:S(2)}, u32[]{:S(2)}) collective-permute-start(f32[272,256]{1,0:T(8,128)} %get-tuple-element.40), channel_id=1, source_target_pairs={{0,4},{1,5},{2,6},{3,7},{4,0},{5,1},{6,2},{7,3},{8,12},{9,13},{10,... | collective-permute-start | bytes 835592 | tf_op jit(solution)/shard_map/ppermute | solution.py:504
  7.2 10.1 %collective-permute-start.2 = (f32[272,256]{1,0:T(8,128)}, f32[272,256]{1,0:T(8,128)S(1)}, u32[]{:S(2)}, u32[]{:S(2)}) collective-permute-start(f32[272,256]{1,0:T(8,128)} %get-tuple-element.39), channel_id=1, source_target_pairs={{0,2},{1,3},{2,0},{3,1},{4,6},{5,7},{6,4},{7,5},{8,10},{9,11},{10,... | collective-permute-start | bytes 835592 | tf_op jit(solution)/shard_map/ppermute | solution.py:504
  8.7 13.8 %collective-permute-start.4 = (f32[272,256]{1,0:T(8,128)}, f32[272,256]{1,0:T(8,128)S(1)}, u32[]{:S(2)}, u32[]{:S(2)}) collective-permute-start(f32[272,256]{1,0:T(8,128)} %get-tuple-element.41), channel_id=1, source_target_pairs={{0,6},{1,7},{2,4},{3,5},{4,2},{5,3},{6,0},{7,1},{8,14},{9,15},{10,... | collective-permute-start | bytes 835592 | tf_op jit(solution)/shard_map/ppermute | solution.py:504
  8.7 1.2 %copy-start.1 = (f32[32,4,2048]{2,1,0:T(4,128)S(1)}, f32[32,4,2048]{2,1,0:T(4,128)}, u32[]{:S(2)}) copy-start(f32[32,4,2048]{2,1,0:T(4,128)} %wet_hbm.3) | copy-start | bytes 3145732
  10.0 7.3 %copy-start.2 = (f32[272,256]{1,0:T(8,128)S(1)}, f32[272,256]{1,0:T(8,128)}, u32[]{:S(2)}) copy-start(f32[272,256]{1,0:T(8,128)} %get-tuple-element.38.own) | copy-start | bytes 835588
  10.0 16.5 %copy-start.4 = (f32[128,128]{1,0:T(8,128)S(1)}, f32[128,128]{1,0:T(8,128)}, u32[]{:S(2)}) copy-start(f32[128,128]{1,0:T(8,128)} %thermal_ref.1) | copy-start | bytes 196612
  10.0 16.5 %copy-start.5 = (f32[128,128]{1,0:T(8,128)S(1)}, f32[128,128]{1,0:T(8,128)}, u32[]{:S(2)}) copy-start(f32[128,128]{1,0:T(8,128)} %water_ref.1) | copy-start | bytes 196612
  10.0 16.6 %copy-start.6 = (f32[128,128]{1,0:T(8,128)S(1)}, f32[128,128]{1,0:T(8,128)}, u32[]{:S(2)}) copy-start(f32[128,128]{1,0:T(8,128)} %constant.2.clone.cheb_ref) | copy-start | bytes 196612
  10.0 17.3 %copy-start.7 = (f32[12]{0:T(128)S(1)}, f32[12]{0:T(128)}, u32[]{:S(2)}) copy-start(f32[12]{0:T(128)} %spread_ref.7) | copy-start | bytes 148
  10.0 17.3 %copy-start.8 = (f32[12]{0:T(128)S(1)}, f32[12]{0:T(128)}, u32[]{:S(2)}) copy-start(f32[12]{0:T(128)} %factor_ref.7) | copy-start | bytes 148
  11.8 18.5 %collective-permute-start = (f32[272,256]{1,0:T(8,128)S(1)}, f32[272,256]{1,0:T(8,128)S(1)}, u32[]{:S(2)}, u32[]{:S(2)}) collective-permute-start(f32[272,256]{1,0:T(8,128)S(1)} %get-tuple-element.36), channel_id=1, source_target_pairs={{0,2},{1,3},{2,0},{3,1},{4,6},{5,7},{6,4},{7,5},{8,10},{9,11},{10,... | collective-permute-start | bytes 835592 | tf_op jit(solution)/shard_map/ppermute | solution.py:504
  13.8 16.5 %collective-permute-start.1 = (f32[272,256]{1,0:T(8,128)S(1)}, f32[272,256]{1,0:T(8,128)S(1)}, u32[]{:S(2)}, u32[]{:S(2)}) collective-permute-start(f32[272,256]{1,0:T(8,128)S(1)} %get-tuple-element.37), channel_id=1, source_target_pairs={{0,4},{1,5},{2,6},{3,7},{4,0},{5,1},{6,2},{7,3},{8,12},{9,13},{10,... | collective-permute-start | bytes 835592 | tf_op jit(solution)/shard_map/ppermute | solution.py:504
  15.3 18.0 %collective-permute-start.5 = (f32[272,256]{1,0:T(8,128)S(1)}, f32[272,256]{1,0:T(8,128)S(1)}, u32[]{:S(2)}, u32[]{:S(2)}) collective-permute-start(f32[272,256]{1,0:T(8,128)S(1)} %get-tuple-element.46), channel_id=1, source_target_pairs={{0,6},{1,7},{2,4},{3,5},{4,2},{5,3},{6,0},{7,1},{8,14},{9,15},{10,... | collective-permute-start | bytes 835592 | tf_op jit(solution)/shard_map/ppermute | solution.py:504
  17.3 22.2 %collective-permute-start.9 = (f32[2,272,256]{2,1,0:T(8,128)S(1)}, f32[2,272,256]{2,1,0:T(8,128)S(1)}, u32[]{:S(2)}, u32[]{:S(2)}) collective-permute-start(f32[2,272,256]{2,1,0:T(8,128)S(1)} %pad_maximum_fusion.3), channel_id=1, source_target_pairs={{4,12},{5,13},{6,14},{7,15},{8,0},{9,1},{10,2},{11,3},{12,20},{13,... | collective-permute-start | bytes 1671176 | tf_op jit(solution)/shard_map/ppermute | solution.py:504
  22.5 17.1 %collective-permute-start.10 = (f32[2,272,256]{2,1,0:T(8,128)S(1)}, f32[2,272,256]{2,1,0:T(8,128)S(1)}, u32[]{:S(2)}, u32[]{:S(2)}) collective-permute-start(f32[2,272,256]{2,1,0:T(8,128)S(1)} %pad_maximum_fusion.4), channel_id=1, source_target_pairs={{0,8},{1,9},{2,10},{3,11},{8,16},{9,17},{10,18},{11,19},{12,4},{13... | collective-permute-start | bytes 1671176 | tf_op jit(solution)/shard_map/ppermute | solution.py:504
  33.3 17.5 %collective-permute-start.8 = (f32[816,256]{1,0:T(8,128)S(1)}, f32[816,256]{1,0:T(8,128)S(1)}, u32[]{:S(2)}, u32[]{:S(2)}) collective-permute-start(f32[816,256]{1,0:T(8,128)S(1)} %pad_maximum_fusion), channel_id=1, source_target_pairs={{0,1},{1,0},{2,3},{3,2},{4,5},{5,4},{6,7},{7,6},{8,9},{9,8},{10,11... | collective-permute-start | bytes 2506760 | tf_op jit(solution)/shard_map/ppermute | solution.py:504
  33.5 21.8 %collective-permute-start.6 = (f32[2,272,256]{2,1,0:T(8,128)S(1)}, f32[2,272,256]{2,1,0:T(8,128)S(1)}, u32[]{:S(2)}, u32[]{:S(2)}) collective-permute-start(f32[2,272,256]{2,1,0:T(8,128)S(1)} %pad_maximum_fusion.1), channel_id=1, source_target_pairs={{4,12},{5,13},{6,14},{7,15},{8,0},{9,1},{10,2},{11,3},{12,20},{13,... | collective-permute-start | bytes 1671176 | tf_op jit(solution)/shard_map/ppermute | solution.py:504
  34.8 20.4 %collective-permute-start.7 = (f32[2,272,256]{2,1,0:T(8,128)S(1)}, f32[2,272,256]{2,1,0:T(8,128)S(1)}, u32[]{:S(2)}, u32[]{:S(2)}) collective-permute-start(f32[2,272,256]{2,1,0:T(8,128)S(1)} %pad_maximum_fusion.2), channel_id=1, source_target_pairs={{0,8},{1,9},{2,10},{3,11},{8,16},{9,17},{10,18},{11,19},{12,4},{13... | collective-permute-start | bytes 1671176 | tf_op jit(solution)/shard_map/ppermute | solution.py:504
  44.9 2.0 %collective-permute-start.11 = (f32[2,4,64,256]{3,2,1,0:T(8,128)S(1)}, f32[2,4,64,256]{3,2,1,0:T(8,128)S(1)}, u32[]{:S(2)}, u32[]{:S(2)}) collective-permute-start(f32[2,4,64,256]{3,2,1,0:T(8,128)S(1)} %get-tuple-element.51.refs_0_), channel_id=1, source_target_pairs={{0,1},{1,0},{2,3},{3,2},{4,5},{5,4},{6,7},{7,6},{8,9},{9,8},{10,11... | collective-permute-start | bytes 1572872 | tf_op jit(solution)/shard_map/ppermute | solution.py:504
  45.0 2.6 %collective-permute-start.12 = (f32[2,4,64,256]{3,2,1,0:T(8,128)S(1)}, f32[2,4,64,256]{3,2,1,0:T(8,128)S(1)}, u32[]{:S(2)}, u32[]{:S(2)}) collective-permute-start(f32[2,4,64,256]{3,2,1,0:T(8,128)S(1)} %get-tuple-element.52.refs_1_), channel_id=1, source_target_pairs={{0,1},{1,0},{2,3},{3,2},{4,5},{5,4},{6,7},{7,6},{8,9},{9,8},{10,11... | collective-permute-start | bytes 1572872 | tf_op jit(solution)/shard_map/ppermute | solution.py:504
  48.7 12.5 %collective-permute-start.18 = (f32[256,256]{1,0:T(8,128)S(1)}, f32[256,256]{1,0:T(8,128)S(1)}, u32[]{:S(2)}, u32[]{:S(2)}) collective-permute-start(f32[256,256]{1,0:T(8,128)S(1)} %get-tuple-element.63), channel_id=1, source_target_pairs={{0,2},{1,3},{2,0},{3,1},{4,6},{5,7},{6,4},{7,5},{8,10},{9,11},{10,... | collective-permute-start | bytes 786440 | tf_op jit(solution)/shard_map/ppermute | solution.py:504
  50.4 13.7 %collective-permute-start.19 = (f32[256,256]{1,0:T(8,128)S(1)}, f32[256,256]{1,0:T(8,128)S(1)}, u32[]{:S(2)}, u32[]{:S(2)}) collective-permute-start(f32[256,256]{1,0:T(8,128)S(1)} %get-tuple-element.64), channel_id=1, source_target_pairs={{0,4},{1,5},{2,6},{3,7},{4,0},{5,1},{6,2},{7,3},{8,12},{9,13},{10,... | collective-permute-start | bytes 786440 | tf_op jit(solution)/shard_map/ppermute | solution.py:504
  50.8 13.2 %collective-permute-start.20 = (f32[256,256]{1,0:T(8,128)S(1)}, f32[256,256]{1,0:T(8,128)S(1)}, u32[]{:S(2)}, u32[]{:S(2)}) collective-permute-start(f32[256,256]{1,0:T(8,128)S(1)} %get-tuple-element.65), channel_id=1, source_target_pairs={{0,6},{1,7},{2,4},{3,5},{4,2},{5,3},{6,0},{7,1},{8,14},{9,15},{10,... | collective-permute-start | bytes 786440 | tf_op jit(solution)/shard_map/ppermute | solution.py:504
  60.6 3.6 %collective-permute-start.13 = (f32[2,4,64,256]{3,2,1,0:T(8,128)S(1)}, f32[2,4,64,256]{3,2,1,0:T(8,128)S(1)}, u32[]{:S(2)}, u32[]{:S(2)}) collective-permute-start(f32[2,4,64,256]{3,2,1,0:T(8,128)S(1)} %get-tuple-element.56.refs_0_), channel_id=1, source_target_pairs={{0,1},{1,0},{2,3},{3,2},{4,5},{5,4},{6,7},{7,6},{8,9},{9,8},{10,11... | collective-permute-start | bytes 1572872 | tf_op jit(solution)/shard_map/ppermute | solution.py:504
  60.7 3.6 %collective-permute-start.14 = (f32[2,4,64,256]{3,2,1,0:T(8,128)S(1)}, f32[2,4,64,256]{3,2,1,0:T(8,128)S(1)}, u32[]{:S(2)}, u32[]{:S(2)}) collective-permute-start(f32[2,4,64,256]{3,2,1,0:T(8,128)S(1)} %get-tuple-element.57.refs_1_), channel_id=1, source_target_pairs={{0,1},{1,0},{2,3},{3,2},{4,5},{5,4},{6,7},{7,6},{8,9},{9,8},{10,11... | collective-permute-start | bytes 1572872 | tf_op jit(solution)/shard_map/ppermute | solution.py:504
  64.1 5.7 %collective-permute-start.21 = (f32[408,256]{1,0:T(8,128)S(1)}, f32[408,256]{1,0:T(8,128)S(1)}, u32[]{:S(2)}, u32[]{:S(2)}) collective-permute-start(f32[408,256]{1,0:T(8,128)S(1)} %pad_maximum_fusion.5), channel_id=1, source_target_pairs={{0,1},{1,0},{2,3},{3,2},{4,5},{5,4},{6,7},{7,6},{8,9},{9,8},{10,11... | collective-permute-start | bytes 1253384 | tf_op jit(solution)/shard_map/ppermute | solution.py:504
  65.2 9.2 %collective-permute-start.15 = (f32[256,256]{1,0:T(8,128)S(1)}, f32[256,256]{1,0:T(8,128)S(1)}, u32[]{:S(2)}, u32[]{:S(2)}) collective-permute-start(f32[256,256]{1,0:T(8,128)S(1)} %get-tuple-element.60), channel_id=1, source_target_pairs={{0,2},{1,3},{2,0},{3,1},{4,6},{5,7},{6,4},{7,5},{8,10},{9,11},{10,... | collective-permute-start | bytes 786440 | tf_op jit(solution)/shard_map/ppermute | solution.py:504
  66.0 13.7 %collective-permute-start.16 = (f32[256,256]{1,0:T(8,128)S(1)}, f32[256,256]{1,0:T(8,128)S(1)}, u32[]{:S(2)}, u32[]{:S(2)}) collective-permute-start(f32[256,256]{1,0:T(8,128)S(1)} %get-tuple-element.61), channel_id=1, source_target_pairs={{0,4},{1,5},{2,6},{3,7},{4,0},{5,1},{6,2},{7,3},{8,12},{9,13},{10,... | collective-permute-start | bytes 786440 | tf_op jit(solution)/shard_map/ppermute | solution.py:504
  67.0 12.7 %collective-permute-start.17 = (f32[256,256]{1,0:T(8,128)S(1)}, f32[256,256]{1,0:T(8,128)S(1)}, u32[]{:S(2)}, u32[]{:S(2)}) collective-permute-start(f32[256,256]{1,0:T(8,128)S(1)} %get-tuple-element.62), channel_id=1, source_target_pairs={{0,6},{1,7},{2,4},{3,5},{4,2},{5,3},{6,0},{7,1},{8,14},{9,15},{10,... | collective-permute-start | bytes 786440 | tf_op jit(solution)/shard_map/ppermute | solution.py:504

commit v6 on v5

--- a/solution.py
+++ b/solution.py
@@ -434,20 +434,20 @@
     )(*mine, *other, stack_w, stack_h, km)
 
 
-def assemble_kernel(k, width, *refs):
-    blocks, outs, scratch, sems = refs[:4], refs[-4:-2], refs[-2], refs[-1]
+def assemble_kernel(k, width, masks, *refs):
+    blocks, outs, scratch, sems = refs[: len(masks)], refs[-4:-2], refs[-2], refs[-1]
     columns = outs[0].shape[2]
     copies = []
-    for mask in range(4):
+    for n, mask in enumerate(masks):
         start = column_start(k, mask, columns)
         for f in range(2):
             for r in range(ROWS):
                 base = (f * ROWS + r) * SLAB
-                scratch[mask, f, :, r, :] = blocks[mask][base : base + SLAB, :]
+                scratch[n, f, :, r, :] = blocks[n][base : base + SLAB, :]
             copy = pltpu.make_async_copy(
-                scratch.at[mask, f],
+                scratch.at[n, f],
                 outs[f].at[:, :, pl.ds(start, width)],
-                sems.at[2 * mask + f],
+                sems.at[2 * n + f],
             )
             copy.start()
             copies.append(copy)
@@ -455,20 +455,20 @@
         copy.wait()
 
 
-def assemble(k, width, columns, blocks, outs, tail):
+def assemble(k, width, columns, masks, blocks, outs, tail):
     shape = jax.ShapeDtypeStruct((SLAB, ROWS, columns), jnp.float32)
     return pl.pallas_call(
-        functools.partial(assemble_kernel, k, width),
+        functools.partial(assemble_kernel, k, width, masks),
         out_shape=[shape] * 2,
-        in_specs=[pl.BlockSpec(memory_space=pltpu.VMEM)] * 4
+        in_specs=[pl.BlockSpec(memory_space=pltpu.VMEM)] * len(masks)
         + [pl.BlockSpec(memory_space=pltpu.HBM)] * len(outs)
         + [pl.BlockSpec(memory_space=pl.ANY)] * len(tail),
         out_specs=[pl.BlockSpec(memory_space=pltpu.HBM)] * 2,
         scratch_shapes=[
-            pltpu.VMEM((4, 2, SLAB, ROWS, width), jnp.float32),
-            pltpu.SemaphoreType.DMA((8,)),
+            pltpu.VMEM((len(masks), 2, SLAB, ROWS, width), jnp.float32),
+            pltpu.SemaphoreType.DMA((2 * len(masks),)),
         ],
-        input_output_aliases={4 + i: i for i in range(len(outs))},
+        input_output_aliases={len(masks) + i: i for i in range(len(outs))},
         compiler_params=params(),
         cost_estimate=cost(0, 4 << 20),
         name="assemble",
@@ -531,7 +531,11 @@
         kept, bx, by, bxy = solve(width, mine, other, stack_w, stack_h, km)
         arrived = [send(bx, "x"), send(by, "y"), send(bxy, "xy")]
         before = (kept, km)
-        outs = assemble(k, width, columns, [kept, *arrived], outs, tail)
+        if k + 1 < len(widths):
+            outs = assemble(k, width, columns, (0, 1, 2, 3), [kept, *arrived], outs, tail)
+        else:
+            outs = assemble(k, width, columns, (0, 1), [kept, arrived[0]], outs, tail)
+            outs = assemble(k, width, columns, (2, 3), arrived[1:], outs, [])
         if k + 1 < len(widths):
             tail = [send(jnp.concatenate([block[:TAIL_ROWS] for block in arrived]), "core")]
         else:

time: 81.2 us -> 81 us (level)
  waiting for transfers between devices: 21.7 us -> 20.8 us
    ppermute x22, waiting for transfers between devices: 21.7 us -> 20.8 us  [send(): return lax.ppermute(array, JOINT, route[name])]
    pallas_call x2 -> x3, Pallas kernels: 2.14 us -> 2.8 us  [assemble(): pl.pallas_call(functools.partial(assemble_kernel, k, width, masks), out_s...]
  transfers between devices with their start and end apart: 22 -> 22, of which waited for: 7 -> 7; matrix products, arithmetic and copies ran while one was open for 0% -> 0% of each run, Pallas kernels for 28% -> 29%
where the time goes in v6:
time: 81 us; the launch traced here: 80.7 us
  starting transfers between devices  29.8 us (37%)
  Pallas kernels  27.5 us (34%)
  waiting for transfers between devices  20.8 us (26%)
  local copies, waits for them, and re-layouts  1.29 us (2%)
  between operations  1.15 us (1%)
    ppermute x22, starting transfers between devices, send(): return lax.ppermute(array, JOINT, route[name])  29.8 us
    ppermute x22, waiting for transfers between devices, send(): return lax.ppermute(array, JOINT, route[name])  20.8 us
    pallas_call x2, Pallas kernels, stencil(): pl.pallas_call(functools.partial(stencil_kernel, width), out_shape=[jax.S...  10.7 us
    pallas_call x2, Pallas kernels, pre(): pl.pallas_call(functools.partial(pre_kernel, width), out_shape=[jax.Shape...  6.04 us
    pallas_call x2, Pallas kernels, pack(): pl.pallas_call(functools.partial(pack_kernel, k, width), out_shape=[shape...  5.31 us
    pallas_call x3, Pallas kernels, assemble(): pl.pallas_call(functools.partial(assemble_kernel, k, width, masks), out_s...  2.8 us
    pallas_call x2, Pallas kernels, solve(): pl.pallas_call(solve_kernel, out_shape=[shape] * 4, in_specs=[pl.BlockSpe...  1.98 us
  transfers between devices with their start and end apart: 22, of which 7 were waited for; matrix products, arithmetic and copies ran while one was open for 0% of the time, Pallas kernels for 29%

profile of v6, /device:TPU:0, one launch (start us, length us, event | category | flops | bytes accessed | tf_op | source)
XLA Modules:
  0.0 80.7 jit_solution(9164430999877397548)
XLA Ops:
  0.6 0.0 copy-start.3
  0.6 0.0 copy-start
  0.6 3.5 %pack.3 = (f32[272,256]{1,0:T(8,128)}, f32[272,256]{1,0:T(8,128)}, f32[272,256]{1,0:T(8,128)}, f32[272,256]{1,0:T(8,128)}) custom-call(f32[32,4,2048]{2,1,0:T(4,128)} %heat_hbm.3, f32[32,4,2048]{2,1,0:T(4,128)} %wet_hbm.3, s32[4,2048]{1,0:T(4,128)} %label_hbm.3), custom_call_target="tpu_custom_call" | custom-call | bytes 1024 | tf_op jit(solution)/shard_map/pack/pallas_call | solution.py:172
  4.2 3.0 %collective-permute-start.3 = (f32[272,256]{1,0:T(8,128)}, f32[272,256]{1,0:T(8,128)S(1)}, u32[]{:S(2)}, u32[]{:S(2)}) collective-permute-start(f32[272,256]{1,0:T(8,128)} %get-tuple-element.42), channel_id=1, source_target_pairs={{0,4},{1,5},{2,6},{3,7},{4,0},{5,1},{6,2},{7,3},{8,12},{9,13},{10,... | collective-permute-start | bytes 835592 | tf_op jit(solution)/shard_map/ppermute | solution.py:504
  7.2 1.5 %collective-permute-start.2 = (f32[272,256]{1,0:T(8,128)}, f32[272,256]{1,0:T(8,128)S(1)}, u32[]{:S(2)}, u32[]{:S(2)}) collective-permute-start(f32[272,256]{1,0:T(8,128)} %get-tuple-element.41), channel_id=1, source_target_pairs={{0,2},{1,3},{2,0},{3,1},{4,6},{5,7},{6,4},{7,5},{8,10},{9,11},{10,... | collective-permute-start | bytes 835592 | tf_op jit(solution)/shard_map/ppermute | solution.py:504
  8.7 0.0 collective-permute-start.4
  8.8 1.2 %copy-done.1 = f32[32,4,2048]{2,1,0:T(4,128)S(1)} copy-done((f32[32,4,2048]{2,1,0:T(4,128)S(1)}, f32[32,4,2048]{2,1,0:T(4,128)}, u32[]{:S(2)}) %copy-start.1) | copy-done | bytes 1048600
  10.0 0.0 copy-start.7
  10.0 0.0 copy-start.8
  10.0 1.8 %pack.2 = (f32[272,256]{1,0:T(8,128)S(1)}, f32[272,256]{1,0:T(8,128)S(1)}, f32[272,256]{1,0:T(8,128)S(1)}, f32[272,256]{1,0:T(8,128)S(1)}) custom-call(f32[32,4,2048]{2,1,0:T(4,128)S(1)} %copy-done, f32[32,4,2048]{2,1,0:T(4,128)S(1)} %copy-done.1, s32[4,2048]{1,0:T(4,128)S(1)} %copy-done.3), custom_call_target="tpu_custom_call" | custom-call | bytes 1024 | tf_op jit(solution)/shard_map/pack/pallas_call | solution.py:172
  11.8 2.0 %collective-permute-start = (f32[272,256]{1,0:T(8,128)S(1)}, f32[272,256]{1,0:T(8,128)S(1)}, u32[]{:S(2)}, u32[]{:S(2)}) collective-permute-start(f32[272,256]{1,0:T(8,128)S(1)} %get-tuple-element.38), channel_id=1, source_target_pairs={{0,2},{1,3},{2,0},{3,1},{4,6},{5,7},{6,4},{7,5},{8,10},{9,11},{10,... | collective-permute-start | bytes 835592 | tf_op jit(solution)/shard_map/ppermute | solution.py:504
  13.8 1.5 %collective-permute-start.1 = (f32[272,256]{1,0:T(8,128)S(1)}, f32[272,256]{1,0:T(8,128)S(1)}, u32[]{:S(2)}, u32[]{:S(2)}) collective-permute-start(f32[272,256]{1,0:T(8,128)S(1)} %get-tuple-element.39), channel_id=1, source_target_pairs={{0,4},{1,5},{2,6},{3,7},{4,0},{5,1},{6,2},{7,3},{8,12},{9,13},{10,... | collective-permute-start | bytes 835592 | tf_op jit(solution)/shard_map/ppermute | solution.py:504
  15.3 0.0 collective-permute-done.3.ry
  15.3 2.0 %collective-permute-start.5 = (f32[272,256]{1,0:T(8,128)S(1)}, f32[272,256]{1,0:T(8,128)S(1)}, u32[]{:S(2)}, u32[]{:S(2)}) collective-permute-start(f32[272,256]{1,0:T(8,128)S(1)} %get-tuple-element.48), channel_id=1, source_target_pairs={{0,6},{1,7},{2,4},{3,5},{4,2},{5,3},{6,0},{7,1},{8,14},{9,15},{10,... | collective-permute-start | bytes 835592 | tf_op jit(solution)/shard_map/ppermute | solution.py:504
  17.3 0.0 collective-permute-done.2.rx
  17.4 1.3 %collective-permute-start.9 = (f32[2,272,256]{2,1,0:T(8,128)S(1)}, f32[2,272,256]{2,1,0:T(8,128)S(1)}, u32[]{:S(2)}, u32[]{:S(2)}) collective-permute-start(f32[2,272,256]{2,1,0:T(8,128)S(1)} %pad_maximum_fusion.3), channel_id=1, source_target_pairs={{4,12},{5,13},{6,14},{7,15},{8,0},{9,1},{10,2},{11,3},{12,20},{13,... | collective-permute-start | bytes 1671176 | tf_op jit(solution)/shard_map/ppermute | solution.py:504
  18.7 3.8 %collective-permute-done.4.rxy = f32[272,256]{1,0:T(8,128)S(1)} collective-permute-done((f32[272,256]{1,0:T(8,128)}, f32[272,256]{1,0:T(8,128)S(1)}, u32[]{:S(2)}, u32[]{:S(2)}) %collective-permute-start.4) | collective-permute-done | bytes 278560 | tf_op jit(solution)/shard_map/ppermute | solution.py:504
  22.5 4.0 %collective-permute-start.10 = (f32[2,272,256]{2,1,0:T(8,128)S(1)}, f32[2,272,256]{2,1,0:T(8,128)S(1)}, u32[]{:S(2)}, u32[]{:S(2)}) collective-permute-start(f32[2,272,256]{2,1,0:T(8,128)S(1)} %pad_maximum_fusion.4), channel_id=1, source_target_pairs={{0,8},{1,9},{2,10},{3,11},{8,16},{9,17},{10,18},{11,19},{12,4},{13... | collective-permute-start | bytes 1671176 | tf_op jit(solution)/shard_map/ppermute | solution.py:504
  26.5 0.7 prep.1
  27.3 0.0 copy-done.7
  27.3 0.0 copy-done.8
  27.3 3.0 %inner_substeps.2 = (f32[10,2,64,384]{3,2,1,0:T(8,128)S(1)}, f32[2,8,384]{2,1,0:T(8,128)S(1)}, f32[8,256]{1,0:T(8,128)S(1)}) custom-call(f32[272,256]{1,0:T(8,128)S(1)} %copy-done.2, f32[272,256]{1,0:T(8,128)S(1)} %collective-permute-done.2.rx, f32[272,256]{1,0:T(8,128)S(1)} %collective-permute-done.3.ry, f32[272,256]{1,0:T(8,128)S(1)} %collective-permute-done.4.rxy, ...), custom_call_target="tpu_custom_call" | custom-call | bytes 1024 | tf_op jit(solution)/shard_map/inner_substeps/pallas_call | solution.py:325
  30.3 0.0 collective-permute-done.1.ry
  30.3 0.0 collective-permute-done.rx
  30.3 2.9 %collective-permute-done.5.rxy = f32[272,256]{1,0:T(8,128)S(1)} collective-permute-done((f32[272,256]{1,0:T(8,128)S(1)}, f32[272,256]{1,0:T(8,128)S(1)}, u32[]{:S(2)}, u32[]{:S(2)}) %collective-permute-start.5) | collective-permute-done | bytes 278560 | tf_op jit(solution)/shard_map/ppermute | solution.py:504
  33.3 0.1 pad_maximum_fusion
  33.3 0.1 collective-permute-start.8
  33.5 1.3 %collective-permute-start.6 = (f32[2,272,256]{2,1,0:T(8,128)S(1)}, f32[2,272,256]{2,1,0:T(8,128)S(1)}, u32[]{:S(2)}, u32[]{:S(2)}) collective-permute-start(f32[2,272,256]{2,1,0:T(8,128)S(1)} %pad_maximum_fusion.1), channel_id=1, source_target_pairs={{4,12},{5,13},{6,14},{7,15},{8,0},{9,1},{10,2},{11,3},{12,20},{13,... | collective-permute-start | bytes 1671176 | tf_op jit(solution)/shard_map/ppermute | solution.py:504
  34.8 4.8 %collective-permute-start.7 = (f32[2,272,256]{2,1,0:T(8,128)S(1)}, f32[2,272,256]{2,1,0:T(8,128)S(1)}, u32[]{:S(2)}, u32[]{:S(2)}) collective-permute-start(f32[2,272,256]{2,1,0:T(8,128)S(1)} %pad_maximum_fusion.2), channel_id=1, source_target_pairs={{0,8},{1,9},{2,10},{3,11},{8,16},{9,17},{10,18},{11,19},{12,4},{13... | collective-permute-start | bytes 1671176 | tf_op jit(solution)/shard_map/ppermute | solution.py:504
  39.6 0.0 collective-permute-done.9.p1
  39.6 0.0 collective-permute-done.10.p2
  39.6 5.3 %outer_substeps.2 = (f32[2,4,64,256]{3,2,1,0:T(8,128)S(1)}, f32[2,4,64,256]{3,2,1,0:T(8,128)S(1)}) custom-call(f32[272,256]{1,0:T(8,128)S(1)} %copy-done.2, f32[272,256]{1,0:T(8,128)S(1)} %collective-permute-done.2.rx, f32[272,256]{1,0:T(8,128)S(1)} %collective-permute-done.3.ry, f32[272,256]{1,0:T(8,128)S(1)} %collective-permute-done.4.rxy, ...), custom_call_target="tpu_custom_call" | custom-call | bytes 1024 | tf_op jit(solution)/shard_map/outer_substeps/pallas_call | solution.py:378
  44.9 0.1 collective-permute-start.11
  45.0 0.5 collective-permute-start.12
  45.5 1.4 %collective-permute-done.11.refs_2_ = f32[2,4,64,256]{3,2,1,0:T(8,128)S(1)} collective-permute-done((f32[2,4,64,256]{3,2,1,0:T(8,128)S(1)}, f32[2,4,64,256]{3,2,1,0:T(8,128)S(1)}, u32[]{:S(2)}, u32[]{:S(2)}) %collective-permute-start.11) | collective-permute-done | bytes 524320 | tf_op jit(solution)/shard_map/ppermute | solution.py:504
  46.9 0.7 collective-permute-done.12.refs_3_
  47.7 1.0 %solve.2 = (f32[256,256]{1,0:T(8,128)S(1)}, f32[256,256]{1,0:T(8,128)S(1)}, f32[256,256]{1,0:T(8,128)S(1)}, f32[256,256]{1,0:T(8,128)S(1)}) custom-call(f32[2,4,64,256]{3,2,1,0:T(8,128)S(1)} %get-tuple-element.53.refs_0_, f32[2,4,64,256]{3,2,1,0:T(8,128)S(1)} %get-tuple-element.54.refs_1_, f32[2,4,64,256]{3,2,1,0:T(8,128)S(1)} %collective-permute-done.11.refs_2_, ...), custom_call_target="tpu_custom_call" | custom-call | bytes 1024 | tf_op jit(solution)/shard_map/solve/pallas_call | solution.py:426
  48.7 1.7 %collective-permute-start.18 = (f32[256,256]{1,0:T(8,128)S(1)}, f32[256,256]{1,0:T(8,128)S(1)}, u32[]{:S(2)}, u32[]{:S(2)}) collective-permute-start(f32[256,256]{1,0:T(8,128)S(1)} %get-tuple-element.65), channel_id=1, source_target_pairs={{0,2},{1,3},{2,0},{3,1},{4,6},{5,7},{6,4},{7,5},{8,10},{9,11},{10,... | collective-permute-start | bytes 786440 | tf_op jit(solution)/shard_map/ppermute | solution.py:504
  50.4 0.5 collective-permute-start.19
  50.8 0.0 collective-permute-done.8._
  50.8 1.4 %collective-permute-start.20 = (f32[256,256]{1,0:T(8,128)S(1)}, f32[256,256]{1,0:T(8,128)S(1)}, u32[]{:S(2)}, u32[]{:S(2)}) collective-permute-start(f32[256,256]{1,0:T(8,128)S(1)} %get-tuple-element.67), channel_id=1, source_target_pairs={{0,6},{1,7},{2,4},{3,5},{4,2},{5,3},{6,0},{7,1},{8,14},{9,15},{10,... | collective-permute-start | bytes 786440 | tf_op jit(solution)/shard_map/ppermute | solution.py:504
  52.2 3.0 %inner_substeps.3 = (f32[10,2,64,384]{3,2,1,0:T(8,128)S(1)}, f32[2,8,384]{2,1,0:T(8,128)S(1)}, f32[8,256]{1,0:T(8,128)S(1)}) custom-call(f32[272,256]{1,0:T(8,128)S(1)} %get-tuple-element.37.own, f32[272,256]{1,0:T(8,128)S(1)} %collective-permute-done.rx, f32[272,256]{1,0:T(8,128)S(1)} %collective-permute-done.1.ry, ...), custom_call_target="tpu_custom_call" | custom-call | bytes 1024 | tf_op jit(solution)/shard_map/inner_substeps/pallas_call | solution.py:325
  55.2 0.0 collective-permute-done.6.p1
  55.3 0.0 collective-permute-done.7.p2
  55.3 5.3 %outer_substeps.3 = (f32[2,4,64,256]{3,2,1,0:T(8,128)S(1)}, f32[2,4,64,256]{3,2,1,0:T(8,128)S(1)}) custom-call(f32[272,256]{1,0:T(8,128)S(1)} %get-tuple-element.37.own, f32[272,256]{1,0:T(8,128)S(1)} %collective-permute-done.rx, f32[272,256]{1,0:T(8,128)S(1)} %collective-permute-done.1.ry, f32[272,256]{1,0:T(8,128)S(1)} %collective-permute-done.5.rxy, ...), custom_call_target="tpu_custom_call" | custom-call | bytes 1024 | tf_op jit(solution)/shard_map/outer_substeps/pallas_call | solution.py:378
  60.6 0.1 collective-permute-start.13
  60.7 0.5 collective-permute-start.14
  61.2 0.0 collective-permute-done.18.refs_1_
  61.2 2.9 %collective-permute-done.19.refs_2_ = f32[256,256]{1,0:T(8,128)S(1)} collective-permute-done((f32[256,256]{1,0:T(8,128)S(1)}, f32[256,256]{1,0:T(8,128)S(1)}, u32[]{:S(2)}, u32[]{:S(2)}) %collective-permute-start.19) | collective-permute-done | bytes 262176 | tf_op jit(solution)/shard_map/ppermute | solution.py:504
  64.1 0.0 collective-permute-done.20.refs_3_
  64.1 0.1 collective-permute-start.21
  64.2 0.0 collective-permute-done.13.refs_2_
  64.2 0.0 collective-permute-done.14.refs_3_
  64.2 1.0 %solve.3 = (f32[256,256]{1,0:T(8,128)S(1)}, f32[256,256]{1,0:T(8,128)S(1)}, f32[256,256]{1,0:T(8,128)S(1)}, f32[256,256]{1,0:T(8,128)S(1)}) custom-call(f32[2,4,64,256]{3,2,1,0:T(8,128)S(1)} %get-tuple-element.58.refs_0_, f32[2,4,64,256]{3,2,1,0:T(8,128)S(1)} %get-tuple-element.59.refs_1_, f32[2,4,64,256]{3,2,1,0:T(8,128)S(1)} %collective-permute-done.13.refs_2_, ...), custom_call_target="tpu_custom_call" | custom-call | bytes 1024 | tf_op jit(solution)/shard_map/solve/pallas_call | solution.py:426
  65.2 0.8 collective-permute-start.17
  66.0 1.0 %collective-permute-start.15 = (f32[256,256]{1,0:T(8,128)S(1)}, f32[256,256]{1,0:T(8,128)S(1)}, u32[]{:S(2)}, u32[]{:S(2)}) collective-permute-start(f32[256,256]{1,0:T(8,128)S(1)} %get-tuple-element.61), channel_id=1, source_target_pairs={{0,4},{1,5},{2,6},{3,7},{4,0},{5,1},{6,2},{7,3},{8,12},{9,13},{10,... | collective-permute-start | bytes 786440 | tf_op jit(solution)/shard_map/ppermute | solution.py:504
  67.0 1.8 %collective-permute-start.16 = (f32[256,256]{1,0:T(8,128)S(1)}, f32[256,256]{1,0:T(8,128)S(1)}, u32[]{:S(2)}, u32[]{:S(2)}) collective-permute-start(f32[256,256]{1,0:T(8,128)S(1)} %get-tuple-element.62), channel_id=1, source_target_pairs={{0,6},{1,7},{2,4},{3,5},{4,2},{5,3},{6,0},{7,1},{8,14},{9,15},{10,... | collective-permute-start | bytes 786440 | tf_op jit(solution)/shard_map/ppermute | solution.py:504
  68.8 1.1 %assemble.3 = (f32[32,4,2048]{2,1,0:T(4,128)}, f32[32,4,2048]{2,1,0:T(4,128)}) custom-call(f32[256,256]{1,0:T(8,128)S(1)} %get-tuple-element.56.refs_0_, f32[256,256]{1,0:T(8,128)S(1)} %collective-permute-done.18.refs_1_, f32[256,256]{1,0:T(8,128)S(1)} %collective-permute-done.19.refs_2_, f32[256,256]{1,0:T(8,128)S(1)} %collective-permute-done.20.refs_3_), custom_call_target="tpu_custom_call" | custom-call | bytes 1024 | tf_op jit(solution)/shard_map/assemble/pallas_call | solution.py:460
  69.9 0.0 collective-permute-done.21.refs_4_
  69.9 4.5 %collective-permute-done.17.refs_1_ = f32[256,256]{1,0:T(8,128)S(1)} collective-permute-done((f32[256,256]{1,0:T(8,128)S(1)}, f32[256,256]{1,0:T(8,128)S(1)}, u32[]{:S(2)}, u32[]{:S(2)}) %collective-permute-start.17) | collective-permute-done | bytes 262176 | tf_op jit(solution)/shard_map/ppermute | solution.py:504
  74.4 0.9 %assemble.4 = (f32[32,4,2048]{2,1,0:T(4,128)}, f32[32,4,2048]{2,1,0:T(4,128)}) custom-call(f32[256,256]{1,0:T(8,128)S(1)} %get-tuple-element.63.refs_0_, f32[256,256]{1,0:T(8,128)S(1)} %collective-permute-done.17.refs_1_, f32[32,4,2048]{2,1,0:T(4,128)} %get-tuple-element.68.refs_2_, ...), custom_call_target="tpu_custom_call", output_to_operand_aliasing={{0}: (2, {}), {1}: (3, {})} | custom-call | bytes 1024 | tf_op jit(solution)/shard_map/assemble/pallas_call | solution.py:460
  75.3 4.4 %collective-permute-done.15.refs_0_ = f32[256,256]{1,0:T(8,128)S(1)} collective-permute-done((f32[256,256]{1,0:T(8,128)S(1)}, f32[256,256]{1,0:T(8,128)S(1)}, u32[]{:S(2)}, u32[]{:S(2)}) %collective-permute-start.15) | collective-permute-done | bytes 262176 | tf_op jit(solution)/shard_map/ppermute | solution.py:504
  79.7 0.0 collective-permute-done.16.refs_1_
  79.7 0.9 %assemble.5 = (f32[32,4,2048]{2,1,0:T(4,128)}, f32[32,4,2048]{2,1,0:T(4,128)}) custom-call(f32[256,256]{1,0:T(8,128)S(1)} %collective-permute-done.15.refs_0_, f32[256,256]{1,0:T(8,128)S(1)} %collective-permute-done.16.refs_1_, f32[32,4,2048]{2,1,0:T(4,128)} %get-tuple-element.70.refs_2_, ...), custom_call_target="tpu_custom_call", output_to_operand_aliasing={{0}: (2, {}), {1}: (3, {})} | custom-call | bytes 1024 | tf_op jit(solution)/shard_map/assemble/pallas_call | solution.py:460
  (19 shorter events, 0.2 us)
Async XLA Ops:
  0.6 8.1 %copy-start.3 = (s32[4,2048]{1,0:T(4,128)S(1)}, s32[4,2048]{1,0:T(4,128)}, u32[]{:S(2)}) copy-start(s32[4,2048]{1,0:T(4,128)} %label_hbm.3) | copy-start | bytes 98308
  0.6 8.1 %copy-start = (f32[32,4,2048]{2,1,0:T(4,128)S(1)}, f32[32,4,2048]{2,1,0:T(4,128)}, u32[]{:S(2)}) copy-start(f32[32,4,2048]{2,1,0:T(4,128)} %heat_hbm.3) | copy-start | bytes 3145732
  4.2 11.2 %collective-permute-start.3 = (f32[272,256]{1,0:T(8,128)}, f32[272,256]{1,0:T(8,128)S(1)}, u32[]{:S(2)}, u32[]{:S(2)}) collective-permute-start(f32[272,256]{1,0:T(8,128)} %get-tuple-element.42), channel_id=1, source_target_pairs={{0,4},{1,5},{2,6},{3,7},{4,0},{5,1},{6,2},{7,3},{8,12},{9,13},{10,... | collective-permute-start | bytes 835592 | tf_op jit(solution)/shard_map/ppermute | solution.py:504
  7.2 10.1 %collective-permute-start.2 = (f32[272,256]{1,0:T(8,128)}, f32[272,256]{1,0:T(8,128)S(1)}, u32[]{:S(2)}, u32[]{:S(2)}) collective-permute-start(f32[272,256]{1,0:T(8,128)} %get-tuple-element.41), channel_id=1, source_target_pairs={{0,2},{1,3},{2,0},{3,1},{4,6},{5,7},{6,4},{7,5},{8,10},{9,11},{10,... | collective-permute-start | bytes 835592 | tf_op jit(solution)/shard_map/ppermute | solution.py:504
  8.7 13.8 %collective-permute-start.4 = (f32[272,256]{1,0:T(8,128)}, f32[272,256]{1,0:T(8,128)S(1)}, u32[]{:S(2)}, u32[]{:S(2)}) collective-permute-start(f32[272,256]{1,0:T(8,128)} %get-tuple-element.43), channel_id=1, source_target_pairs={{0,6},{1,7},{2,4},{3,5},{4,2},{5,3},{6,0},{7,1},{8,14},{9,15},{10,... | collective-permute-start | bytes 835592 | tf_op jit(solution)/shard_map/ppermute | solution.py:504
  8.8 1.2 %copy-start.1 = (f32[32,4,2048]{2,1,0:T(4,128)S(1)}, f32[32,4,2048]{2,1,0:T(4,128)}, u32[]{:S(2)}) copy-start(f32[32,4,2048]{2,1,0:T(4,128)} %wet_hbm.3) | copy-start | bytes 3145732
  10.0 7.3 %copy-start.2 = (f32[272,256]{1,0:T(8,128)S(1)}, f32[272,256]{1,0:T(8,128)}, u32[]{:S(2)}) copy-start(f32[272,256]{1,0:T(8,128)} %get-tuple-element.40.own) | copy-start | bytes 835588
  10.0 16.5 %copy-start.4 = (f32[128,128]{1,0:T(8,128)S(1)}, f32[128,128]{1,0:T(8,128)}, u32[]{:S(2)}) copy-start(f32[128,128]{1,0:T(8,128)} %thermal_ref.1) | copy-start | bytes 196612
  10.0 16.5 %copy-start.5 = (f32[128,128]{1,0:T(8,128)S(1)}, f32[128,128]{1,0:T(8,128)}, u32[]{:S(2)}) copy-start(f32[128,128]{1,0:T(8,128)} %water_ref.1) | copy-start | bytes 196612
  10.0 16.6 %copy-start.6 = (f32[128,128]{1,0:T(8,128)S(1)}, f32[128,128]{1,0:T(8,128)}, u32[]{:S(2)}) copy-start(f32[128,128]{1,0:T(8,128)} %constant.2.clone.cheb_ref) | copy-start | bytes 196612
  10.0 17.3 %copy-start.7 = (f32[12]{0:T(128)S(1)}, f32[12]{0:T(128)}, u32[]{:S(2)}) copy-start(f32[12]{0:T(128)} %spread_ref.7) | copy-start | bytes 148
  10.0 17.3 %copy-start.8 = (f32[12]{0:T(128)S(1)}, f32[12]{0:T(128)}, u32[]{:S(2)}) copy-start(f32[12]{0:T(128)} %factor_ref.7) | copy-start | bytes 148
  11.8 18.5 %collective-permute-start = (f32[272,256]{1,0:T(8,128)S(1)}, f32[272,256]{1,0:T(8,128)S(1)}, u32[]{:S(2)}, u32[]{:S(2)}) collective-permute-start(f32[272,256]{1,0:T(8,128)S(1)} %get-tuple-element.38), channel_id=1, source_target_pairs={{0,2},{1,3},{2,0},{3,1},{4,6},{5,7},{6,4},{7,5},{8,10},{9,11},{10,... | collective-permute-start | bytes 835592 | tf_op jit(solution)/shard_map/ppermute | solution.py:504
  13.8 16.5 %collective-permute-start.1 = (f32[272,256]{1,0:T(8,128)S(1)}, f32[272,256]{1,0:T(8,128)S(1)}, u32[]{:S(2)}, u32[]{:S(2)}) collective-permute-start(f32[272,256]{1,0:T(8,128)S(1)} %get-tuple-element.39), channel_id=1, source_target_pairs={{0,4},{1,5},{2,6},{3,7},{4,0},{5,1},{6,2},{7,3},{8,12},{9,13},{10,... | collective-permute-start | bytes 835592 | tf_op jit(solution)/shard_map/ppermute | solution.py:504
  15.3 18.0 %collective-permute-start.5 = (f32[272,256]{1,0:T(8,128)S(1)}, f32[272,256]{1,0:T(8,128)S(1)}, u32[]{:S(2)}, u32[]{:S(2)}) collective-permute-start(f32[272,256]{1,0:T(8,128)S(1)} %get-tuple-element.48), channel_id=1, source_target_pairs={{0,6},{1,7},{2,4},{3,5},{4,2},{5,3},{6,0},{7,1},{8,14},{9,15},{10,... | collective-permute-start | bytes 835592 | tf_op jit(solution)/shard_map/ppermute | solution.py:504
  17.4 22.2 %collective-permute-start.9 = (f32[2,272,256]{2,1,0:T(8,128)S(1)}, f32[2,272,256]{2,1,0:T(8,128)S(1)}, u32[]{:S(2)}, u32[]{:S(2)}) collective-permute-start(f32[2,272,256]{2,1,0:T(8,128)S(1)} %pad_maximum_fusion.3), channel_id=1, source_target_pairs={{4,12},{5,13},{6,14},{7,15},{8,0},{9,1},{10,2},{11,3},{12,20},{13,... | collective-permute-start | bytes 1671176 | tf_op jit(solution)/shard_map/ppermute | solution.py:504
  22.5 17.1 %collective-permute-start.10 = (f32[2,272,256]{2,1,0:T(8,128)S(1)}, f32[2,272,256]{2,1,0:T(8,128)S(1)}, u32[]{:S(2)}, u32[]{:S(2)}) collective-permute-start(f32[2,272,256]{2,1,0:T(8,128)S(1)} %pad_maximum_fusion.4), channel_id=1, source_target_pairs={{0,8},{1,9},{2,10},{3,11},{8,16},{9,17},{10,18},{11,19},{12,4},{13... | collective-permute-start | bytes 1671176 | tf_op jit(solution)/shard_map/ppermute | solution.py:504
  33.3 17.5 %collective-permute-start.8 = (f32[816,256]{1,0:T(8,128)S(1)}, f32[816,256]{1,0:T(8,128)S(1)}, u32[]{:S(2)}, u32[]{:S(2)}) collective-permute-start(f32[816,256]{1,0:T(8,128)S(1)} %pad_maximum_fusion), channel_id=1, source_target_pairs={{0,1},{1,0},{2,3},{3,2},{4,5},{5,4},{6,7},{7,6},{8,9},{9,8},{10,11... | collective-permute-start | bytes 2506760 | tf_op jit(solution)/shard_map/ppermute | solution.py:504
  33.5 21.8 %collective-permute-start.6 = (f32[2,272,256]{2,1,0:T(8,128)S(1)}, f32[2,272,256]{2,1,0:T(8,128)S(1)}, u32[]{:S(2)}, u32[]{:S(2)}) collective-permute-start(f32[2,272,256]{2,1,0:T(8,128)S(1)} %pad_maximum_fusion.1), channel_id=1, source_target_pairs={{4,12},{5,13},{6,14},{7,15},{8,0},{9,1},{10,2},{11,3},{12,20},{13,... | collective-permute-start | bytes 1671176 | tf_op jit(solution)/shard_map/ppermute | solution.py:504
  34.8 20.4 %collective-permute-start.7 = (f32[2,272,256]{2,1,0:T(8,128)S(1)}, f32[2,272,256]{2,1,0:T(8,128)S(1)}, u32[]{:S(2)}, u32[]{:S(2)}) collective-permute-start(f32[2,272,256]{2,1,0:T(8,128)S(1)} %pad_maximum_fusion.2), channel_id=1, source_target_pairs={{0,8},{1,9},{2,10},{3,11},{8,16},{9,17},{10,18},{11,19},{12,4},{13... | collective-permute-start | bytes 1671176 | tf_op jit(solution)/shard_map/ppermute | solution.py:504
  44.9 2.0 %collective-permute-start.11 = (f32[2,4,64,256]{3,2,1,0:T(8,128)S(1)}, f32[2,4,64,256]{3,2,1,0:T(8,128)S(1)}, u32[]{:S(2)}, u32[]{:S(2)}) collective-permute-start(f32[2,4,64,256]{3,2,1,0:T(8,128)S(1)} %get-tuple-element.53.refs_0_), channel_id=1, source_target_pairs={{0,1},{1,0},{2,3},{3,2},{4,5},{5,4},{6,7},{7,6},{8,9},{9,8},{10,11... | collective-permute-start | bytes 1572872 | tf_op jit(solution)/shard_map/ppermute | solution.py:504
  45.0 2.6 %collective-permute-start.12 = (f32[2,4,64,256]{3,2,1,0:T(8,128)S(1)}, f32[2,4,64,256]{3,2,1,0:T(8,128)S(1)}, u32[]{:S(2)}, u32[]{:S(2)}) collective-permute-start(f32[2,4,64,256]{3,2,1,0:T(8,128)S(1)} %get-tuple-element.54.refs_1_), channel_id=1, source_target_pairs={{0,1},{1,0},{2,3},{3,2},{4,5},{5,4},{6,7},{7,6},{8,9},{9,8},{10,11... | collective-permute-start | bytes 1572872 | tf_op jit(solution)/shard_map/ppermute | solution.py:504
  48.7 12.5 %collective-permute-start.18 = (f32[256,256]{1,0:T(8,128)S(1)}, f32[256,256]{1,0:T(8,128)S(1)}, u32[]{:S(2)}, u32[]{:S(2)}) collective-permute-start(f32[256,256]{1,0:T(8,128)S(1)} %get-tuple-element.65), channel_id=1, source_target_pairs={{0,2},{1,3},{2,0},{3,1},{4,6},{5,7},{6,4},{7,5},{8,10},{9,11},{10,... | collective-permute-start | bytes 786440 | tf_op jit(solution)/shard_map/ppermute | solution.py:504
  50.4 13.7 %collective-permute-start.19 = (f32[256,256]{1,0:T(8,128)S(1)}, f32[256,256]{1,0:T(8,128)S(1)}, u32[]{:S(2)}, u32[]{:S(2)}) collective-permute-start(f32[256,256]{1,0:T(8,128)S(1)} %get-tuple-element.66), channel_id=1, source_target_pairs={{0,4},{1,5},{2,6},{3,7},{4,0},{5,1},{6,2},{7,3},{8,12},{9,13},{10,... | collective-permute-start | bytes 786440 | tf_op jit(solution)/shard_map/ppermute | solution.py:504
  50.8 13.2 %collective-permute-start.20 = (f32[256,256]{1,0:T(8,128)S(1)}, f32[256,256]{1,0:T(8,128)S(1)}, u32[]{:S(2)}, u32[]{:S(2)}) collective-permute-start(f32[256,256]{1,0:T(8,128)S(1)} %get-tuple-element.67), channel_id=1, source_target_pairs={{0,6},{1,7},{2,4},{3,5},{4,2},{5,3},{6,0},{7,1},{8,14},{9,15},{10,... | collective-permute-start | bytes 786440 | tf_op jit(solution)/shard_map/ppermute | solution.py:504
  60.6 3.6 %collective-permute-start.13 = (f32[2,4,64,256]{3,2,1,0:T(8,128)S(1)}, f32[2,4,64,256]{3,2,1,0:T(8,128)S(1)}, u32[]{:S(2)}, u32[]{:S(2)}) collective-permute-start(f32[2,4,64,256]{3,2,1,0:T(8,128)S(1)} %get-tuple-element.58.refs_0_), channel_id=1, source_target_pairs={{0,1},{1,0},{2,3},{3,2},{4,5},{5,4},{6,7},{7,6},{8,9},{9,8},{10,11... | collective-permute-start | bytes 1572872 | tf_op jit(solution)/shard_map/ppermute | solution.py:504
  60.7 3.6 %collective-permute-start.14 = (f32[2,4,64,256]{3,2,1,0:T(8,128)S(1)}, f32[2,4,64,256]{3,2,1,0:T(8,128)S(1)}, u32[]{:S(2)}, u32[]{:S(2)}) collective-permute-start(f32[2,4,64,256]{3,2,1,0:T(8,128)S(1)} %get-tuple-element.59.refs_1_), channel_id=1, source_target_pairs={{0,1},{1,0},{2,3},{3,2},{4,5},{5,4},{6,7},{7,6},{8,9},{9,8},{10,11... | collective-permute-start | bytes 1572872 | tf_op jit(solution)/shard_map/ppermute | solution.py:504
  64.1 5.7 %collective-permute-start.21 = (f32[408,256]{1,0:T(8,128)S(1)}, f32[408,256]{1,0:T(8,128)S(1)}, u32[]{:S(2)}, u32[]{:S(2)}) collective-permute-start(f32[408,256]{1,0:T(8,128)S(1)} %pad_maximum_fusion.5), channel_id=1, source_target_pairs={{0,1},{1,0},{2,3},{3,2},{4,5},{5,4},{6,7},{7,6},{8,9},{9,8},{10,11... | collective-permute-start | bytes 1253384 | tf_op jit(solution)/shard_map/ppermute | solution.py:504
  65.2 9.2 %collective-permute-start.17 = (f32[256,256]{1,0:T(8,128)S(1)}, f32[256,256]{1,0:T(8,128)S(1)}, u32[]{:S(2)}, u32[]{:S(2)}) collective-permute-start(f32[256,256]{1,0:T(8,128)S(1)} %get-tuple-element.64), channel_id=1, source_target_pairs={{0,2},{1,3},{2,0},{3,1},{4,6},{5,7},{6,4},{7,5},{8,10},{9,11},{10,... | collective-permute-start | bytes 786440 | tf_op jit(solution)/shard_map/ppermute | solution.py:504
  66.0 13.7 %collective-permute-start.15 = (f32[256,256]{1,0:T(8,128)S(1)}, f32[256,256]{1,0:T(8,128)S(1)}, u32[]{:S(2)}, u32[]{:S(2)}) collective-permute-start(f32[256,256]{1,0:T(8,128)S(1)} %get-tuple-element.61), channel_id=1, source_target_pairs={{0,4},{1,5},{2,6},{3,7},{4,0},{5,1},{6,2},{7,3},{8,12},{9,13},{10,... | collective-permute-start | bytes 786440 | tf_op jit(solution)/shard_map/ppermute | solution.py:504
  67.0 12.7 %collective-permute-start.16 = (f32[256,256]{1,0:T(8,128)S(1)}, f32[256,256]{1,0:T(8,128)S(1)}, u32[]{:S(2)}, u32[]{:S(2)}) collective-permute-start(f32[256,256]{1,0:T(8,128)S(1)} %get-tuple-element.62), channel_id=1, source_target_pairs={{0,6},{1,7},{2,4},{3,5},{4,2},{5,3},{6,0},{7,1},{8,14},{9,15},{10,... | collective-permute-start | bytes 786440 | tf_op jit(solution)/shard_map/ppermute | solution.py:504
